TPU v7x, 32 devices: a whole 2x2x4 slice. The times are simulated.
32 devices in a mesh: member: 2 (over x), seq: 4 (over z), head: 4 (over y, core).
Axes of the slice: x: 2, y: 2, z: 4, core: 2. Of those that a mesh axis runs over, the one named last changes fastest.
Arguments:
- tokens: bfloat16 [2048, 5120], P(('seq', 'head')), may hold values from -6 to 6
- lattice: int32 [3, 2048], P(None, 'seq'), may hold values from 0 to 63
- timestep: int32 [4], replicated, may hold values from 0 to 999
- time_weight: bfloat16 [2, 256, 5120], P(None, None, 'seq'), may hold values from -0.375 to 0.375
- query_weight: bfloat16 [2, 5120, 2560], P('member', 'seq', 'head'), may hold values from -6 to 6
- key_weight: bfloat16 [5120, 2560], P('seq', 'head'), may hold values from -6 to 6
- values: bfloat16 [2048, 2560], P(('seq', 'head')), may hold values from -6 to 6
- cotangent: bfloat16 [2, 2048, 2560], P('member', ('seq', 'head')), may hold values from -72 to 72
Outputs:
- fisher: float32 [2, 5120, 2560], P('member', 'seq', 'head')
- merged: float32 [5120, 2560], P('seq', 'head')
All inputs are finite; a program needn't handle non-finite values.
Results may differ from a plain program's by a relative error of at most 0.022.
Values may be sent and summed in bfloat16 or wider, within the bound.
No kernel may reach another device: no remote copies, remote signals or barrier semaphores. Data moves between devices by JAX's collectives and lax.ppermute only.
A program may use at most 128 MiB of HBM per device.

v0:
```python
import math

import jax
import jax.numpy as jnp
from jax import lax
from jax.sharding import PartitionSpec as P

HEAD_SIZE = 128


damping = 0.01


def time_features(timestep, feature_count):
    halfway = feature_count // 2
    ladder = jnp.arange(halfway).astype(jnp.float32)
    frequency = jnp.exp(-math.log(10000.0) * 2.0 * ladder / feature_count)
    angles = timestep.astype(jnp.float32)[:, None] * frequency[None, :]
    return jnp.concatenate([jnp.cos(angles), jnp.sin(angles)], axis=1).astype(jnp.bfloat16)


def rope_tables(lattice, head_width):
    halfway = head_width // 2
    side_pairs = head_width // 6
    frame_pairs = halfway - 2 * side_pairs
    column = jnp.arange(head_width)
    pair_index = column % halfway
    which_axis = jnp.where(
        pair_index < frame_pairs, 0, jnp.where(pair_index < frame_pairs + side_pairs, 1, 2)
    )
    anchor = jnp.where(
        which_axis == 0, 0, jnp.where(which_axis == 1, frame_pairs, frame_pairs + side_pairs)
    )
    pair_span = jnp.where(which_axis == 0, frame_pairs, side_pairs)
    frequency = jnp.exp(
        -math.log(10000.0)
        * (pair_index - anchor).astype(jnp.float32)
        / pair_span.astype(jnp.float32)
    )
    position = lattice.astype(jnp.float32)
    angles = jnp.zeros((lattice.shape[1], head_width), jnp.float32)
    for axis_number in range(3):
        chosen = jnp.where(which_axis == axis_number, frequency, 0.0)
        angles = angles + position[axis_number][:, None] * chosen[None, :]
    sign_flip = jnp.where(column < halfway, -1.0, 1.0).astype(jnp.float32)
    return (jnp.cos(angles), jnp.sin(angles) * sign_flip[None, :])


def normed_rotation(stacked, cosine, sine_table):
    halfway = stacked.shape[2] // 2
    inverse = lax.rsqrt(jnp.mean(stacked * stacked, axis=2, keepdims=True) + 1e-06)
    normed = stacked * inverse
    rotated = (
        normed * cosine[:, None, :] + jnp.roll(normed, halfway, axis=2) * sine_table[:, None, :]
    )
    return (normed, inverse, rotated)


def attention_backward(query_pre, key_pre, values, cotangent, cosine, sine_table, head_width):
    length, width = query_pre.shape
    head_count = width // head_width
    halfway = head_width // 2
    query_normed, query_inverse, query_rotated = normed_rotation(
        query_pre.reshape(length, head_count, head_width), cosine, sine_table
    )
    unused_normed, unused_inverse, key_rotated = normed_rotation(
        key_pre.reshape(length, head_count, head_width), cosine, sine_table
    )
    query_round = query_rotated.astype(jnp.bfloat16)
    key_round = key_rotated.astype(jnp.bfloat16)
    value_heads = values.reshape(length, head_count, head_width)
    block_rows = min(length, 512)
    block_count = length // block_rows
    score_scale = head_width ** (-0.5)

    def one_block(portion):
        query_block, grad_block = portion
        scores = (
            jnp.einsum("qhd,khd->hqk", query_block, key_round, preferred_element_type=jnp.float32)
            * score_scale
        )
        raised = jnp.exp(scores)
        weights = raised / jnp.sum(raised, axis=2, keepdims=True)
        rounded = weights.astype(jnp.bfloat16)
        attended = jnp.einsum(
            "hqk,khd->qhd", rounded, value_heads, preferred_element_type=jnp.float32
        )
        inner = jnp.sum(grad_block.astype(jnp.float32) * attended, axis=2)
        grad_weights = jnp.einsum(
            "qhd,khd->hqk", grad_block, value_heads, preferred_element_type=jnp.float32
        )
        grad_scores = (weights * (grad_weights - inner.T[:, :, None])).astype(jnp.bfloat16)
        return (
            jnp.einsum("hqk,khd->qhd", grad_scores, key_round, preferred_element_type=jnp.float32)
            * score_scale
        )

    grad_rotated = lax.map(
        one_block,
        (
            query_round.reshape(block_count, block_rows, head_count, head_width),
            cotangent.reshape(block_count, block_rows, head_count, head_width),
        ),
    )
    grad_rotated = grad_rotated.reshape(length, head_count, head_width)
    grad_normed = grad_rotated * cosine[:, None, :] + jnp.roll(
        grad_rotated * sine_table[:, None, :], halfway, axis=2
    )
    grad_query = query_inverse * (
        grad_normed - query_normed * jnp.mean(grad_normed * query_normed, axis=2, keepdims=True)
    )
    return grad_query.reshape(length, width).astype(jnp.bfloat16)


def on_device(tokens, lattice, timestep, time_weight, query_weight, key_weight, values, cotangent):
    features = time_features(timestep, time_weight.shape[1])
    local_shift = jnp.einsum(
        "cf,jfd->cjd", features, time_weight, preferred_element_type=jnp.float32
    )
    own_shift = lax.all_to_all(
        local_shift.astype(jnp.bfloat16), "seq", split_axis=0, concat_axis=2, tiled=True
    ).astype(local_shift.dtype)
    hidden = tokens.astype(jnp.float32)
    average = jnp.mean(hidden, axis=1, keepdims=True)
    centred = hidden - average
    variance = jnp.mean(centred * centred, axis=1, keepdims=True)
    normed = centred * lax.rsqrt(variance + 1e-06)
    modulated = (normed * (1.0 + own_shift[0, 1][None, :]) + own_shift[0, 0][None, :]).astype(
        jnp.bfloat16
    )
    clip_rows = lax.all_gather(modulated, "head", axis=0, tiled=True)
    cosine, sine_table = rope_tables(lattice, HEAD_SIZE)
    own_query = query_weight[0]

    def contract(portion):
        return jnp.dot(clip_rows, portion, preferred_element_type=jnp.float32)

    query_pre = contract(lax.all_gather(own_query, "seq", axis=0, tiled=True))
    key_pre = contract(lax.all_gather(key_weight, "seq", axis=0, tiled=True))
    value_heads, cot_heads = (
        lax.all_to_all(values, "head", split_axis=1, concat_axis=0, tiled=True),
        lax.all_to_all(cotangent[0], "head", split_axis=1, concat_axis=0, tiled=True),
    )
    grad_query = attention_backward(
        query_pre, key_pre, value_heads, cot_heads, cosine, sine_table, HEAD_SIZE
    )
    grad = lax.dot_general(
        clip_rows, grad_query, (((0,), (0,)), ((), ())), preferred_element_type=jnp.float32
    )
    fisher = lax.psum_scatter(
        (grad * grad).astype(jnp.bfloat16), "seq", scatter_dimension=0, tiled=True
    ).astype(jnp.float32)
    weighted = fisher + damping
    upper = weighted * own_query.astype(jnp.float32)
    upper_sum, lower_sum = (
        lax.psum(upper.astype(jnp.bfloat16), "member").astype(jnp.float32),
        lax.psum(weighted.astype(jnp.bfloat16), "member").astype(jnp.float32),
    )
    merged = upper_sum / lower_sum
    return (fisher[None], merged)


def solution(mesh):
    return jax.shard_map(
        on_device,
        mesh=mesh,
        in_specs=(
            P(("seq", "head"), None),
            P(None, "seq"),
            P(),
            P(None, None, "seq"),
            P("member", "seq", "head"),
            P("seq", "head"),
            P(("seq", "head"), None),
            P("member", ("seq", "head"), None),
        ),
        out_specs=(P("member", "seq", "head"), P("seq", "head")),
        check_vma=False,
    )
```

profile of v0, /device:TPU:0, one launch (start us, length us, event | category | flops | bytes accessed | tf_op | source)
XLA Modules:
  0.0 561.1 jit_solution(5071785804502388701)
XLA Ops:
  7.2 0.0 copy-start
  7.2 0.8 convert_element_type.123
  8.0 0.1 fusion.40
  8.1 0.4 copy-done
  8.5 0.3 convolution_convert_fusion
  8.8 0.6 copy.22
  9.4 6.3 %all-to-all-start = ((bf16[4,2,1280]{2,1,0:T(2,128)(2,1)}), bf16[4,2,1280]{2,1,0:T(2,128)(2,1)S(1)}, u32[]{:S(2)}, u32[]{:S(2)}) async-start(bf16[4,2,1280]{2,1,0:T(2,128)(2,1)} %copy.22), calls=%async_computation | async-start | bytes 40960 | tf_op jit(solution)/shard_map/all_to_all | solution.py:120
  15.7 0.3 convert_reduce_fusion
  16.0 0.5 fusion.9
  16.5 4.8 all-to-all-done
  21.4 1.6 fusion.12
  23.1 0.0 all-gather.5.cloned.1.call-update
  23.1 0.0 all-gather.7.cloned.1.call-start
  23.1 0.7 all-gather.7.cloned.1.call-update
  23.8 0.0 all-gather.9.cloned.1.call-start
  23.9 0.7 all-gather.9.cloned.1.call-update
  24.6 0.0 copy-start.11
  24.6 1.1 copy.29
  25.7 3.5 all-to-all-start.2
  29.2 0.0 copy-start.17
  29.2 1.1 copy.27
  30.3 16.0 %all-to-all-done.2 = bf16[128,4,640]{0,2,1:T(8,128)(2,1)S(1)} async-done(((bf16[128,4,640]{0,2,1:T(8,128)(2,1)}), bf16[128,4,640]{0,2,1:T(8,128)(2,1)S(1)}, u32[]{:S(2)}, u32[]{:S(2)}) %all-to-all-start.2) | async-done | bytes 655392 | tf_op jit(solution)/shard_map/all_to_all | solution.py:141
  46.3 3.5 all-to-all-start.1
  49.8 0.0 reduce-scatter.2.cloned.1.call-start
  49.9 2.0 broadcast_multiply_fusion.3
  51.9 0.5 copy.30
  52.4 1.1 reshape.303
  53.5 13.9 %all-to-all-done.1 = bf16[128,4,640]{0,2,1:T(8,128)(2,1)S(1)} async-done(((bf16[128,4,640]{0,2,1:T(8,128)(2,1)}), bf16[128,4,640]{0,2,1:T(8,128)(2,1)S(1)}, u32[]{:S(2)}, u32[]{:S(2)}) %all-to-all-start.1) | async-done | bytes 655392 | tf_op jit(solution)/shard_map/all_to_all | solution.py:142
  67.4 0.5 copy.28
  67.9 1.1 squeeze.12
  69.0 7.1 %all-gather.5.cloned.1.call-done = bf16[512,5120]{1,0:T(8,128)(2,1)} async-done(((bf16[128,5120]{1,0:T(8,128)(2,1)}), bf16[512,5120]{1,0:T(8,128)(2,1)}) %all-gather.5.cloned.1.call-update) | async-done | bytes 5242896 | tf_op jit(solution)/shard_map/all_gather | solution.py:131
  76.0 118.7 %all-gather.7.cloned.1.call-done = bf16[5120,640]{1,0:T(8,128)(2,1)} async-done(((bf16[1280,640]{1,0:T(8,128)(2,1)}), bf16[5120,640]{1,0:T(8,128)(2,1)}) %all-gather.7.cloned.1.call-update) | async-done | bytes 6553616 | tf_op jit(solution)/shard_map/all_gather | solution.py:139
  194.8 8.4 %fusion.55 = f32[512,640]{0,1:T(8,128)S(1)} fusion(bf16[512,5120]{1,0:T(8,128)(2,1)} %all-gather.5.cloned.1.call-done, bf16[5120,640]{1,0:T(8,128)(2,1)} %all-gather.7.cloned.1.call-done), kind=kOutput, calls=%fused_computation.88 | convolution fusion | flops 3355443200 | bytes 13107200 | tf_op jit(solution)/shard_map/dot_general | solution.py:136
  203.2 0.2 multiply_reduce_fusion.1
  203.4 0.1 broadcast_multiply_fusion.1
  203.5 1.1 fusion.53
  204.7 109.6 %all-gather.9.cloned.1.call-done = bf16[1,5120,640]{2,1,0:T(8,128)(2,1)} async-done(((bf16[1,1280,640]{2,1,0:T(8,128)(2,1)}), bf16[1,5120,640]{2,1,0:T(8,128)(2,1)}) %all-gather.9.cloned.1.call-update) | async-done | bytes 6553616 | tf_op jit(solution)/shard_map/all_gather | solution.py:138
  314.3 8.6 %fusion = f32[512,640]{0,1:T(8,128)S(1)} fusion(bf16[512,5120]{1,0:T(8,128)(2,1)} %all-gather.5.cloned.1.call-done, bf16[1,5120,640]{2,1,0:T(8,128)(2,1)} %all-gather.9.cloned.1.call-done), kind=kOutput, calls=%fused_computation.1 | convolution fusion | flops 3355443200 | bytes 13107200 | tf_op jit(solution)/shard_map/dot_general | solution.py:136
  322.9 0.2 multiply_reduce_fusion.2
  323.0 0.1 broadcast_multiply_fusion.2
  323.2 0.1 fusion.52
  323.3 0.9 copy-done.6
  324.3 0.2 copy-done.7
  324.5 0.1 copy-done.8
  324.5 0.1 copy-done.9
  324.6 0.4 fusion.29
  325.0 1.1 fusion.3
  326.2 0.1 copy-done.13
  326.3 2.2 fusion.32
  328.5 5.9 %broadcast_multiply_fusion = (f32[512,5,128]{0,2,1:T(8,128)}, f32[512,5,128]{0,2,1:T(8,128)S(1)}) fusion(f32[512,128]{0,1:T(8,128)} %get-tuple-element.32, bf16[512,5,128]{0,2,1:T(8,128)(2,1)S(1)} %fusion.29, bf16[512,5,128]{0,2,1:T(8,128)(2,1)} %squeeze.12, bf16[512,5,128]{0,2,1:T(8,128)(2,1)} %reshape.303, f32[5,512]{1,0:T(8,128)} %bitcast.71, ...), kind=kOutput, calls=%fused_computation.43 | convolution fusion | flops 677969920 | bytes 10113024 | tf_op jit(solution)/shard_map/while/body/eval_jaxpr/hqk,khd->qhd/dot_general | solution.py:94
  334.4 1.6 fusion.51
  336.0 0.5 multiply_reduce_fusion
  336.5 0.6 multiply_convert_fusion.5
  337.1 0.4 slice-done.1
  337.5 6.3 %multiply_convert_fusion = bf16[5120,640]{1,0:T(8,128)(2,1)} fusion(bf16[512,5120]{1,0:T(8,128)(2,1)S(1)} %bitcast.70, bf16[512,640]{0,1:T(8,128)(2,1)S(1)} %bitcast.62), kind=kOutput, calls=%fused_computation | convolution fusion | flops 3361996800 | bytes 12451840 | tf_op jit(solution)/shard_map/dot_general | solution.py:147
  343.8 0.0 reduce-scatter.2.cloned.1.call-update
  343.8 0.0 all-reduce.3.cloned.1.call-start
  343.8 113.3 %reduce-scatter.2.cloned.1.call-done = bf16[1280,640]{1,0:T(8,128)(2,1)} async-done(((bf16[5120,640]{1,0:T(8,128)(2,1)}), bf16[1280,640]{1,0:T(8,128)(2,1)}) %reduce-scatter.2.cloned.1.call-update) | async-done | bytes 1638416 | tf_op jit(solution)/shard_map/reduce_scatter | solution.py:150
  457.2 3.7 fusion.6
  460.9 0.0 all-reduce.3.cloned.1.call-update
  460.9 1.4 copy-done.4
  462.3 1.9 convert_bitcast_fusion
  464.3 86.2 %all-reduce.3.cloned.1.call-done = (bf16[1280,640]{1,0:T(8,128)(2,1)}, bf16[1280,640]{1,0:T(8,128)(2,1)}) async-done(((bf16[1280,640]{1,0:T(8,128)(2,1)}, bf16[1280,640]{1,0:T(8,128)(2,1)}), (bf16[1280,640]{1,0:T(8,128)(2,1)}, bf16[1280,640]{1,0:T(8,128)(2,1)})) %all-reduce.3.cloned.1.call-update) | async-done | bytes 3276816 | tf_op jit(solution)/shard_map/psum | solution.py:157
  550.4 4.2 convert_divide_fusion
  (43 shorter events, 0.2 us)
Async XLA Ops:
  7.2 1.3 copy-start
  7.2 8.6 %copy-start.2 = (bf16[128,5120]{1,0:T(8,128)(2,1)S(1)}, bf16[128,5120]{1,0:T(8,128)(2,1)}, u32[]{:S(2)}) copy-start(bf16[128,5120]{1,0:T(8,128)(2,1)} %param.8) | copy-start | bytes 3932164
  9.4 11.9 %all-to-all-start = ((bf16[4,2,1280]{2,1,0:T(2,128)(2,1)}), bf16[4,2,1280]{2,1,0:T(2,128)(2,1)S(1)}, u32[]{:S(2)}, u32[]{:S(2)}) async-start(bf16[4,2,1280]{2,1,0:T(2,128)(2,1)} %copy.22), calls=%async_computation | async-start | bytes 40960 | tf_op jit(solution)/shard_map/all_to_all | solution.py:120
  15.7 60.3 %all-gather.5.cloned.1.call-start = ((), (), s32[]{:S(2)}) async-start(), calls=%async_computation.4 | async-start | bytes 6553600 | tf_op jit(solution)/shard_map/all_gather | solution.py:131
  23.1 1.5 copy-start.10
  23.1 171.7 %all-gather.7.cloned.1.call-start = ((), (), s32[]{:S(2)}) async-start(), calls=%async_computation.5 | async-start | bytes 8192000 | tf_op jit(solution)/shard_map/all_gather | solution.py:139
  23.8 290.4 %all-gather.9.cloned.1.call-start = ((), (), s32[]{:S(2)}) async-start(), calls=%async_computation.7 | async-start | bytes 8192000 | tf_op jit(solution)/shard_map/all_gather | solution.py:138
  24.6 4.6 copy-start.11
  25.7 20.7 %all-to-all-start.2 = ((bf16[128,4,640]{0,2,1:T(8,128)(2,1)}), bf16[128,4,640]{0,2,1:T(8,128)(2,1)S(1)}, u32[]{:S(2)}, u32[]{:S(2)}) async-start(bf16[128,4,640]{0,2,1:T(8,128)(2,1)} %bitcast.16), calls=%async_computation.2 | async-start | bytes 1310720 | tf_op jit(solution)/shard_map/all_to_all | solution.py:141
  29.2 20.7 %copy-start.17 = (s32[3,512]{1,0:T(4,128)S(1)}, s32[3,512]{1,0:T(4,128)}, u32[]{:S(2)}) copy-start(s32[3,512]{1,0:T(4,128)} %param.9) | copy-start | bytes 18436
  46.3 21.0 %all-to-all-start.1 = ((bf16[128,4,640]{0,2,1:T(8,128)(2,1)}), bf16[128,4,640]{0,2,1:T(8,128)(2,1)S(1)}, u32[]{:S(2)}, u32[]{:S(2)}) async-start(bf16[128,4,640]{0,2,1:T(8,128)(2,1)} %bitcast.14), calls=%async_computation.1 | async-start | bytes 1310720 | tf_op jit(solution)/shard_map/all_to_all | solution.py:142
  49.8 407.3 %reduce-scatter.2.cloned.1.call-start = ((), (), s32[]{:S(2)}) async-start(), calls=%async_computation.6 | async-start | bytes 8192000 | tf_op jit(solution)/shard_map/reduce_scatter | solution.py:150
  203.4 1.3 copy-start.14
  323.2 1.1 copy-start.6
  323.2 1.3 copy-start.7
  323.2 1.3 copy-start.8
  323.2 1.4 copy-start.9
  323.2 1.4 copy-start.15
  325.0 1.2 copy-start.12
  325.0 1.3 copy-start.13
  326.2 2.3 copy-start.5
  326.2 2.3 copy-start.16
  334.4 2.7 slice-start
  336.0 1.5 slice-start.1
  343.8 113.4 %copy-start.3 = (bf16[1,1280,640]{2,1,0:T(8,128)(2,1)S(1)}, bf16[1,1280,640]{2,1,0:T(8,128)(2,1)}, u32[]{:S(2)}) copy-start(bf16[1,1280,640]{2,1,0:T(8,128)(2,1)} %param.12) | copy-start | bytes 4915204
  343.8 206.6 %all-reduce.3.cloned.1.call-start = ((), (), s32[]{:S(2)}) async-start(), calls=%async_computation.8 | async-start | bytes 6553600 | tf_op jit(solution)/shard_map/psum | solution.py:157
  460.9 1.4 copy-start.4
  550.4 4.2 copy-start.1
Sparse Core Ops, SparseCore 0:
  23.2 52.7 all-gather.4
  77.6 117.1 all-gather.6
  196.4 117.8 all-gather.8
  343.9 113.2 reduce-scatter.1
  461.1 89.3 all-reduce.2
where the time goes:
time: 562 us; the launch traced here: 561 us
  waiting for transfers between devices  471 us (84%)
  matrix products  32.7 us (6%)
  other arithmetic  17.3 us (3%)
  between operations  14.1 us (3%)
  starting transfers between devices  13.5 us (2%)
  local copies, waits for them, and re-layouts  12.4 us (2%)
    all_gather x1, waiting for transfers between devices, on_device(): key_pre = contract(lax.all_gather(key_weight, 'seq', axis=0, tiled=True))  119 us
    reduce_scatter x1, waiting for transfers between devices, on_device(): lax.psum_scatter((grad * grad).astype(jnp.bfloat16), 'seq', scatter_dimen...  113 us
    all_gather x1, waiting for transfers between devices, on_device(): query_pre = contract(lax.all_gather(own_query, 'seq', axis=0, tiled=True))  110 us
    psum x1, waiting for transfers between devices, on_device(): lax.psum(weighted.astype(jnp.bfloat16), 'member').astype(jnp.float32)  86.2 us
    dot_general x2, matrix products, contract(): return jnp.dot(clip_rows, portion, preferred_element_type=jnp.float32)  17 us
    all_to_all x1, waiting for transfers between devices, on_device(): lax.all_to_all(values, 'head', split_axis=1, concat_axis=0, tiled=True)  16 us
    all_to_all x1, waiting for transfers between devices, on_device(): lax.all_to_all(cotangent[0], 'head', split_axis=1, concat_axis=0, tiled=T...  13.9 us
  transfers between devices with their start and end apart: 8, of which 8 were waited for; matrix products, arithmetic and copies ran while one was open for 4% of the time, Pallas kernels for 0%

commit v1 on v0

v1 whole, which is shorter than its diff:
```python
import functools
import math

import jax
import jax.numpy as jnp
from jax import lax
from jax.experimental import pallas as pl
from jax.experimental.pallas import tpu as pltpu
from jax.sharding import PartitionSpec as P

HEAD_SIZE = 128
damping = 0.01
VMEM_BYTES = 56 * 1024 * 1024


def time_features(timestep, feature_count):
    halfway = feature_count // 2
    ladder = jnp.arange(halfway).astype(jnp.float32)
    frequency = jnp.exp(-math.log(10000.0) * 2.0 * ladder / feature_count)
    angles = timestep.astype(jnp.float32)[:, None] * frequency[None, :]
    return jnp.concatenate([jnp.cos(angles), jnp.sin(angles)], axis=1).astype(jnp.bfloat16)


def rope_tables(lattice, head_width):
    halfway = head_width // 2
    side_pairs = head_width // 6
    frame_pairs = halfway - 2 * side_pairs
    column = jnp.arange(head_width)
    pair_index = column % halfway
    which_axis = jnp.where(
        pair_index < frame_pairs, 0, jnp.where(pair_index < frame_pairs + side_pairs, 1, 2)
    )
    anchor = jnp.where(
        which_axis == 0, 0, jnp.where(which_axis == 1, frame_pairs, frame_pairs + side_pairs)
    )
    pair_span = jnp.where(which_axis == 0, frame_pairs, side_pairs)
    frequency = jnp.exp(
        -math.log(10000.0)
        * (pair_index - anchor).astype(jnp.float32)
        / pair_span.astype(jnp.float32)
    )
    position = lattice.astype(jnp.float32)
    angles = jnp.zeros((lattice.shape[1], head_width), jnp.float32)
    for axis_number in range(3):
        chosen = jnp.where(which_axis == axis_number, frequency, 0.0)
        angles = angles + position[axis_number][:, None] * chosen[None, :]
    sign_flip = jnp.where(column < halfway, -1.0, 1.0).astype(jnp.float32)
    return (jnp.cos(angles), jnp.sin(angles) * sign_flip[None, :])


def partner(rows):
    return pltpu.roll(rows, rows.shape[1] // 2, 1)


def head_rotation(rows, cosine, sine):
    inverse = lax.rsqrt(jnp.mean(rows * rows, axis=1, keepdims=True) + 1e-06)
    normed = rows * inverse
    return normed, inverse, normed * cosine + partner(normed) * sine


def rotate_kernel(rows_ref, cosine_ref, sine_ref, out_ref):
    out_ref[...] = head_rotation(rows_ref[...], cosine_ref[...], sine_ref[...])[2].astype(
        out_ref.dtype
    )


def rotate_heads(rows, cosine, sine):
    length, width = rows.shape
    column = pl.BlockSpec((length, HEAD_SIZE), lambda j: (0, j))
    table = pl.BlockSpec((length, HEAD_SIZE), lambda j: (0, 0))
    return pl.pallas_call(
        rotate_kernel,
        grid=(width // HEAD_SIZE,),
        in_specs=[column, table, table],
        out_specs=column,
        out_shape=jax.ShapeDtypeStruct((length, width), jnp.bfloat16),
        compiler_params=pltpu.CompilerParams(vmem_limit_bytes=VMEM_BYTES),
        name="rotate_heads",
    )(rows, cosine, sine)


def attention_kernel(query_ref, key_ref, value_ref, cot_ref, cosine_ref, sine_ref, out_ref):
    cosine, sine = cosine_ref[...], sine_ref[...]
    key, value, cot = key_ref[...], value_ref[...], cot_ref[...]
    scale = query_ref.shape[1] ** (-0.5)
    normed, inverse, rotated = head_rotation(query_ref[...], cosine, sine)
    across = (((1,), (1,)), ((), ()))
    scores = lax.dot_general(
        rotated.astype(jnp.bfloat16), key, across, preferred_element_type=jnp.float32
    )
    raised = jnp.exp2(scores * (scale * math.log2(math.e)))
    weights = raised * (1.0 / jnp.sum(raised, axis=1, keepdims=True))
    attended = jnp.dot(weights.astype(jnp.bfloat16), value, preferred_element_type=jnp.float32)
    inner = jnp.sum(cot.astype(jnp.float32) * attended, axis=1, keepdims=True)
    grad_weights = lax.dot_general(cot, value, across, preferred_element_type=jnp.float32)
    grad_scores = (weights * (grad_weights - inner)).astype(jnp.bfloat16)
    grad_rotated = jnp.dot(grad_scores, key, preferred_element_type=jnp.float32) * scale
    grad_normed = grad_rotated * cosine + partner(grad_rotated * sine)
    shared = jnp.mean(grad_normed * normed, axis=1, keepdims=True)
    grad_query = inverse * (grad_normed - normed * shared)
    out_ref[...] = grad_query.T.astype(out_ref.dtype)


def attention_grad(query_pre, key, value, cot, cosine, sine, first, count):
    length = query_pre.shape[0]
    column = pl.BlockSpec((length, HEAD_SIZE), lambda j: (0, j + first))
    table = pl.BlockSpec((length, HEAD_SIZE), lambda j: (0, 0))
    return pl.pallas_call(
        attention_kernel,
        grid=(count,),
        in_specs=[column, column, column, column, table, table],
        out_specs=pl.BlockSpec((HEAD_SIZE, length), lambda j: (j, 0)),
        out_shape=jax.ShapeDtypeStruct((count * HEAD_SIZE, length), jnp.bfloat16),
        compiler_params=pltpu.CompilerParams(vmem_limit_bytes=VMEM_BYTES),
        name="attention_grad",
    )(query_pre, key, value, cot, cosine, sine)


def row_tile(rows):
    return 256 if rows % 256 == 0 else rows


def fisher_kernel(groups, *refs):
    rows, grads, own_ref, low_ref = refs[:groups], refs[groups:-2], refs[-2], refs[-1]

    def squared(clip, grad):
        total, start = 0.0, 0
        for ref in rows:
            block = ref[clip]
            part = grad[:, start : start + block.shape[0]]
            total = total + jnp.dot(part, block, preferred_element_type=jnp.float32)
            start += block.shape[0]
        return total * total

    total = jnp.zeros(own_ref.shape[::-1], jnp.float32)
    clip = 0
    for ref in grads:
        if len(ref.shape) == 2:
            total = total + squared(clip, ref[...])
            clip += 1
        else:
            total = lax.fori_loop(0, ref.shape[0], lambda i, t: t + squared(i, ref[i]), total)
            clip += ref.shape[0]
    fisher = total.T
    own_ref[...] = fisher
    low_ref[...] = fisher.astype(low_ref.dtype)


def drop(kernel, place):
    def run(*refs):
        kernel(*refs[:place], *refs[place + 1 :])

    return run


def in_place(kernel, inputs, specs, previous):
    if previous is None:
        return kernel, inputs, specs, {}
    place = len(inputs)
    return (
        drop(kernel, place),
        list(inputs) + [previous],
        list(specs) + [pl.BlockSpec(memory_space=pl.ANY)],
        {place: 0},
    )


def fisher_rows(rows, grads, first, total_columns, previous):
    width = rows[0].shape[2]
    columns = grads[0].shape[-2]
    tile = row_tile(width)
    specs = [pl.BlockSpec((block.shape[0], block.shape[1], tile), lambda i: (0, 0, i)) for block in rows]
    specs += [pl.BlockSpec(grad.shape, lambda i, n=grad.ndim: (0,) * n) for grad in grads]
    kernel, inputs, specs, aliases = in_place(
        functools.partial(fisher_kernel, len(rows)), [*rows, *grads], specs, previous
    )
    return pl.pallas_call(
        kernel,
        grid=(width // tile,),
        in_specs=specs,
        out_specs=[
            pl.BlockSpec((pl.Element(tile), pl.Element(columns)), lambda i: (i * tile, first)),
            pl.BlockSpec((tile, columns), lambda i: (i, 0)),
        ],
        out_shape=[
            jax.ShapeDtypeStruct((width, total_columns), jnp.float32),
            jax.ShapeDtypeStruct((width, columns), jnp.bfloat16),
        ],
        input_output_aliases=aliases,
        compiler_params=pltpu.CompilerParams(vmem_limit_bytes=VMEM_BYTES),
        name="fisher_rows",
    )(*inputs)


def merge_kernel(here_ref, there_ref, own_ref, other_ref, out_ref):
    zero = lax.axis_index("member") == 0
    here, there = to_f32(here_ref[...]) + damping, to_f32(there_ref[...]) + damping
    one, two = here * to_f32(own_ref[...]), there * to_f32(other_ref[...])
    upper = jnp.where(zero, one, two) + jnp.where(zero, two, one)
    out_ref[...] = upper / (here + there)


def merge_rows(here, there, own_weight, other_weight, first, previous):
    width, columns = here.shape
    tile = row_tile(width)
    plain = pl.BlockSpec((tile, columns), lambda i: (i, 0))
    part = pl.BlockSpec((pl.Element(tile), pl.Element(columns)), lambda i: (i * tile, first))
    kernel, inputs, specs, aliases = in_place(
        merge_kernel, [here, there, own_weight, other_weight], [plain, plain, part, part], previous
    )
    return pl.pallas_call(
        kernel,
        grid=(width // tile,),
        in_specs=specs,
        out_specs=part,
        out_shape=jax.ShapeDtypeStruct(own_weight.shape, jnp.float32),
        input_output_aliases=aliases,
        compiler_params=pltpu.CompilerParams(vmem_limit_bytes=VMEM_BYTES),
        name="merge_rows",
    )(*inputs)


def spread_kernel(place_ref, rows_ref, *outs):
    rows = to_f32(rows_ref[...])
    average = jnp.mean(rows, axis=1, keepdims=True)
    centred = rows - average
    inverse = lax.rsqrt(jnp.mean(centred * centred, axis=1, keepdims=True) + 1e-06)
    size, width = len(outs), outs[0].shape[1]
    for away, out_ref in enumerate(outs):
        start = pl.multiple_of(lax.rem(place_ref[1] + away, size) * width, 128)
        part = to_f32(rows_ref[:, pl.ds(start, width)])
        out_ref[...] = ((part - average) * inverse).astype(out_ref.dtype)


def spread_rows(tokens, member, place, share, size):
    width = tokens.shape[1] // size
    return pl.pallas_call(
        spread_kernel,
        grid_spec=pltpu.PrefetchScalarGridSpec(
            num_scalar_prefetch=1,
            grid=(1,),
            in_specs=[pl.BlockSpec((share, tokens.shape[1]), lambda i, where: (where[0], 0))],
            out_specs=[pl.BlockSpec((share, width), lambda i, where: (0, 0))] * size,
        ),
        out_shape=[jax.ShapeDtypeStruct((share, width), jnp.bfloat16)] * size,
        compiler_params=pltpu.CompilerParams(vmem_limit_bytes=VMEM_BYTES),
        name="spread_rows",
    )(jnp.stack([member, place]).astype(jnp.int32), tokens)


def modulate(rows, modulation):
    return (rows * (1.0 + modulation[1:2]) + modulation[0:1]).astype(jnp.bfloat16)


def project_kernel(pieces, weights, waits, *refs):
    piece_refs, modulation_ref = refs[:pieces], refs[pieces]
    weight_refs = refs[pieces + 1 : pieces + 1 + weights]
    rows_ref, *outs = refs[pieces + 1 + weights + waits :]
    size = rows_ref.shape[0]
    share = piece_refs[0].shape[1]
    order = sorted(range(size), key=lambda away: -min(away, size - away))
    for away in order:
        modulation = modulation_ref[away]
        for i, ref in enumerate(piece_refs):
            rows_ref[away, i * share : (i + 1) * share] = modulate(to_f32(ref[away]), modulation)
        for i, ref in enumerate(weight_refs):
            start = i * pieces * share
            outs[away][start : start + pieces * share] = jnp.dot(
                rows_ref[away], ref[...], preferred_element_type=jnp.float32
            ).astype(outs[away].dtype)


def project_rows(pieces, modulation, weights, waits):
    size, share, width = pieces[0].shape
    length, columns = len(pieces) * share, weights[0].shape[1]
    types = [jnp.bfloat16 if 2 * away == size else jnp.float32 for away in range(size)]
    whole = pl.BlockSpec(memory_space=pltpu.VMEM)
    return pl.pallas_call(
        functools.partial(project_kernel, len(pieces), len(weights), len(waits)),
        in_specs=[whole] * (len(pieces) + 1 + len(weights))
        + [pl.BlockSpec(memory_space=pl.ANY)] * len(waits),
        out_specs=[whole] * (1 + size),
        out_shape=[jax.ShapeDtypeStruct((size, length, width), jnp.bfloat16)]
        + [jax.ShapeDtypeStruct((len(weights) * length, columns), kind) for kind in types],
        compiler_params=pltpu.CompilerParams(vmem_limit_bytes=VMEM_BYTES),
        name="project_rows",
    )(*pieces, modulation, *weights, *waits)


def to_f32(block):
    return block.astype(jnp.float32)


class Ring:
    def __init__(self, size):
        self.size = size
        self.place = lax.axis_index("seq")
        self.short = size <= 8 and size % 2 == 0

    def by_distance(self, blocks):
        return jnp.take(blocks, (self.place - jnp.arange(self.size)) % self.size, axis=0)

    def step(self, block, away):
        pairs = [(i, (i + away) % self.size) for i in range(self.size)]
        return lax.ppermute(block, "seq", pairs)

    def exchange(self, tokens, member, share):
        size = self.size
        width = tokens.shape[1] // size
        if self.short and width % 128 == 0:
            parts = spread_rows(tokens, member, self.place, share, size)
            return jnp.stack(
                list(parts[:1]) + [self.step(part, away) for away, part in enumerate(parts) if away]
            )
        mine = to_f32(lax.dynamic_slice_in_dim(tokens, member * share, share, 0))
        centred = mine - jnp.mean(mine, axis=1, keepdims=True)
        variance = jnp.mean(centred * centred, axis=1, keepdims=True)
        normed = (centred * lax.rsqrt(variance + 1e-06)).astype(jnp.bfloat16)
        parts = normed.reshape(share, size, width)
        return self.by_distance(
            lax.all_to_all(parts, "seq", split_axis=1, concat_axis=0, tiled=False)
        )

    def project(self, pieces, modulation, weights, waits):
        size, half = self.size, self.size // 2
        if not self.short:
            rows = jnp.concatenate(pieces, axis=1)
            rows = jax.vmap(modulate)(to_f32(rows), modulation)
            terms = [
                jnp.einsum("crw,wn->crn", rows, weight, preferred_element_type=jnp.float32)
                for weight in weights
            ]
            terms = jnp.concatenate(terms, axis=1).astype(jnp.bfloat16)
            total = to_f32(lax.psum_scatter(self.by_distance(terms), "seq", tiled=False))
            return rows, total, total
        rows, *terms = project_rows(pieces, modulation, weights, waits)
        middle = terms[0].shape[0] // 2
        right = self.step(terms[half][:middle], 1)
        left = self.step(terms[half][middle:], -1)
        sent = right
        for away in range(half - 1, 0, -1):
            term_right, term_left = terms[size - away], terms[away]
            if away == half - 1:
                term_right = jnp.concatenate(
                    [term_right[:middle] + to_f32(right), term_right[middle:]], axis=0
                )
                term_left = jnp.concatenate(
                    [term_left[:middle], term_left[middle:] + to_f32(left)], axis=0
                )
            else:
                term_right, term_left = term_right + to_f32(right), term_left + to_f32(left)
            sent = term_left.astype(jnp.bfloat16)
            right = self.step(term_right.astype(jnp.bfloat16), 1)
            left = self.step(sent, -1)
        if half == 1:
            total = terms[0] + to_f32(jnp.concatenate([right, left], axis=0))
        else:
            total = terms[0] + to_f32(right) + to_f32(left)
        return rows, total, sent

    def gather(self, block):
        size, half = self.size, self.size // 2
        if not self.short:
            return [self.by_distance(lax.all_gather(block, "seq"))]
        blocks = [None] * size
        blocks[0] = block
        right, left = block, block
        for away in range(1, half):
            right, left = self.step(right, 1), self.step(left, -1)
            blocks[away], blocks[size - away] = right, left
        middle = block.shape[0] // 2
        blocks[half] = jnp.concatenate(
            [self.step(right[:middle], 1), self.step(left[middle:], -1)], axis=0
        )
        return blocks


def on_device(
    axes, tokens, lattice, timestep, time_weight, query_weight, key_weight, values, cotangent
):
    members, clips, heads = axes
    member = lax.axis_index("member")
    clip = lax.axis_index("seq")
    head = lax.axis_index("head")
    own_query = query_weight[0]
    width, columns = own_query.shape
    share = tokens.shape[0] // members

    ring = Ring(clips)

    def x_swap(block):
        return lax.ppermute(block, "member", [(i, i ^ 1) for i in range(members)])

    def h_swap(block, bits):
        return lax.ppermute(block, "head", [(i, i ^ bits) for i in range(heads)])

    own = ring.exchange(tokens, member, share)

    near_y = h_swap(own, 2)
    near_x, far = x_swap(own), x_swap(near_y)

    ordered = timestep[(clip - jnp.arange(clips)) % clips]
    features = time_features(ordered, time_weight.shape[1])
    modulation = jnp.einsum(
        "cf,jfd->cjd", features, time_weight, preferred_element_type=jnp.float32
    )

    def both(block):
        return [block, h_swap(block, 1)]

    rows_near, near, sent = ring.project(
        both(own) + both(near_y), modulation, [own_query, key_weight], []
    )
    rows_far, query_far, _ = ring.project(
        both(near_x) + both(far), modulation, [own_query], [sent]
    )
    rows_here = near.shape[0] // 2
    query_near, key_here = near[:rows_here], near[rows_here:]
    query_pre = jnp.concatenate([query_near, query_far], axis=0)

    grid = lattice.reshape(3, 2, 2, members, share).transpose(0, 3, 1, 2, 4)
    for axis, bit in ((1, member), (2, head // 2), (3, head % 2)):
        grid = jnp.where(bit == 1, jnp.flip(grid, axis), grid)
    cosine, sine = rope_tables(grid.reshape(3, -1), HEAD_SIZE)

    pair = jnp.stack([values, cotangent[0]])
    blocks = []
    for bits in range(heads):
        block = lax.dynamic_slice_in_dim(pair, (head ^ bits) * columns, columns, 2)
        blocks.append(h_swap(block, bits) if bits else block)
    halves = jnp.stack(blocks, axis=1).reshape(2, heads, members, share, columns)
    halves = jnp.concatenate(
        [lax.dynamic_slice_in_dim(halves, member ^ i, 1, 2)[:, :, 0] for i in range(members)], axis=1
    ).reshape(2, members * heads * share, columns)
    value_rows, cot_rows = halves[0], halves[1]

    key_here = rotate_heads(key_here, cosine[:rows_here], sine[:rows_here])
    key_rows = jnp.concatenate([key_here, x_swap(key_here)], axis=0)

    other_query = x_swap(lax.optimization_barrier((own_query, far))[0])

    head_count = columns // HEAD_SIZE
    bounds = [0, (head_count + 1) // 2, head_count]
    fisher, merged = None, None
    for first, last in zip(bounds[:-1], bounds[1:]):
        grad_query = attention_grad(
            query_pre, key_rows, value_rows, cot_rows, cosine, sine, first, last - first
        )
        fisher, low = fisher_rows(
            [rows_near, rows_far], ring.gather(grad_query), first * HEAD_SIZE, columns, fisher
        )
        merged = merge_rows(
            low, x_swap(low), own_query, other_query, first * HEAD_SIZE, merged
        )
    return fisher[None], merged


def solution(mesh):
    axes = (mesh.shape["member"], mesh.shape["seq"], mesh.shape["head"])
    return jax.shard_map(
        functools.partial(on_device, axes),
        mesh=mesh,
        in_specs=(
            P(("seq", "head"), None),
            P(None, "seq"),
            P(),
            P(None, None, "seq"),
            P("member", "seq", "head"),
            P("seq", "head"),
            P(("seq", "head"), None),
            P("member", ("seq", "head"), None),
        ),
        out_specs=(P("member", "seq", "head"), P("seq", "head")),
        check_vma=False,
    )
```

time: 562 us -> 221 us (0.39)
  waiting for transfers between devices: 471 us -> 88.7 us
  Pallas kernels: 0 us -> 61.2 us
  starting transfers between devices: 13.5 us -> 46.6 us
  matrix products: 32.7 us -> 0.28 us
  between operations: 14.1 us -> 1.21 us
  other arithmetic: 17.3 us -> 10.8 us
    all_gather x3 -> x0, waiting for transfers between devices: 235 us -> none  [the longest x1 119 us: on_device(): key_pre = contract(lax.all_gather(key_weight, 'seq', axis=0, tiled=True))]
    reduce_scatter x1 -> x0, waiting for transfers between devices: 113 us -> none  [on_device(): lax.psum_scatter((grad * grad).astype(jnp.bfloat16), 'seq', scatter_dimen...]
    ppermute x0 -> x33, waiting for transfers between devices: none -> 88.7 us  [the longest x19 67 us: step(): return lax.ppermute(block, 'seq', pairs)]
    psum x1 -> x0, waiting for transfers between devices: 86.2 us -> none  [on_device(): lax.psum(weighted.astype(jnp.bfloat16), 'member').astype(jnp.float32)]
    pallas_call x0 -> x10, Pallas kernels: none -> 61.2 us  [the longest x2 15.1 us: project_rows(): pl.pallas_call(functools.partial(project_kernel, len(pieces), len(weights...]
    ppermute x0 -> x33, starting transfers between devices: none -> 46.6 us  [the longest x19 36.5 us: step(): return lax.ppermute(block, 'seq', pairs)]
    all_to_all x3 -> x0, waiting for transfers between devices: 34.7 us -> none  [the longest x1 16 us: on_device(): lax.all_to_all(values, 'head', split_axis=1, concat_axis=0, tiled=True)]
    dot_general x6 -> x0, matrix products: 32.5 us -> none  [the longest x2 17 us: contract(): return jnp.dot(clip_rows, portion, preferred_element_type=jnp.float32)]
  transfers between devices with their start and end apart: 8 -> 33, of which waited for: 8 -> 14; matrix products, arithmetic and copies ran while one was open for 4% -> 7% of each run, Pallas kernels for 0% -> 20%
where the time goes in v1:
time: 221 us; the launch traced here: 220 us
  waiting for transfers between devices  88.7 us (40%)
  Pallas kernels  61.2 us (28%)
  starting transfers between devices  46.6 us (21%)
  local copies, waits for them, and re-layouts  11.1 us (5%)
  other arithmetic  10.8 us (5%)
    ppermute x19, waiting for transfers between devices, step(): return lax.ppermute(block, 'seq', pairs)  67 us
    ppermute x19, starting transfers between devices, step(): return lax.ppermute(block, 'seq', pairs)  36.5 us
    pallas_call x2, Pallas kernels, project_rows(): pl.pallas_call(functools.partial(project_kernel, len(pieces), len(weights...  15.1 us
    pallas_call x2, Pallas kernels, attention_grad(): pl.pallas_call(attention_kernel, grid=(count,), in_specs=[column, column,...  14.9 us
    ppermute x8, waiting for transfers between devices, h_swap(): return lax.ppermute(block, 'head', [(i, i ^ bits) for i in range(heads)])  14.5 us
    pallas_call x2, Pallas kernels, fisher_rows(): pl.pallas_call(kernel, grid=(width // tile,), in_specs=specs, out_specs=[...  13.9 us
    pallas_call x2, Pallas kernels, merge_rows(): pl.pallas_call(kernel, grid=(width // tile,), in_specs=specs, out_specs=p...  9.98 us
    ppermute x6, waiting for transfers between devices, x_swap(): return lax.ppermute(block, 'member', [(i, i ^ 1) for i in range(members)])  7.18 us
  transfers between devices with their start and end apart: 33, of which 14 were waited for; matrix products, arithmetic and copies ran while one was open for 7% of the time, Pallas kernels for 20%

profile of v1, /device:TPU:0, one launch (start us, length us, event | category | flops | bytes accessed | tf_op | source)
XLA Modules:
  0.0 219.8 jit_solution(10980536341787292502)
XLA Ops:
  0.7 0.6 pad_add_fusion.place_ref
  1.3 3.3 %spread_rows.1 = (bf16[64,1280]{1,0:T(8,128)(2,1)}, bf16[64,1280]{1,0:T(8,128)(2,1)}, bf16[64,1280]{1,0:T(8,128)(2,1)}, bf16[64,1280]{1,0:T(8,128)(2,1)}) custom-call(s32[2]{0:T(128)} %pad_add_fusion.place_ref, bf16[128,5120]{1,0:T(8,128)(2,1)} %rows_ref.1), custom_call_target="tpu_custom_call" | custom-call | tf_op jit(solution)/shard_map/spread_rows/pallas_call | solution.py:237
  4.5 5.0 %collective-permute-start.2 = (bf16[64,1280]{1,0:T(8,128)(2,1)}, bf16[64,1280]{1,0:T(8,128)(2,1)}, u32[]{:S(2)}, u32[]{:S(2)}) collective-permute-start(bf16[64,1280]{1,0:T(8,128)(2,1)} %get-tuple-element.24), channel_id=1, source_target_pairs={{0,12},{4,0},{8,4},{12,8},{1,13},{5,1},{9,5},{13,9},{2,14},{6,2},{... | collective-permute-start | bytes 491528 | tf_op jit(solution)/shard_map/ppermute | solution.py:305
  9.6 1.0 collective-permute-start
  10.6 1.0 fusion.2
  11.7 1.4 collective-permute-start.20
  13.4 0.6 gather_fusion
  14.5 9.2 %collective-permute-done.1 = bf16[64,1280]{1,0:T(8,128)(2,1)} collective-permute-done((bf16[64,1280]{1,0:T(8,128)(2,1)}, bf16[64,1280]{1,0:T(8,128)(2,1)}, u32[]{:S(2)}, u32[]{:S(2)}) %collective-permute-start.1) | collective-permute-done | bytes 163872 | tf_op jit(solution)/shard_map/ppermute | solution.py:305
  23.8 1.2 pad_maximum_fusion.3.refs_0_
  24.9 1.6 collective-permute-start.4
  26.9 1.6 collective-permute-start.6
  28.5 14.5 %collective-permute-done.4.refs_2_ = bf16[4,64,1280]{2,1,0:T(8,128)(2,1)} collective-permute-done((bf16[4,64,1280]{2,1,0:T(8,128)(2,1)S(1)}, bf16[4,64,1280]{2,1,0:T(8,128)(2,1)}, u32[]{:S(2)}, u32[]{:S(2)}) %collective-permute-start.4) | collective-permute-done | bytes 655392 | tf_op jit(solution)/shard_map/ppermute | solution.py:395
  43.8 1.6 collective-permute-start.8
  45.3 1.0 sine_multiply_fusion
  46.4 0.7 copy.16.refs_4_
  47.1 0.7 slice.120.cosine_ref
  47.8 0.7 slice.121.sine_ref
  48.4 1.4 pad_maximum_fusion.1
  50.1 8.9 %project_rows.2 = (bf16[4,256,1280]{2,1,0:T(8,128)(2,1)}, f32[512,640]{1,0:T(8,128)}, f32[512,640]{1,0:T(8,128)}, bf16[512,640]{1,0:T(8,128)(2,1)}, f32[512,640]{1,0:T(8,128)}) custom-call(bf16[4,64,1280]{2,1,0:T(8,128)(2,1)} %copy-done.7, bf16[4,64,1280]{2,1,0:T(8,128)(2,1)} %collective-permute-done.3.refs_1_, ...), custom_call_target="tpu_custom_call" | custom-call | tf_op jit(solution)/shard_map/project_rows/pallas_call | solution.py:278
  59.0 1.1 fusion.18
  60.2 2.9 %collective-permute-start.10 = (bf16[256,640]{1,0:T(8,128)(2,1)S(1)}, bf16[256,640]{1,0:T(8,128)(2,1)S(1)}, u32[]{:S(2)}, u32[]{:S(2)}) collective-permute-start(bf16[256,640]{1,0:T(8,128)(2,1)S(1)} %get-tuple-element.51), channel_id=1, source_target_pairs={{0,12},{4,0},{8,4},{12,8},{1,13},{5,1},{9,5},{13,9},{2,14},{6,2},{... | collective-permute-start | bytes 983048 | tf_op jit(solution)/shard_map/ppermute | solution.py:305
  63.3 1.2 pad_maximum_fusion.2
  64.5 0.6 copy-done.14
  65.7 5.4 %collective-permute-done.10 = bf16[256,640]{1,0:T(8,128)(2,1)S(1)} collective-permute-done((bf16[256,640]{1,0:T(8,128)(2,1)S(1)}, bf16[256,640]{1,0:T(8,128)(2,1)S(1)}, u32[]{:S(2)}, u32[]{:S(2)}) %collective-permute-start.10) | collective-permute-done | bytes 327712 | tf_op jit(solution)/shard_map/ppermute | solution.py:305
  71.3 4.3 %collective-permute-start.13 = (bf16[512,640]{1,0:T(8,128)(2,1)S(1)}, bf16[512,640]{1,0:T(8,128)(2,1)S(1)}, u32[]{:S(2)}, u32[]{:S(2)}) collective-permute-start(bf16[512,640]{1,0:T(8,128)(2,1)S(1)} %pad_maximum_fusion.4.refs_6_), channel_id=1, source_target_pairs={{0,12},{4,0},{8,4},{12,8},{1,13},{5,1},{9,5},{13,9},{2,14},{6,2},{... | collective-permute-start | bytes 1966088 | tf_op jit(solution)/shard_map/ppermute | solution.py:305
  75.6 0.8 copy-done.16
  76.5 0.9 copy-done.17
  77.3 6.1 %project_rows.3 = (bf16[4,256,1280]{2,1,0:T(8,128)(2,1)}, f32[256,640]{1,0:T(8,128)}, f32[256,640]{1,0:T(8,128)}, bf16[256,640]{1,0:T(8,128)(2,1)}, f32[256,640]{1,0:T(8,128)}) custom-call(bf16[4,64,1280]{2,1,0:T(8,128)(2,1)} %copy-done.15, bf16[4,64,1280]{2,1,0:T(8,128)(2,1)} %copy-done.16, bf16[4,64,1280]{2,1,0:T(8,128)(2,1)} %collective-permute-done.8.refs_2_, ...), custom_call_target="tpu_custom_call" | custom-call | tf_op jit(solution)/shard_map/project_rows/pallas_call | solution.py:278
  83.5 1.0 fusion.19
  84.5 4.9 %collective-permute-start.16 = (bf16[128,640]{1,0:T(8,128)(2,1)S(1)}, bf16[128,640]{1,0:T(8,128)(2,1)S(1)}, u32[]{:S(2)}, u32[]{:S(2)}) collective-permute-start(bf16[128,640]{1,0:T(8,128)(2,1)S(1)} %get-tuple-element.53), channel_id=1, source_target_pairs={{0,12},{4,0},{8,4},{12,8},{1,13},{5,1},{9,5},{13,9},{2,14},{6,2},{... | collective-permute-start | bytes 491528 | tf_op jit(solution)/shard_map/ppermute | solution.py:305
  89.7 2.0 collective-permute-start.14
  91.7 20.7 %collective-permute-done.16 = bf16[128,640]{1,0:T(8,128)(2,1)S(1)} collective-permute-done((bf16[128,640]{1,0:T(8,128)(2,1)S(1)}, bf16[128,640]{1,0:T(8,128)(2,1)S(1)}, u32[]{:S(2)}, u32[]{:S(2)}) %collective-permute-start.16) | collective-permute-done | bytes 163872 | tf_op jit(solution)/shard_map/ppermute | solution.py:305
  112.5 4.7 %collective-permute-done.14 = bf16[128,640]{1,0:T(8,128)(2,1)S(1)} collective-permute-done((bf16[128,640]{1,0:T(8,128)(2,1)S(1)}, bf16[128,640]{1,0:T(8,128)(2,1)S(1)}, u32[]{:S(2)}, u32[]{:S(2)}) %collective-permute-start.14) | collective-permute-done | bytes 163872 | tf_op jit(solution)/shard_map/ppermute | solution.py:305
  117.8 0.9 fusion.17
  118.8 4.2 %rotate_heads.1 = bf16[256,640]{1,0:T(8,128)(2,1)} custom-call(f32[256,640]{1,0:T(8,128)} %get-tuple-element.48.rows_ref, f32[256,128]{1,0:T(8,128)} %slice.120.cosine_ref, f32[256,128]{1,0:T(8,128)} %slice.121.sine_ref), custom_call_target="tpu_custom_call" | custom-call | tf_op jit(solution)/shard_map/rotate_heads/pallas_call | solution.py:71
  122.9 0.5 collective-permute-start.18
  123.5 2.1 collective-permute-done.17
  125.5 3.6 %collective-permute-done.15 = bf16[256,640]{1,0:T(8,128)(2,1)S(1)} collective-permute-done((bf16[256,640]{1,0:T(8,128)(2,1)S(1)}, bf16[256,640]{1,0:T(8,128)(2,1)S(1)}, u32[]{:S(2)}, u32[]{:S(2)}) %collective-permute-start.15) | collective-permute-done | bytes 327712 | tf_op jit(solution)/shard_map/ppermute | solution.py:305
  129.2 1.1 pad_maximum_fusion.query_ref
  130.4 0.9 pad_maximum_fusion.6.key_ref
  131.3 8.6 %attention_grad.3.refs_2_ = bf16[384,512]{1,0:T(8,128)(2,1)} custom-call(f32[512,640]{1,0:T(8,128)} %pad_maximum_fusion.query_ref, bf16[512,640]{1,0:T(8,128)(2,1)} %pad_maximum_fusion.6.key_ref, bf16[512,640]{1,0:T(8,128)(2,1)} %bitcast.35, bf16[512,640]{1,0:T(8,128)(2,1)} %bitcast.33, f32[512,128]{1,0:T(8,128)} %copy-done.5, f32[512,128]{1,0:T(8,128)} %copy-done.4), custom_call_target="tpu_custom_call" | custom-call | tf_op jit(solution)/shard_map/attention_grad/pallas_call | solution.py:108
  139.9 3.6 %collective-permute-start.28 = (bf16[384,512]{1,0:T(8,128)(2,1)}, bf16[384,512]{1,0:T(8,128)(2,1)S(1)}, u32[]{:S(2)}, u32[]{:S(2)}) collective-permute-start(bf16[384,512]{1,0:T(8,128)(2,1)} %attention_grad.3.refs_2_), channel_id=1, source_target_pairs={{0,12},{4,0},{8,4},{12,8},{1,13},{5,1},{9,5},{13,9},{2,14},{6,2},{... | collective-permute-start | bytes 1179656 | tf_op jit(solution)/shard_map/ppermute | solution.py:305
  143.5 0.5 collective-permute-start.31
  144.0 9.3 %collective-permute-done.28.refs_5_ = bf16[384,512]{1,0:T(8,128)(2,1)S(1)} collective-permute-done((bf16[384,512]{1,0:T(8,128)(2,1)}, bf16[384,512]{1,0:T(8,128)(2,1)S(1)}, u32[]{:S(2)}, u32[]{:S(2)}) %collective-permute-start.28) | collective-permute-done | bytes 393248 | tf_op jit(solution)/shard_map/ppermute | solution.py:305
  153.4 4.2 %collective-permute-start.29 = (bf16[192,512]{1,0:T(8,128)(2,1)S(1)}, bf16[192,512]{1,0:T(8,128)(2,1)S(1)}, u32[]{:S(2)}, u32[]{:S(2)}) collective-permute-start(bf16[192,512]{1,0:T(8,128)(2,1)S(1)} %slice.127), channel_id=1, source_target_pairs={{0,12},{4,0},{8,4},{12,8},{1,13},{5,1},{9,5},{13,9},{2,14},{6,2},{... | collective-permute-start | bytes 589832 | tf_op jit(solution)/shard_map/ppermute | solution.py:305
  157.6 4.8 %collective-permute-done.26.refs_3_ = bf16[384,512]{1,0:T(8,128)(2,1)S(1)} collective-permute-done((bf16[384,512]{1,0:T(8,128)(2,1)}, bf16[384,512]{1,0:T(8,128)(2,1)S(1)}, u32[]{:S(2)}, u32[]{:S(2)}) %collective-permute-start.26) | collective-permute-done | bytes 393248 | tf_op jit(solution)/shard_map/ppermute | solution.py:305
  162.4 1.9 collective-permute-start.27
  164.2 6.3 %attention_grad.2.refs_2_ = bf16[256,512]{1,0:T(8,128)(2,1)} custom-call(f32[512,640]{1,0:T(8,128)} %pad_maximum_fusion.query_ref, bf16[512,640]{1,0:T(8,128)(2,1)} %pad_maximum_fusion.6.key_ref, bf16[512,640]{1,0:T(8,128)(2,1)} %bitcast.36, bf16[512,640]{1,0:T(8,128)(2,1)} %bitcast.34, f32[512,128]{1,0:T(8,128)} %copy-done.5, f32[512,128]{1,0:T(8,128)} %copy-done.4), custom_call_target="tpu_custom_call" | custom-call | tf_op jit(solution)/shard_map/attention_grad/pallas_call | solution.py:108
  170.6 2.1 collective-permute-start.24
  172.6 0.8 pad_maximum_fusion.7.refs_4_
  173.5 7.3 %fisher_rows.2 = (f32[1280,640]{1,0:T(8,128)}, bf16[1280,384]{1,0:T(8,128)(2,1)}) custom-call(bf16[4,256,1280]{2,1,0:T(8,128)(2,1)} %get-tuple-element.25.refs_0_, bf16[4,256,1280]{2,1,0:T(8,128)(2,1)} %get-tuple-element.28.refs_1_, bf16[384,512]{1,0:T(8,128)(2,1)} %attention_grad.3.refs_2_, bf16[384,512]{1,0:T(8,128)(2,1)} %copy-done.12, ...), custom_call_target="tpu_custom_call" | custom-call | tf_op jit(solution)/shard_map/fisher_rows/pallas_call | solution.py:177
  180.8 0.5 collective-permute-start.32
  181.4 3.8 %collective-permute-start.25 = (bf16[128,512]{1,0:T(8,128)(2,1)S(1)}, bf16[128,512]{1,0:T(8,128)(2,1)S(1)}, u32[]{:S(2)}, u32[]{:S(2)}) collective-permute-start(bf16[128,512]{1,0:T(8,128)(2,1)S(1)} %slice.125), channel_id=1, source_target_pairs={{0,12},{4,0},{8,4},{12,8},{1,13},{5,1},{9,5},{13,9},{2,14},{6,2},{... | collective-permute-start | bytes 393224 | tf_op jit(solution)/shard_map/ppermute | solution.py:305
  185.3 2.4 %collective-permute-done.25 = bf16[128,512]{1,0:T(8,128)(2,1)S(1)} collective-permute-done((bf16[128,512]{1,0:T(8,128)(2,1)S(1)}, bf16[128,512]{1,0:T(8,128)(2,1)S(1)}, u32[]{:S(2)}, u32[]{:S(2)}) %collective-permute-start.25) | collective-permute-done | bytes 131104 | tf_op jit(solution)/shard_map/ppermute | solution.py:305
  187.7 4.3 %collective-permute-done.23 = bf16[128,512]{1,0:T(8,128)(2,1)S(1)} collective-permute-done((bf16[128,512]{1,0:T(8,128)(2,1)S(1)}, bf16[128,512]{1,0:T(8,128)(2,1)S(1)}, u32[]{:S(2)}, u32[]{:S(2)}) %collective-permute-start.23) | collective-permute-done | bytes 131104 | tf_op jit(solution)/shard_map/ppermute | solution.py:305
  192.0 0.7 pad_maximum_fusion.10.refs_4_
  192.8 6.6 %fisher_rows.3 = (f32[1280,640]{1,0:T(8,128)}, bf16[1280,256]{1,0:T(8,128)(2,1)}) custom-call(bf16[4,256,1280]{2,1,0:T(8,128)(2,1)} %get-tuple-element.25.refs_0_, bf16[4,256,1280]{2,1,0:T(8,128)(2,1)} %get-tuple-element.28.refs_1_, bf16[256,512]{1,0:T(8,128)(2,1)} %attention_grad.2.refs_2_, ...), custom_call_target="tpu_custom_call", output_to_operand_aliasing={{0}: (6, {})} | custom-call | tf_op jit(solution)/shard_map/fisher_rows/pallas_call | solution.py:177
  199.4 1.5 collective-permute-start.30
  200.9 4.8 %collective-permute-done.32.there_ref = bf16[1280,384]{1,0:T(8,128)(2,1)S(1)} collective-permute-done((bf16[1280,384]{1,0:T(8,128)(2,1)}, bf16[1280,384]{1,0:T(8,128)(2,1)S(1)}, u32[]{:S(2)}, u32[]{:S(2)}) %collective-permute-start.32) | collective-permute-done | bytes 983072 | tf_op jit(solution)/shard_map/ppermute | solution.py:392
  205.7 0.9 copy-done.10
  206.6 5.3 %merge_rows.2.refs_4_ = f32[1280,640]{1,0:T(8,128)} custom-call(bf16[1280,384]{1,0:T(8,128)(2,1)} %get-tuple-element.39.here_ref, bf16[1280,384]{1,0:T(8,128)(2,1)} %copy-done.10, bf16[1280,640]{1,0:T(8,128)(2,1)} %bitcast.30, bf16[1280,640]{1,0:T(8,128)(2,1)} %copy-done.3), custom_call_target="tpu_custom_call" | custom-call | tf_op jit(solution)/shard_map/merge_rows/pallas_call | solution.py:211
  212.0 2.3 %collective-permute-done.30.refs_1_ = bf16[1280,256]{1,0:T(8,128)(2,1)S(1)} collective-permute-done((bf16[1280,256]{1,0:T(8,128)(2,1)}, bf16[1280,256]{1,0:T(8,128)(2,1)S(1)}, u32[]{:S(2)}, u32[]{:S(2)}) %collective-permute-start.30) | collective-permute-done | bytes 655392 | tf_op jit(solution)/shard_map/ppermute | solution.py:392
  214.3 0.8 copy-done.21
  215.2 4.7 %merge_rows.3 = f32[1280,640]{1,0:T(8,128)} custom-call(bf16[1280,256]{1,0:T(8,128)(2,1)} %get-tuple-element.37.refs_0_, bf16[1280,256]{1,0:T(8,128)(2,1)} %copy-done.21, bf16[1280,640]{1,0:T(8,128)(2,1)} %bitcast.31, bf16[1280,640]{1,0:T(8,128)(2,1)} %copy-done.3, f32[1280,640]{1,0:T(8,128)} %merge_rows.2.refs_4_), custom_call_target="tpu_custom_call", output_to_operand_aliasing={{}: (4, {})} | custom-call | tf_op jit(solution)/shard_map/merge_rows/pallas_call | solution.py:211
  (125 shorter events, 4.4 us)
Async XLA Ops:
  0.6 26.0 %copy-start = (bf16[2,256,1280]{2,1,0:T(8,128)(2,1)S(1)}, bf16[2,256,1280]{2,1,0:T(8,128)(2,1)}, u32[]{:S(2)}) copy-start(bf16[2,256,1280]{2,1,0:T(8,128)(2,1)} %param.11) | copy-start | bytes 3932164
  0.6 9.9 %copy-start.18 = (bf16[128,2560]{1,0:T(8,128)(2,1)S(1)}, bf16[128,2560]{1,0:T(8,128)(2,1)}, u32[]{:S(2)}) copy-start(bf16[128,2560]{1,0:T(8,128)(2,1)} %param.14) | copy-start | bytes 1966084
  0.7 9.9 %copy-start.19 = (bf16[1,128,2560]{2,1,0:T(8,128)(2,1)S(1)}, bf16[1,128,2560]{2,1,0:T(8,128)(2,1)}, u32[]{:S(2)}) copy-start(bf16[1,128,2560]{2,1,0:T(8,128)(2,1)} %param.15) | copy-start | bytes 1966084
  4.5 10.0 %collective-permute-start.2 = (bf16[64,1280]{1,0:T(8,128)(2,1)}, bf16[64,1280]{1,0:T(8,128)(2,1)}, u32[]{:S(2)}, u32[]{:S(2)}) collective-permute-start(bf16[64,1280]{1,0:T(8,128)(2,1)} %get-tuple-element.24), channel_id=1, source_target_pairs={{0,12},{4,0},{8,4},{12,8},{1,13},{5,1},{9,5},{13,9},{2,14},{6,2},{... | collective-permute-start | bytes 491528 | tf_op jit(solution)/shard_map/ppermute | solution.py:305
  9.6 14.2 %collective-permute-start.1 = (bf16[64,1280]{1,0:T(8,128)(2,1)}, bf16[64,1280]{1,0:T(8,128)(2,1)}, u32[]{:S(2)}, u32[]{:S(2)}) collective-permute-start(bf16[64,1280]{1,0:T(8,128)(2,1)} %get-tuple-element.23), channel_id=1, source_target_pairs={{0,8},{4,12},{8,0},{12,4},{1,9},{5,13},{9,1},{13,5},{2,10},{6,14},... | collective-permute-start | bytes 491528 | tf_op jit(solution)/shard_map/ppermute | solution.py:305
  9.6 14.2 %collective-permute-start = (bf16[64,1280]{1,0:T(8,128)(2,1)}, bf16[64,1280]{1,0:T(8,128)(2,1)}, u32[]{:S(2)}, u32[]{:S(2)}) collective-permute-start(bf16[64,1280]{1,0:T(8,128)(2,1)} %get-tuple-element.22), channel_id=1, source_target_pairs={{0,4},{4,8},{8,12},{12,0},{1,5},{5,9},{9,13},{13,1},{2,6},{6,10},{... | collective-permute-start | bytes 491528 | tf_op jit(solution)/shard_map/ppermute | solution.py:305
  10.6 2.6 %copy-start.28 = (s32[3,512]{1,0:T(4,128)S(1)}, s32[3,512]{1,0:T(4,128)}, u32[]{:S(2)}) copy-start(s32[3,512]{1,0:T(4,128)} %param.9) | copy-start | bytes 18436
  10.6 2.8 %copy-start.1 = (s32[4]{0:T(128)S(1)}, s32[4]{0:T(128)}, u32[]{:S(2)}) copy-start(s32[4]{0:T(128)} %param.10) | copy-start | bytes 52
  10.6 13.2 %copy-start.27 = (bf16[64,1280]{1,0:T(8,128)(2,1)S(1)}, bf16[64,1280]{1,0:T(8,128)(2,1)}, u32[]{:S(2)}) copy-start(bf16[64,1280]{1,0:T(8,128)(2,1)} %get-tuple-element.21) | copy-start | bytes 491524
  11.6 31.7 %collective-permute-start.21 = (bf16[2,128,640]{2,1,0:T(8,128)(2,1)}, bf16[2,128,640]{2,1,0:T(8,128)(2,1)S(1)}, u32[]{:S(2)}, u32[]{:S(2)}) collective-permute-start(bf16[2,128,640]{2,1,0:T(8,128)(2,1)} %get-tuple-element.47), channel_id=1, source_target_pairs={{0,3},{1,2},{2,1},{3,0},{4,7},{5,6},{6,5},{7,4},{8,11},{9,10},{10,... | collective-permute-start | bytes 983048 | tf_op jit(solution)/shard_map/ppermute | solution.py:395
  11.7 32.1 %collective-permute-start.20 = (bf16[2,128,640]{2,1,0:T(8,128)(2,1)}, bf16[2,128,640]{2,1,0:T(8,128)(2,1)}, u32[]{:S(2)}, u32[]{:S(2)}) collective-permute-start(bf16[2,128,640]{2,1,0:T(8,128)(2,1)} %get-tuple-element.46), channel_id=1, source_target_pairs={{0,2},{1,3},{2,0},{3,1},{4,6},{5,7},{6,4},{7,5},{8,10},{9,11},{10,... | collective-permute-start | bytes 983048 | tf_op jit(solution)/shard_map/ppermute | solution.py:395
  24.9 24.9 %copy-start.7 = (bf16[4,64,1280]{2,1,0:T(8,128)(2,1)}, bf16[4,64,1280]{2,1,0:T(8,128)(2,1)S(1)}, u32[]{:S(2)}) copy-start(bf16[4,64,1280]{2,1,0:T(8,128)(2,1)S(1)} %pad_maximum_fusion.3.refs_0_) | copy-start | bytes 1966084
  24.9 18.0 %collective-permute-start.4 = (bf16[4,64,1280]{2,1,0:T(8,128)(2,1)S(1)}, bf16[4,64,1280]{2,1,0:T(8,128)(2,1)}, u32[]{:S(2)}, u32[]{:S(2)}) collective-permute-start(bf16[4,64,1280]{2,1,0:T(8,128)(2,1)S(1)} %pad_maximum_fusion.3.refs_0_), channel_id=1, source_target_pairs={{0,2},{1,3},{2,0},{3,1},{4,6},{5,7},{6,4},{7,5},{8,10},{9,11},{10,... | collective-permute-start | bytes 1966088 | tf_op jit(solution)/shard_map/ppermute | solution.py:395
  26.9 23.2 %collective-permute-start.3 = (bf16[4,64,1280]{2,1,0:T(8,128)(2,1)S(1)}, bf16[4,64,1280]{2,1,0:T(8,128)(2,1)}, u32[]{:S(2)}, u32[]{:S(2)}) collective-permute-start(bf16[4,64,1280]{2,1,0:T(8,128)(2,1)S(1)} %pad_maximum_fusion.3.refs_0_), channel_id=1, source_target_pairs={{0,1},{1,0},{2,3},{3,2},{4,5},{5,4},{6,7},{7,6},{8,9},{9,8},{10,11... | collective-permute-start | bytes 1966088 | tf_op jit(solution)/shard_map/ppermute | solution.py:395
  26.9 23.1 %collective-permute-start.6 = (bf16[4,64,1280]{2,1,0:T(8,128)(2,1)S(1)}, bf16[4,64,1280]{2,1,0:T(8,128)(2,1)S(1)}, u32[]{:S(2)}, u32[]{:S(2)}) collective-permute-start(bf16[4,64,1280]{2,1,0:T(8,128)(2,1)S(1)} %pad_maximum_fusion.3.refs_0_), channel_id=1, source_target_pairs={{0,16},{16,0},{1,17},{17,1},{2,18},{18,2},{3,19},{19,3},{4,20},{20... | collective-permute-start | bytes 1966088 | tf_op jit(solution)/shard_map/ppermute | solution.py:392
  43.0 7.1 %collective-permute-start.5 = (bf16[4,64,1280]{2,1,0:T(8,128)(2,1)}, bf16[4,64,1280]{2,1,0:T(8,128)(2,1)}, u32[]{:S(2)}, u32[]{:S(2)}) collective-permute-start(bf16[4,64,1280]{2,1,0:T(8,128)(2,1)} %collective-permute-done.4.refs_2_), channel_id=1, source_target_pairs={{0,1},{1,0},{2,3},{3,2},{4,5},{5,4},{6,7},{7,6},{8,9},{9,8},{10,11... | collective-permute-start | bytes 1966088 | tf_op jit(solution)/shard_map/ppermute | solution.py:395
  43.3 2.1 copy-start.26
  43.3 5.2 %collective-permute-start.19 = (bf16[2,128,640]{2,1,0:T(8,128)(2,1)}, bf16[2,128,640]{2,1,0:T(8,128)(2,1)}, u32[]{:S(2)}, u32[]{:S(2)}) collective-permute-start(bf16[2,128,640]{2,1,0:T(8,128)(2,1)} %get-tuple-element.45), channel_id=1, source_target_pairs={{0,1},{1,0},{2,3},{3,2},{4,5},{5,4},{6,7},{7,6},{8,9},{9,8},{10,11... | collective-permute-start | bytes 983048 | tf_op jit(solution)/shard_map/ppermute | solution.py:395
  43.8 19.3 %collective-permute-start.8 = (bf16[4,64,1280]{2,1,0:T(8,128)(2,1)}, bf16[4,64,1280]{2,1,0:T(8,128)(2,1)}, u32[]{:S(2)}, u32[]{:S(2)}) collective-permute-start(bf16[4,64,1280]{2,1,0:T(8,128)(2,1)} %collective-permute-done.4.refs_2_), channel_id=1, source_target_pairs={{0,16},{16,0},{1,17},{17,1},{2,18},{18,2},{3,19},{19,3},{4,20},{20... | collective-permute-start | bytes 1966088 | tf_op jit(solution)/shard_map/ppermute | solution.py:392
  46.4 3.4 %copy-start.4 = (f32[512,128]{1,0:T(8,128)}, f32[512,128]{1,0:T(8,128)S(1)}, u32[]{:S(2)}) copy-start(f32[512,128]{1,0:T(8,128)S(1)} %get-tuple-element.57.sine_ref) | copy-start | bytes 786436
  46.4 3.4 %copy-start.5 = (f32[512,128]{1,0:T(8,128)}, f32[512,128]{1,0:T(8,128)S(1)}, u32[]{:S(2)}) copy-start(f32[512,128]{1,0:T(8,128)S(1)} %get-tuple-element.58.cosine_ref) | copy-start | bytes 786436
  50.0 9.0 %copy-start.15 = (bf16[4,64,1280]{2,1,0:T(8,128)(2,1)}, bf16[4,64,1280]{2,1,0:T(8,128)(2,1)S(1)}, u32[]{:S(2)}) copy-start(bf16[4,64,1280]{2,1,0:T(8,128)(2,1)S(1)} %collective-permute-done.6.refs_0_) | copy-start | bytes 1966084
  50.0 25.6 %collective-permute-start.7 = (bf16[4,64,1280]{2,1,0:T(8,128)(2,1)S(1)}, bf16[4,64,1280]{2,1,0:T(8,128)(2,1)S(1)}, u32[]{:S(2)}, u32[]{:S(2)}) collective-permute-start(bf16[4,64,1280]{2,1,0:T(8,128)(2,1)S(1)} %collective-permute-done.6.refs_0_), channel_id=1, source_target_pairs={{0,1},{1,0},{2,3},{3,2},{4,5},{5,4},{6,7},{7,6},{8,9},{9,8},{10,11... | collective-permute-start | bytes 1966088 | tf_op jit(solution)/shard_map/ppermute | solution.py:395
  60.2 11.0 %collective-permute-start.10 = (bf16[256,640]{1,0:T(8,128)(2,1)S(1)}, bf16[256,640]{1,0:T(8,128)(2,1)S(1)}, u32[]{:S(2)}, u32[]{:S(2)}) collective-permute-start(bf16[256,640]{1,0:T(8,128)(2,1)S(1)} %get-tuple-element.51), channel_id=1, source_target_pairs={{0,12},{4,0},{8,4},{12,8},{1,13},{5,1},{9,5},{13,9},{2,14},{6,2},{... | collective-permute-start | bytes 983048 | tf_op jit(solution)/shard_map/ppermute | solution.py:305
  63.1 12.6 %collective-permute-start.9 = (bf16[4,64,1280]{2,1,0:T(8,128)(2,1)}, bf16[4,64,1280]{2,1,0:T(8,128)(2,1)S(1)}, u32[]{:S(2)}, u32[]{:S(2)}) collective-permute-start(bf16[4,64,1280]{2,1,0:T(8,128)(2,1)} %collective-permute-done.8.refs_2_), channel_id=1, source_target_pairs={{0,1},{1,0},{2,3},{3,2},{4,5},{5,4},{6,7},{7,6},{8,9},{9,8},{10,11... | collective-permute-start | bytes 1966088 | tf_op jit(solution)/shard_map/ppermute | solution.py:395
  63.2 1.8 copy-start.14
  63.2 2.2 copy-start.13
  65.5 24.0 %collective-permute-start.11 = (bf16[256,640]{1,0:T(8,128)(2,1)S(1)}, bf16[256,640]{1,0:T(8,128)(2,1)S(1)}, u32[]{:S(2)}, u32[]{:S(2)}) collective-permute-start(bf16[256,640]{1,0:T(8,128)(2,1)S(1)} %get-tuple-element.50), channel_id=1, source_target_pairs={{0,4},{4,8},{8,12},{12,0},{1,5},{5,9},{9,13},{13,1},{2,6},{6,10},{... | collective-permute-start | bytes 983048 | tf_op jit(solution)/shard_map/ppermute | solution.py:305
  71.3 4.4 %copy-start.6 = (bf16[512,640]{1,0:T(8,128)(2,1)}, bf16[512,640]{1,0:T(8,128)(2,1)S(1)}, u32[]{:S(2)}) copy-start(bf16[512,640]{1,0:T(8,128)(2,1)S(1)} %pad_maximum_fusion.4.refs_6_) | copy-start | bytes 1966084
  71.3 46.3 %collective-permute-start.13 = (bf16[512,640]{1,0:T(8,128)(2,1)S(1)}, bf16[512,640]{1,0:T(8,128)(2,1)S(1)}, u32[]{:S(2)}, u32[]{:S(2)}) collective-permute-start(bf16[512,640]{1,0:T(8,128)(2,1)S(1)} %pad_maximum_fusion.4.refs_6_), channel_id=1, source_target_pairs={{0,12},{4,0},{8,4},{12,8},{1,13},{5,1},{9,5},{13,9},{2,14},{6,2},{... | collective-permute-start | bytes 1966088 | tf_op jit(solution)/shard_map/ppermute | solution.py:305
  75.6 0.8 copy-start.16
  76.5 0.9 copy-start.17
  84.5 5.1 %copy-start.25 = (f32[256,640]{1,0:T(8,128)S(1)}, f32[256,640]{1,0:T(8,128)}, u32[]{:S(2)}) copy-start(f32[256,640]{1,0:T(8,128)} %get-tuple-element.34) | copy-start | bytes 1966084
  84.5 5.2 %copy-start.24 = (f32[256,640]{1,0:T(8,128)S(1)}, f32[256,640]{1,0:T(8,128)}, u32[]{:S(2)}) copy-start(f32[256,640]{1,0:T(8,128)} %get-tuple-element.32) | copy-start | bytes 1966084
  84.5 27.9 %collective-permute-start.16 = (bf16[128,640]{1,0:T(8,128)(2,1)S(1)}, bf16[128,640]{1,0:T(8,128)(2,1)S(1)}, u32[]{:S(2)}, u32[]{:S(2)}) collective-permute-start(bf16[128,640]{1,0:T(8,128)(2,1)S(1)} %get-tuple-element.53), channel_id=1, source_target_pairs={{0,12},{4,0},{8,4},{12,8},{1,13},{5,1},{9,5},{13,9},{2,14},{6,2},{... | collective-permute-start | bytes 491528 | tf_op jit(solution)/shard_map/ppermute | solution.py:305
  89.6 28.0 %collective-permute-start.12 = (bf16[512,640]{1,0:T(8,128)(2,1)S(1)}, bf16[512,640]{1,0:T(8,128)(2,1)S(1)}, u32[]{:S(2)}, u32[]{:S(2)}) collective-permute-start(bf16[512,640]{1,0:T(8,128)(2,1)S(1)} %pad_maximum_fusion.5), channel_id=1, source_target_pairs={{0,4},{4,8},{8,12},{12,0},{1,5},{5,9},{9,13},{13,1},{2,6},{6,10},{... | collective-permute-start | bytes 1966088 | tf_op jit(solution)/shard_map/ppermute | solution.py:305
  89.7 27.9 %copy-start.9 = (f32[512,640]{1,0:T(8,128)S(1)}, f32[512,640]{1,0:T(8,128)}, u32[]{:S(2)}) copy-start(f32[512,640]{1,0:T(8,128)} %get-tuple-element.29) | copy-start | bytes 3932164
  89.7 27.5 %collective-permute-start.14 = (bf16[128,640]{1,0:T(8,128)(2,1)S(1)}, bf16[128,640]{1,0:T(8,128)(2,1)S(1)}, u32[]{:S(2)}, u32[]{:S(2)}) collective-permute-start(bf16[128,640]{1,0:T(8,128)(2,1)S(1)} %get-tuple-element.52), channel_id=1, source_target_pairs={{0,4},{4,8},{8,12},{12,0},{1,5},{5,9},{9,13},{13,1},{2,6},{6,10},{... | collective-permute-start | bytes 491528 | tf_op jit(solution)/shard_map/ppermute | solution.py:305
  112.5 13.0 %collective-permute-start.17 = (bf16[256,640]{1,0:T(8,128)(2,1)S(1)}, bf16[256,640]{1,0:T(8,128)(2,1)S(1)}, u32[]{:S(2)}, u32[]{:S(2)}) collective-permute-start(bf16[256,640]{1,0:T(8,128)(2,1)S(1)} %pad_maximum_fusion.9), channel_id=1, source_target_pairs={{0,12},{4,0},{8,4},{12,8},{1,13},{5,1},{9,5},{13,9},{2,14},{6,2},{... | collective-permute-start | bytes 983048 | tf_op jit(solution)/shard_map/ppermute | solution.py:305
  117.3 11.8 %collective-permute-start.15 = (bf16[256,640]{1,0:T(8,128)(2,1)S(1)}, bf16[256,640]{1,0:T(8,128)(2,1)S(1)}, u32[]{:S(2)}, u32[]{:S(2)}) collective-permute-start(bf16[256,640]{1,0:T(8,128)(2,1)S(1)} %pad_maximum_fusion.8), channel_id=1, source_target_pairs={{0,4},{4,8},{8,12},{12,0},{1,5},{5,9},{9,13},{13,1},{2,6},{6,10},{... | collective-permute-start | bytes 983048 | tf_op jit(solution)/shard_map/ppermute | solution.py:305
  117.8 11.3 %copy-start.20 = (f32[256,640]{1,0:T(8,128)S(1)}, f32[256,640]{1,0:T(8,128)}, u32[]{:S(2)}) copy-start(f32[256,640]{1,0:T(8,128)} %get-tuple-element.31) | copy-start | bytes 1966084
  122.9 7.4 %collective-permute-start.18 = (bf16[256,640]{1,0:T(8,128)(2,1)}, bf16[256,640]{1,0:T(8,128)(2,1)S(1)}, u32[]{:S(2)}, u32[]{:S(2)}) collective-permute-start(bf16[256,640]{1,0:T(8,128)(2,1)} %rotate_heads.1), channel_id=1, source_target_pairs={{0,16},{16,0},{1,17},{17,1},{2,18},{18,2},{3,19},{19,3},{4,20},{20... | collective-permute-start | bytes 983048 | tf_op jit(solution)/shard_map/ppermute | solution.py:392
  129.2 1.2 copy-start.8
  131.3 12.2 %copy-start.2 = (bf16[1,1280,640]{2,1,0:T(8,128)(2,1)S(1)}, bf16[1,1280,640]{2,1,0:T(8,128)(2,1)}, u32[]{:S(2)}) copy-start(bf16[1,1280,640]{2,1,0:T(8,128)(2,1)} %param.12) | copy-start | bytes 4915204
  139.9 13.5 %collective-permute-start.28 = (bf16[384,512]{1,0:T(8,128)(2,1)}, bf16[384,512]{1,0:T(8,128)(2,1)S(1)}, u32[]{:S(2)}, u32[]{:S(2)}) collective-permute-start(bf16[384,512]{1,0:T(8,128)(2,1)} %attention_grad.3.refs_2_), channel_id=1, source_target_pairs={{0,12},{4,0},{8,4},{12,8},{1,13},{5,1},{9,5},{13,9},{2,14},{6,2},{... | collective-permute-start | bytes 1179656 | tf_op jit(solution)/shard_map/ppermute | solution.py:305
  143.5 18.9 %collective-permute-start.26 = (bf16[384,512]{1,0:T(8,128)(2,1)}, bf16[384,512]{1,0:T(8,128)(2,1)S(1)}, u32[]{:S(2)}, u32[]{:S(2)}) collective-permute-start(bf16[384,512]{1,0:T(8,128)(2,1)} %attention_grad.3.refs_2_), channel_id=1, source_target_pairs={{0,4},{4,8},{8,12},{12,0},{1,5},{5,9},{9,13},{13,1},{2,6},{6,10},{... | collective-permute-start | bytes 1179656 | tf_op jit(solution)/shard_map/ppermute | solution.py:305
  143.5 57.4 %collective-permute-start.31 = (bf16[1280,640]{1,0:T(8,128)(2,1)S(1)}, bf16[1280,640]{1,0:T(8,128)(2,1)S(1)}, u32[]{:S(2)}, u32[]{:S(2)}) collective-permute-start(bf16[1280,640]{1,0:T(8,128)(2,1)S(1)} %bitcast.32), channel_id=1, source_target_pairs={{0,16},{16,0},{1,17},{17,1},{2,18},{18,2},{3,19},{19,3},{4,20},{20... | collective-permute-start | bytes 4915208 | tf_op jit(solution)/shard_map/ppermute | solution.py:392
  153.4 17.2 %copy-start.11 = (bf16[384,512]{1,0:T(8,128)(2,1)}, bf16[384,512]{1,0:T(8,128)(2,1)S(1)}, u32[]{:S(2)}) copy-start(bf16[384,512]{1,0:T(8,128)(2,1)S(1)} %collective-permute-done.28.refs_5_) | copy-start | bytes 1179652
  153.4 19.3 %collective-permute-start.29 = (bf16[192,512]{1,0:T(8,128)(2,1)S(1)}, bf16[192,512]{1,0:T(8,128)(2,1)S(1)}, u32[]{:S(2)}, u32[]{:S(2)}) collective-permute-start(bf16[192,512]{1,0:T(8,128)(2,1)S(1)} %slice.127), channel_id=1, source_target_pairs={{0,12},{4,0},{8,4},{12,8},{1,13},{5,1},{9,5},{13,9},{2,14},{6,2},{... | collective-permute-start | bytes 589832 | tf_op jit(solution)/shard_map/ppermute | solution.py:305
  162.4 8.2 %copy-start.12 = (bf16[384,512]{1,0:T(8,128)(2,1)}, bf16[384,512]{1,0:T(8,128)(2,1)S(1)}, u32[]{:S(2)}) copy-start(bf16[384,512]{1,0:T(8,128)(2,1)S(1)} %collective-permute-done.26.refs_3_) | copy-start | bytes 1179652
  162.4 10.3 %collective-permute-start.27 = (bf16[192,512]{1,0:T(8,128)(2,1)S(1)}, bf16[192,512]{1,0:T(8,128)(2,1)S(1)}, u32[]{:S(2)}, u32[]{:S(2)}) collective-permute-start(bf16[192,512]{1,0:T(8,128)(2,1)S(1)} %slice.126), channel_id=1, source_target_pairs={{0,4},{4,8},{8,12},{12,0},{1,5},{5,9},{9,13},{13,1},{2,6},{6,10},{... | collective-permute-start | bytes 589832 | tf_op jit(solution)/shard_map/ppermute | solution.py:305
  170.6 10.8 %collective-permute-start.24 = (bf16[256,512]{1,0:T(8,128)(2,1)}, bf16[256,512]{1,0:T(8,128)(2,1)S(1)}, u32[]{:S(2)}, u32[]{:S(2)}) collective-permute-start(bf16[256,512]{1,0:T(8,128)(2,1)} %attention_grad.2.refs_2_), channel_id=1, source_target_pairs={{0,12},{4,0},{8,4},{12,8},{1,13},{5,1},{9,5},{13,9},{2,14},{6,2},{... | collective-permute-start | bytes 786440 | tf_op jit(solution)/shard_map/ppermute | solution.py:305
  172.6 12.6 %collective-permute-start.22 = (bf16[256,512]{1,0:T(8,128)(2,1)}, bf16[256,512]{1,0:T(8,128)(2,1)S(1)}, u32[]{:S(2)}, u32[]{:S(2)}) collective-permute-start(bf16[256,512]{1,0:T(8,128)(2,1)} %attention_grad.2.refs_2_), channel_id=1, source_target_pairs={{0,4},{4,8},{8,12},{12,0},{1,5},{5,9},{9,13},{13,1},{2,6},{6,10},{... | collective-permute-start | bytes 786440 | tf_op jit(solution)/shard_map/ppermute | solution.py:305
  180.8 24.9 %collective-permute-start.32 = (bf16[1280,384]{1,0:T(8,128)(2,1)}, bf16[1280,384]{1,0:T(8,128)(2,1)S(1)}, u32[]{:S(2)}, u32[]{:S(2)}) collective-permute-start(bf16[1280,384]{1,0:T(8,128)(2,1)} %get-tuple-element.39.here_ref), channel_id=1, source_target_pairs={{0,16},{16,0},{1,17},{17,1},{2,18},{18,2},{3,19},{19,3},{4,20},{20... | collective-permute-start | bytes 2949128 | tf_op jit(solution)/shard_map/ppermute | solution.py:392
  181.3 11.4 %copy-start.22 = (bf16[256,512]{1,0:T(8,128)(2,1)}, bf16[256,512]{1,0:T(8,128)(2,1)S(1)}, u32[]{:S(2)}) copy-start(bf16[256,512]{1,0:T(8,128)(2,1)S(1)} %collective-permute-done.24.refs_5_) | copy-start | bytes 786436
  181.4 6.4 %collective-permute-start.25 = (bf16[128,512]{1,0:T(8,128)(2,1)S(1)}, bf16[128,512]{1,0:T(8,128)(2,1)S(1)}, u32[]{:S(2)}, u32[]{:S(2)}) collective-permute-start(bf16[128,512]{1,0:T(8,128)(2,1)S(1)} %slice.125), channel_id=1, source_target_pairs={{0,12},{4,0},{8,4},{12,8},{1,13},{5,1},{9,5},{13,9},{2,14},{6,2},{... | collective-permute-start | bytes 393224 | tf_op jit(solution)/shard_map/ppermute | solution.py:305
  185.2 7.6 %copy-start.23 = (bf16[256,512]{1,0:T(8,128)(2,1)}, bf16[256,512]{1,0:T(8,128)(2,1)S(1)}, u32[]{:S(2)}) copy-start(bf16[256,512]{1,0:T(8,128)(2,1)S(1)} %collective-permute-done.22.refs_3_) | copy-start | bytes 786436
  185.2 6.8 %collective-permute-start.23 = (bf16[128,512]{1,0:T(8,128)(2,1)S(1)}, bf16[128,512]{1,0:T(8,128)(2,1)S(1)}, u32[]{:S(2)}, u32[]{:S(2)}) collective-permute-start(bf16[128,512]{1,0:T(8,128)(2,1)S(1)} %slice.124), channel_id=1, source_target_pairs={{0,4},{4,8},{8,12},{12,0},{1,5},{5,9},{9,13},{13,1},{2,6},{6,10},{... | collective-permute-start | bytes 393224 | tf_op jit(solution)/shard_map/ppermute | solution.py:305
  199.4 15.0 %collective-permute-start.30 = (bf16[1280,256]{1,0:T(8,128)(2,1)}, bf16[1280,256]{1,0:T(8,128)(2,1)S(1)}, u32[]{:S(2)}, u32[]{:S(2)}) collective-permute-start(bf16[1280,256]{1,0:T(8,128)(2,1)} %get-tuple-element.37.refs_0_), channel_id=1, source_target_pairs={{0,16},{16,0},{1,17},{17,1},{2,18},{18,2},{3,19},{19,3},{4,20},{20... | collective-permute-start | bytes 1966088 | tf_op jit(solution)/shard_map/ppermute | solution.py:392
  200.9 4.8 %copy-start.3 = (bf16[1280,640]{1,0:T(8,128)(2,1)}, bf16[1280,640]{1,0:T(8,128)(2,1)S(1)}, u32[]{:S(2)}) copy-start(bf16[1280,640]{1,0:T(8,128)(2,1)S(1)} %collective-permute-done.31.other_ref.refs_3_) | copy-start | bytes 4915204
  205.7 1.0 copy-start.10
  214.3 0.8 copy-start.21

commit v2 on v1

v2 whole, which is shorter than its diff:
```python
import functools
import math

import jax
import jax.numpy as jnp
from jax import lax
from jax.experimental import pallas as pl
from jax.experimental.pallas import tpu as pltpu
from jax.sharding import PartitionSpec as P

HEAD_SIZE = 128
damping = 0.01
VMEM_BYTES = 24 * 1024 * 1024
FISHER_BYTES = 32 * 1024 * 1024


def time_features(timestep, feature_count):
    halfway = feature_count // 2
    ladder = jnp.arange(halfway).astype(jnp.float32)
    frequency = jnp.exp(-math.log(10000.0) * 2.0 * ladder / feature_count)
    angles = timestep.astype(jnp.float32)[:, None] * frequency[None, :]
    return jnp.concatenate([jnp.cos(angles), jnp.sin(angles)], axis=1).astype(jnp.bfloat16)


def rope_tables(lattice, head_width):
    halfway = head_width // 2
    side_pairs = head_width // 6
    frame_pairs = halfway - 2 * side_pairs
    column = jnp.arange(head_width)
    pair_index = column % halfway
    which_axis = jnp.where(
        pair_index < frame_pairs, 0, jnp.where(pair_index < frame_pairs + side_pairs, 1, 2)
    )
    anchor = jnp.where(
        which_axis == 0, 0, jnp.where(which_axis == 1, frame_pairs, frame_pairs + side_pairs)
    )
    pair_span = jnp.where(which_axis == 0, frame_pairs, side_pairs)
    frequency = jnp.exp(
        -math.log(10000.0)
        * (pair_index - anchor).astype(jnp.float32)
        / pair_span.astype(jnp.float32)
    )
    position = lattice.astype(jnp.float32)
    angles = jnp.zeros((lattice.shape[1], head_width), jnp.float32)
    for axis_number in range(3):
        chosen = jnp.where(which_axis == axis_number, frequency, 0.0)
        angles = angles + position[axis_number][:, None] * chosen[None, :]
    sign_flip = jnp.where(column < halfway, -1.0, 1.0).astype(jnp.float32)
    return (jnp.cos(angles), jnp.sin(angles) * sign_flip[None, :])


def partner(rows):
    return pltpu.roll(rows, rows.shape[1] // 2, 1)


def head_rotation(rows, cosine, sine):
    inverse = lax.rsqrt(jnp.mean(rows * rows, axis=1, keepdims=True) + 1e-06)
    normed = rows * inverse
    return normed, inverse, normed * cosine + partner(normed) * sine


def rotate_kernel(rows_ref, cosine_ref, sine_ref, out_ref):
    cosine, sine = cosine_ref[...], sine_ref[...]
    for start in range(0, rows_ref.shape[1], HEAD_SIZE):
        span = slice(start, start + HEAD_SIZE)
        rotated = head_rotation(rows_ref[:, span], cosine, sine)[2]
        out_ref[:, span] = rotated.astype(out_ref.dtype)


def rotate_heads(rows, cosine, sine):
    whole = pl.BlockSpec(memory_space=pltpu.VMEM)
    return pl.pallas_call(
        rotate_kernel,
        in_specs=[whole] * 3,
        out_specs=whole,
        out_shape=jax.ShapeDtypeStruct(rows.shape, jnp.bfloat16),
        compiler_params=pltpu.CompilerParams(vmem_limit_bytes=VMEM_BYTES),
        name="rotate_heads",
    )(rows, cosine, sine)


def drop(kernel, place, count=1):
    def run(*refs):
        kernel(*refs[:place], *refs[place + count :])

    return run


def turned_partner(turned):
    half = turned.shape[0] // 2
    return jnp.concatenate([turned[half:], turned[:half]], axis=0)


def attention_kernel(
    first, block, query_ref, key_ref, value_ref, cot_ref, cosine_ref, sine_ref, out_ref
):
    length, heads = query_ref.shape[0], out_ref.shape[0] // HEAD_SIZE
    scale = HEAD_SIZE ** (-0.5)
    for head in range(heads):
        span = slice((first + head) * HEAD_SIZE, (first + head + 1) * HEAD_SIZE)
        key, value = key_ref[:, span], value_ref[:, span]
        key_turned = key.T
        for start in range(0, length, block):
            rows = slice(start, start + block)
            cosine, sine = cosine_ref[:, rows], sine_ref[:, rows]
            query = query_ref[rows, span].T
            inverse = lax.rsqrt(jnp.mean(query * query, axis=0, keepdims=True) + 1e-06)
            normed = query * inverse
            rotated = normed * cosine + turned_partner(normed) * sine
            rotated = (rotated * (scale * math.log2(math.e))).astype(jnp.bfloat16)
            raised = jnp.exp2(jnp.dot(key, rotated, preferred_element_type=jnp.float32))
            grad = jnp.dot(value, cot_ref[rows, span].T, preferred_element_type=jnp.float32)
            product = raised * grad
            share = 1.0 / jnp.sum(raised, axis=0, keepdims=True)
            inner = jnp.sum(product, axis=0, keepdims=True) * share
            grad = (product - raised * inner).astype(jnp.bfloat16)
            grad = jnp.dot(key_turned, grad, preferred_element_type=jnp.float32) * (share * scale)
            grad = grad * cosine + turned_partner(grad * sine)
            shared = jnp.mean(grad * normed, axis=0, keepdims=True)
            grad = inverse * (grad - normed * shared)
            out_ref[head * HEAD_SIZE : (head + 1) * HEAD_SIZE, rows] = grad.astype(out_ref.dtype)


def attention_grad(query_pre, key, value, cot, cosine, sine, first, count, waits, block=512):
    length = query_pre.shape[0]
    whole = pl.BlockSpec(memory_space=pltpu.VMEM)
    return pl.pallas_call(
        drop(functools.partial(attention_kernel, first, block), 6, len(waits)),
        in_specs=[whole] * 6 + [pl.BlockSpec(memory_space=pl.ANY)] * len(waits),
        out_specs=whole,
        out_shape=jax.ShapeDtypeStruct((count * HEAD_SIZE, length), jnp.bfloat16),
        compiler_params=pltpu.CompilerParams(vmem_limit_bytes=VMEM_BYTES),
        name="attention_grad",
    )(query_pre, key, value, cot, cosine, sine, *waits)


def row_tile(rows):
    return 256 if rows % 256 == 0 else rows


def fisher_kernel(groups, first, *refs):
    rows, grads = refs[:groups], refs[groups:-4]
    own_ref, low_ref, held, done = refs[-4:]
    width, columns = low_ref.shape
    tile = row_tile(width)

    def squared(clip, grad, span):
        block = jnp.concatenate([ref[clip, :, span] for ref in rows], axis=0)
        grad = jnp.dot(grad, block, preferred_element_type=jnp.float32)
        return grad * grad

    copies = []
    for start in range(0, width, tile):
        span = slice(start, start + tile)
        total = jnp.zeros((columns, tile), jnp.float32)
        clip = 0
        for ref in grads:
            if len(ref.shape) == 2:
                total = total + squared(clip, ref[...], span)
                clip += 1
            else:
                total = lax.fori_loop(
                    0, ref.shape[0], lambda i, t, r=ref, s=span: t + squared(i, r[i], s), total
                )
                clip += ref.shape[0]
        fisher = total.T
        low_ref[span] = fisher.astype(low_ref.dtype)
        held[span] = fisher
        copies.append(
            pltpu.make_async_copy(
                held.at[span], own_ref.at[span, first : first + columns], done.at[len(copies)]
            )
        )
        copies[-1].start()
    for copy in copies:
        copy.wait()


def in_place(kernel, inputs, specs, previous, waits=()):
    extra = ([] if previous is None else [previous]) + list(waits)
    place = len(inputs)
    return (
        drop(kernel, place, len(extra)),
        list(inputs) + extra,
        list(specs) + [pl.BlockSpec(memory_space=pl.ANY)] * len(extra),
        {} if previous is None else {place: 0},
    )


def fisher_rows(rows, grads, first, total_columns, previous, waits):
    width = rows[0].shape[2]
    columns = grads[0].shape[-2]
    whole = pl.BlockSpec(memory_space=pltpu.VMEM)
    inputs = [*rows, *grads]
    kernel, inputs, specs, aliases = in_place(
        functools.partial(fisher_kernel, len(rows), first),
        inputs,
        [whole] * len(inputs),
        previous,
        waits,
    )
    return pl.pallas_call(
        kernel,
        in_specs=specs,
        out_specs=[pl.BlockSpec(memory_space=pl.ANY), whole],
        out_shape=[
            jax.ShapeDtypeStruct((width, total_columns), jnp.float32),
            jax.ShapeDtypeStruct((width, columns), jnp.bfloat16),
        ],
        scratch_shapes=[
            pltpu.VMEM((width, columns), jnp.float32),
            pltpu.SemaphoreType.DMA((width // row_tile(width),)),
        ],
        input_output_aliases=aliases,
        compiler_params=pltpu.CompilerParams(vmem_limit_bytes=FISHER_BYTES),
        name="fisher_rows",
    )(*inputs)


def merge_kernel(here_ref, there_ref, own_ref, other_ref, out_ref):
    zero = lax.axis_index("member") == 0
    here, there = to_f32(here_ref[...]) + damping, to_f32(there_ref[...]) + damping
    one, two = here * to_f32(own_ref[...]), there * to_f32(other_ref[...])
    upper = jnp.where(zero, one, two) + jnp.where(zero, two, one)
    out_ref[...] = upper / (here + there)


def merge_rows(here, there, own_weight, other_weight, first, offset, previous):
    width, columns = here.shape
    tile = width // 2
    plain = pl.BlockSpec((tile, columns), lambda i: (i, 0))
    part = pl.BlockSpec((pl.Element(tile), pl.Element(columns)), lambda i: (i * tile, first))
    other = pl.BlockSpec((pl.Element(tile), pl.Element(columns)), lambda i: (i * tile, offset))
    kernel, inputs, specs, aliases = in_place(
        merge_kernel, [here, there, own_weight, other_weight], [plain, plain, part, other], previous
    )
    return pl.pallas_call(
        kernel,
        grid=(width // tile,),
        in_specs=specs,
        out_specs=part,
        out_shape=jax.ShapeDtypeStruct(own_weight.shape, jnp.float32),
        input_output_aliases=aliases,
        compiler_params=pltpu.CompilerParams(vmem_limit_bytes=VMEM_BYTES),
        name="merge_rows",
    )(*inputs)


def spread_kernel(place_ref, rows_ref, *outs):
    rows = to_f32(rows_ref[...])
    average = jnp.mean(rows, axis=1, keepdims=True)
    centred = rows - average
    inverse = lax.rsqrt(jnp.mean(centred * centred, axis=1, keepdims=True) + 1e-06)
    size, width = len(outs), outs[0].shape[1]
    for away, out_ref in enumerate(outs):
        start = pl.multiple_of(lax.rem(place_ref[1] + away, size) * width, 128)
        part = to_f32(rows_ref[:, pl.ds(start, width)])
        out_ref[...] = ((part - average) * inverse).astype(out_ref.dtype)


def spread_rows(tokens, member, place, share, size):
    width = tokens.shape[1] // size
    return pl.pallas_call(
        spread_kernel,
        grid_spec=pltpu.PrefetchScalarGridSpec(
            num_scalar_prefetch=1,
            grid=(1,),
            in_specs=[pl.BlockSpec((share, tokens.shape[1]), lambda i, where: (where[0], 0))],
            out_specs=[pl.BlockSpec((share, width), lambda i, where: (0, 0))] * size,
        ),
        out_shape=[jax.ShapeDtypeStruct((share, width), jnp.bfloat16)] * size,
        compiler_params=pltpu.CompilerParams(vmem_limit_bytes=VMEM_BYTES),
        name="spread_rows",
    )(jnp.stack([member, place]).astype(jnp.int32), tokens)


def modulate(rows, modulation):
    return (rows * (1.0 + modulation[1:2]) + modulation[0:1]).astype(jnp.bfloat16)


def project_kernel(pieces, jobs, weights, waits, *refs):
    piece_refs, modulation_ref = refs[:pieces], refs[pieces]
    weight_refs = refs[pieces + 1 : pieces + 1 + weights]
    rows_ref, *outs = refs[pieces + 1 + weights + waits :]
    size = rows_ref.shape[0]
    share = piece_refs[0].shape[1]
    order = sorted(range(size), key=lambda away: -min(away, size - away))
    for away in order:
        modulation = modulation_ref[away]
        for i, ref in enumerate(piece_refs):
            rows_ref[away, i * share : (i + 1) * share] = modulate(to_f32(ref[away]), modulation)
        products = [
            jnp.dot(
                rows_ref[away, : count * share],
                weight_refs[index][...],
                preferred_element_type=jnp.float32,
            )
            for index, count in jobs
        ]
        products = products[0] if len(jobs) == 1 else jnp.concatenate(products, axis=0)
        if 2 * away == size:
            middle = products.shape[0] // 2
            outs[size][...] = products[middle:].astype(outs[size].dtype)
            products = products[:middle]
        outs[away][...] = products.astype(outs[away].dtype)


def project_rows(pieces, modulation, weights, jobs, waits):
    size, share, width = pieces[0].shape
    length = sum(count for _, count in jobs) * share
    columns = weights[0].shape[1]
    terms = [jax.ShapeDtypeStruct((length, columns), jnp.float32)] * size
    halves = [jax.ShapeDtypeStruct((length // 2, columns), jnp.bfloat16)] * 2
    terms = terms[: size // 2] + halves[:1] + terms[size // 2 + 1 :] + halves[1:]
    whole = pl.BlockSpec(memory_space=pltpu.VMEM)
    return pl.pallas_call(
        functools.partial(project_kernel, len(pieces), jobs, len(weights), len(waits)),
        in_specs=[whole] * (len(pieces) + 1 + len(weights))
        + [pl.BlockSpec(memory_space=pl.ANY)] * len(waits),
        out_specs=[whole] * (2 + size),
        out_shape=[jax.ShapeDtypeStruct((size, len(pieces) * share, width), jnp.bfloat16)] + terms,
        compiler_params=pltpu.CompilerParams(vmem_limit_bytes=VMEM_BYTES),
        name="project_rows",
    )(*pieces, modulation, *weights, *waits)


def to_f32(block):
    return block.astype(jnp.float32)


def behind(*arrays):
    return lax.optimization_barrier(arrays)


class Ring:
    def __init__(self, size):
        self.size = size
        self.place = lax.axis_index("seq")
        self.short = size <= 8 and size % 2 == 0

    def by_distance(self, blocks):
        return jnp.take(blocks, (self.place - jnp.arange(self.size)) % self.size, axis=0)

    def step(self, block, away):
        pairs = [(i, (i + away) % self.size) for i in range(self.size)]
        return lax.ppermute(block, "seq", pairs)

    def exchange(self, tokens, member, share):
        size = self.size
        width = tokens.shape[1] // size
        if self.short and width % 128 == 0:
            parts = spread_rows(tokens, member, self.place, share, size)
            return jnp.stack(
                list(parts[:1]) + [self.step(part, away) for away, part in enumerate(parts) if away]
            )
        mine = to_f32(lax.dynamic_slice_in_dim(tokens, member * share, share, 0))
        centred = mine - jnp.mean(mine, axis=1, keepdims=True)
        variance = jnp.mean(centred * centred, axis=1, keepdims=True)
        normed = (centred * lax.rsqrt(variance + 1e-06)).astype(jnp.bfloat16)
        parts = normed.reshape(share, size, width)
        return self.by_distance(
            lax.all_to_all(parts, "seq", split_axis=1, concat_axis=0, tiled=False)
        )

    def project(self, pieces, modulation, weights, jobs, waits):
        size, half = self.size, self.size // 2
        if not self.short:
            share = pieces[0].shape[1]
            rows = jax.vmap(modulate)(to_f32(jnp.concatenate(pieces, axis=1)), modulation)
            terms = [
                jnp.einsum(
                    "crw,wn->crn",
                    rows[:, : count * share],
                    weights[index],
                    preferred_element_type=jnp.float32,
                ).astype(jnp.bfloat16)
                for index, count in jobs
            ]
            return rows, jnp.concatenate(terms, axis=1), ()
        rows, *terms = project_rows(pieces, modulation, weights, jobs, waits)
        first = self.step(terms[half], 1), self.step(terms[size], -1)
        return rows, terms, first

    def sum(self, terms, first):
        size, half = self.size, self.size // 2
        if not self.short:
            return to_f32(lax.psum_scatter(self.by_distance(terms), "seq", tiled=False)), ()
        right, left = first
        middle = right.shape[0]
        for away in range(half - 1, 0, -1):
            term_right, term_left = terms[size - away], terms[away]
            if away == half - 1:
                term_right = jnp.concatenate(
                    [term_right[:middle] + to_f32(right), term_right[middle:]], axis=0
                )
                term_left = jnp.concatenate(
                    [term_left[:middle], term_left[middle:] + to_f32(left)], axis=0
                )
            else:
                term_right, term_left = term_right + to_f32(right), term_left + to_f32(left)
            right = self.step(term_right.astype(jnp.bfloat16), 1)
            left = self.step(term_left.astype(jnp.bfloat16), -1)
        if half == 1:
            return terms[0] + to_f32(jnp.concatenate([right, left], axis=0)), (right, left)
        return terms[0] + to_f32(right) + to_f32(left), (right, left)

    def gather(self, block):
        size, half = self.size, self.size // 2
        if not self.short:
            blocks = self.by_distance(lax.all_gather(block, "seq"))
            return [blocks], [blocks]
        blocks = [None] * size
        blocks[0] = block
        right, left = block, block
        for away in range(1, half):
            right, left = self.step(right, 1), self.step(left, -1)
            blocks[away], blocks[size - away] = right, left
        middle = block.shape[0] // 2
        blocks[half] = jnp.concatenate(
            [self.step(right[:middle], 1), self.step(left[middle:], -1)], axis=0
        )
        return blocks, [right, left]


def on_device(
    axes, tokens, lattice, timestep, time_weight, query_weight, key_weight, values, cotangent
):
    members, clips, heads = axes
    member = lax.axis_index("member")
    clip = lax.axis_index("seq")
    head = lax.axis_index("head")
    own_query = query_weight[0]
    width, columns = own_query.shape
    share = tokens.shape[0] // members

    ring = Ring(clips)

    def x_swap(block):
        return lax.ppermute(block, "member", [(i, i ^ 1) for i in range(members)])

    def h_swap(block, bits):
        return lax.ppermute(block, "head", [(i, i ^ bits) for i in range(heads)])

    own = ring.exchange(tokens, member, share)

    ordered = timestep[(clip - jnp.arange(clips)) % clips]
    features = time_features(ordered, time_weight.shape[1])
    modulation = jnp.einsum(
        "cf,jfd->cjd", features, time_weight, preferred_element_type=jnp.float32
    )

    def both(block):
        return [block, h_swap(block, 1)]

    weights = [own_query, key_weight]
    jobs = [(0, 2), (1, 2)]
    near_y, near_x = h_swap(own, 2), x_swap(own)
    rows_own, terms_own, first_own = ring.project(both(own), modulation, weights, jobs, [])
    near_y, _ = behind(near_y, rows_own)
    far = x_swap(near_y)
    sums_own, last_own = ring.sum(terms_own, first_own)
    near_y = behind(near_y, *first_own)[0]
    rows_y, terms_y, first_y = ring.project(both(near_y), modulation, weights, jobs, [rows_own])
    sums_y, _ = ring.sum(terms_y, first_y)
    rows_x, terms_x, first_x = ring.project(
        both(near_x) + both(far), modulation, [own_query], [(0, 4)], [rows_y, *first_y, *last_own]
    )
    lines = 2 * share
    key_here = jnp.concatenate([sums_own[lines:], sums_y[lines:]], axis=0)

    grid = lattice.reshape(3, 2, 2, members, share).transpose(0, 3, 1, 2, 4)
    for axis, bit in ((1, member), (2, head // 2), (3, head % 2)):
        grid = jnp.where(bit == 1, jnp.flip(grid, axis), grid)
    cosine, sine = rope_tables(grid.reshape(3, -1), HEAD_SIZE)

    pair = jnp.stack([values, cotangent[0]])
    blocks = []
    for bits in range(heads):
        block = lax.dynamic_slice_in_dim(pair, (head ^ bits) * columns, columns, 2)
        blocks.append(h_swap(block, bits) if bits else block)
    halves = jnp.stack(blocks, axis=1).reshape(2, heads, members, share, columns)
    halves = jnp.concatenate(
        [lax.dynamic_slice_in_dim(halves, member ^ i, 1, 2)[:, :, 0] for i in range(members)], axis=1
    ).reshape(2, members * heads * share, columns)
    value_rows, cot_rows = halves[0], halves[1]

    head_count = columns // HEAD_SIZE
    last_heads = max(1, head_count // 5)
    bounds = [0, (head_count - last_heads) // 2, head_count - last_heads, head_count]
    cut = bounds[1] * HEAD_SIZE
    early, _ = behind(own_query[:, :cut], far)
    early = x_swap(early)

    rows_here = key_here.shape[0]
    key_here = rotate_heads(key_here, cosine[:rows_here], sine[:rows_here])
    key_here, early = behind(key_here, early, *first_x)[:2]
    key_there = x_swap(key_here)
    key_rows = jnp.concatenate([key_here, key_there], axis=0)
    late, _ = behind(own_query[:, cut:], key_there)
    late = x_swap(late)

    query_x, _ = ring.sum(terms_x, first_x)
    query_pre = jnp.concatenate([sums_own[:lines], sums_y[:lines], query_x], axis=0)
    operands = query_pre, key_rows, value_rows, cot_rows, cosine.T, sine.T
    spans = [(first, last) for first, last in zip(bounds[:-1], bounds[1:]) if first < last]
    grads, gathered, waits = [], [], []
    for i, (first, last) in enumerate(spans):
        grads.append(attention_grad(*operands, first, last - first, waits + [late] * (i == 1)))
        blocks, waits = ring.gather(grads[-1])
        gathered.append(blocks)
    fisher, merged = None, None
    for i, (first, _) in enumerate(spans):
        first = first * HEAD_SIZE
        rows = [rows_own, rows_y, rows_x]
        fisher, low = fisher_rows(rows, gathered[i], first, columns, fisher, grads[i + 2 : i + 3])
        other, offset = (late, first - cut) if first >= cut else (early, first)
        merged = merge_rows(low, x_swap(low), own_query, other, first, offset, merged)
    return fisher[None], merged


def solution(mesh):
    axes = (mesh.shape["member"], mesh.shape["seq"], mesh.shape["head"])
    return jax.shard_map(
        functools.partial(on_device, axes),
        mesh=mesh,
        in_specs=(
            P(("seq", "head"), None),
            P(None, "seq"),
            P(),
            P(None, None, "seq"),
            P("member", "seq", "head"),
            P("seq", "head"),
            P(("seq", "head"), None),
            P("member", ("seq", "head"), None),
        ),
        out_specs=(P("member", "seq", "head"), P("seq", "head")),
        check_vma=False,
    )
```

time: 221 us -> 198 us (0.90)
  Pallas kernels: 61.2 us -> 27.2 us
  starting transfers between devices: 46.6 us -> 60.5 us
    pallas_call x7 -> x10, Pallas kernels: 48 us -> 21.8 us  [the longest x3 10.2 us: project_rows(): pl.pallas_call(functools.partial(project_kernel, len(pieces), jobs, len(w...]
    ppermute x8, waiting for transfers between devices: 14.5 us -> 0.02 us  [h_swap(): return lax.ppermute(block, 'head', [(i, i ^ bits) for i in range(heads)])]
    ppermute x6 -> x8, waiting for transfers between devices: 7.18 us -> 19.1 us  [x_swap(): return lax.ppermute(block, 'member', [(i, i ^ 1) for i in range(members)])]
    ppermute x19 -> x27, starting transfers between devices: 36.5 us -> 48.1 us  [step(): return lax.ppermute(block, 'seq', pairs)]
    pallas_call x2 -> x3, Pallas kernels: 9.98 us -> 4.31 us  [merge_rows(): pl.pallas_call(kernel, grid=(width // tile,), in_specs=specs, out_specs=p...]
    unnamed x58 -> x43, local copies, waits for them, and re-layouts: 4.52 us -> 7.05 us
    slice x9 -> x10, local copies, waits for them, and re-layouts: 4.51 us -> 2.17 us  [the longest x1 1.04 us: on_device(): late, _ = behind(own_query[:, cut:], key_there)]
    ppermute x6 -> x8, starting transfers between devices: 6.26 us -> 8.45 us  [x_swap(): return lax.ppermute(block, 'member', [(i, i ^ 1) for i in range(members)])]
  transfers between devices with their start and end apart: 33 -> 43, of which waited for: 14 -> 22; matrix products, arithmetic and copies ran while one was open for 7% -> 7% of each run, Pallas kernels for 20% -> 12%
where the time goes in v2:
time: 198 us; the launch traced here: 197 us
  waiting for transfers between devices  87.1 us (44%)
  starting transfers between devices  60.5 us (31%)
  Pallas kernels  27.2 us (14%)
  local copies, waits for them, and re-layouts  10.6 us (5%)
  other arithmetic  10.2 us (5%)
    ppermute x27, waiting for transfers between devices, step(): return lax.ppermute(block, 'seq', pairs)  68 us
    ppermute x27, starting transfers between devices, step(): return lax.ppermute(block, 'seq', pairs)  48.1 us
    ppermute x8, waiting for transfers between devices, x_swap(): return lax.ppermute(block, 'member', [(i, i ^ 1) for i in range(members)])  19.1 us
    pallas_call x3, Pallas kernels, project_rows(): pl.pallas_call(functools.partial(project_kernel, len(pieces), jobs, len(w...  10.2 us
    ppermute x8, starting transfers between devices, x_swap(): return lax.ppermute(block, 'member', [(i, i ^ 1) for i in range(members)])  8.45 us
    unnamed x43, local copies, waits for them, and re-layouts  7.05 us
    pallas_call x3, Pallas kernels, fisher_rows(): pl.pallas_call(kernel, in_specs=specs, out_specs=[pl.BlockSpec(memory_spa...  6.34 us
    pallas_call x3, Pallas kernels, attention_grad(): pl.pallas_call(drop(functools.partial(attention_kernel, first, block), 6,...  4.51 us
  transfers between devices with their start and end apart: 43, of which 22 were waited for; matrix products, arithmetic and copies ran while one was open for 7% of the time, Pallas kernels for 12%

profile of v2, /device:TPU:0, one launch (start us, length us, event | category | flops | bytes accessed | tf_op | source)
XLA Modules:
  0.0 197.1 jit_solution(196844734770446732)
XLA Ops:
  0.7 1.4 copy-done.6
  2.1 1.1 spread_rows.1
  3.3 3.1 %collective-permute-start = (bf16[64,1280]{1,0:T(8,128)(2,1)S(1)}, bf16[64,1280]{1,0:T(8,128)(2,1)S(1)}, u32[]{:S(2)}, u32[]{:S(2)}) collective-permute-start(bf16[64,1280]{1,0:T(8,128)(2,1)S(1)} %get-tuple-element.37), channel_id=1, source_target_pairs={{0,4},{4,8},{8,12},{12,0},{1,5},{5,9},{9,13},{13,1},{2,6},{6,10},{... | collective-permute-start | bytes 491528 | tf_op jit(solution)/shard_map/ppermute | solution.py:346
  6.3 2.6 %collective-permute-start.1 = (bf16[64,1280]{1,0:T(8,128)(2,1)S(1)}, bf16[64,1280]{1,0:T(8,128)(2,1)}, u32[]{:S(2)}, u32[]{:S(2)}) collective-permute-start(bf16[64,1280]{1,0:T(8,128)(2,1)S(1)} %get-tuple-element.38), channel_id=1, source_target_pairs={{0,8},{4,12},{8,0},{12,4},{1,9},{5,13},{9,1},{13,5},{2,10},{6,14},... | collective-permute-start | bytes 491528 | tf_op jit(solution)/shard_map/ppermute | solution.py:346
  8.9 1.3 collective-permute-start.2
  10.3 1.1 fusion.2
  11.4 1.5 collective-permute-start.25
  14.6 5.1 %collective-permute-done.1 = bf16[64,1280]{1,0:T(8,128)(2,1)} collective-permute-done((bf16[64,1280]{1,0:T(8,128)(2,1)S(1)}, bf16[64,1280]{1,0:T(8,128)(2,1)}, u32[]{:S(2)}, u32[]{:S(2)}) %collective-permute-start.1) | collective-permute-done | bytes 163872 | tf_op jit(solution)/shard_map/ppermute | solution.py:346
  19.8 2.0 %pad_maximum_fusion.3.refs_0_ = bf16[4,64,1280]{2,1,0:T(8,128)(2,1)} fusion(bf16[1,64,1280]{2,1,0:T(8,128)(2,1)} %bitcast.5, bf16[1,64,1280]{2,1,0:T(8,128)(2,1)} %bitcast.4, bf16[1,64,1280]{2,1,0:T(8,128)(2,1)S(1)} %bitcast.46, bf16[1,64,1280]{2,1,0:T(8,128)(2,1)S(1)} %bitcast.42), kind=kLoop, calls=%fused_computation.15 | loop fusion | flops 983040 | bytes 1310720 | tf_op jit(solution)/shard_map/stack | solution.py:353
  22.1 1.5 collective-permute-start.4
  23.6 1.0 sine_multiply_fusion
  25.0 1.6 collective-permute-start.8
  26.6 3.5 %project_rows.3 = (bf16[4,128,1280]{2,1,0:T(8,128)(2,1)S(1)}, f32[256,640]{1,0:T(8,128)S(1)}, f32[256,640]{1,0:T(8,128)S(1)}, bf16[128,640]{1,0:T(8,128)(2,1)}, ...) custom-call(bf16[4,64,1280]{2,1,0:T(8,128)(2,1)} %pad_maximum_fusion.3.refs_0_, ...), custom_call_target="tpu_custom_call" | custom-call | tf_op jit(solution)/shard_map/project_rows/pallas_call | solution.py:316
  30.1 1.1 copy-done.2
  33.7 4.0 %collective-permute-start.5 = (bf16[128,640]{1,0:T(8,128)(2,1)}, bf16[128,640]{1,0:T(8,128)(2,1)}, u32[]{:S(2)}, u32[]{:S(2)}) collective-permute-start(bf16[128,640]{1,0:T(8,128)(2,1)} %get-tuple-element.42), channel_id=1, source_target_pairs={{0,4},{4,8},{8,12},{12,0},{1,5},{5,9},{9,13},{13,1},{2,6},{6,10},{... | collective-permute-start | bytes 491528 | tf_op jit(solution)/shard_map/ppermute | solution.py:346
  37.7 1.1 collective-permute-start.6
  38.8 1.2 sine_multiply_fusion.1
  40.9 1.0 slice.155
  42.0 1.5 pad_maximum_fusion.1
  44.1 2.8 %collective-permute-done.6 = bf16[128,640]{1,0:T(8,128)(2,1)} collective-permute-done((bf16[128,640]{1,0:T(8,128)(2,1)}, bf16[128,640]{1,0:T(8,128)(2,1)}, u32[]{:S(2)}, u32[]{:S(2)}) %collective-permute-start.6) | collective-permute-done | bytes 163872 | tf_op jit(solution)/shard_map/ppermute | solution.py:346
  49.9 2.5 %collective-permute-start.15 = (bf16[256,640]{1,0:T(8,128)(2,1)S(1)}, bf16[256,640]{1,0:T(8,128)(2,1)S(1)}, u32[]{:S(2)}, u32[]{:S(2)}) collective-permute-start(bf16[256,640]{1,0:T(8,128)(2,1)S(1)} %pad_maximum_fusion.6), channel_id=1, source_target_pairs={{0,12},{4,0},{8,4},{12,8},{1,13},{5,1},{9,5},{13,9},{2,14},{6,2},{... | collective-permute-start | bytes 983048 | tf_op jit(solution)/shard_map/ppermute | solution.py:346
  52.4 3.3 %project_rows.4 = (bf16[4,128,1280]{2,1,0:T(8,128)(2,1)S(1)}, f32[256,640]{1,0:T(8,128)S(1)}, f32[256,640]{1,0:T(8,128)S(1)}, bf16[128,640]{1,0:T(8,128)(2,1)S(1...) custom-call(bf16[4,64,1280]{2,1,0:T(8,128)(2,1)} %collective-permute-done.4.refs_0_, ...), custom_call_target="tpu_custom_call" | custom-call | tf_op jit(solution)/shard_map/project_rows/pallas_call | solution.py:316
  56.8 2.1 %collective-permute-start.14 = (bf16[256,640]{1,0:T(8,128)(2,1)S(1)}, bf16[256,640]{1,0:T(8,128)(2,1)S(1)}, u32[]{:S(2)}, u32[]{:S(2)}) collective-permute-start(bf16[256,640]{1,0:T(8,128)(2,1)S(1)} %pad_maximum_fusion.5), channel_id=1, source_target_pairs={{0,4},{4,8},{8,12},{12,0},{1,5},{5,9},{9,13},{13,1},{2,6},{6,10},{... | collective-permute-start | bytes 983048 | tf_op jit(solution)/shard_map/ppermute | solution.py:346
  58.9 5.7 %collective-permute-done.10.refs_2_ = bf16[4,64,1280]{2,1,0:T(8,128)(2,1)S(1)} collective-permute-done((bf16[4,64,1280]{2,1,0:T(8,128)(2,1)}, bf16[4,64,1280]{2,1,0:T(8,128)(2,1)S(1)}, u32[]{:S(2)}, u32[]{:S(2)}) %collective-permute-start.10) | collective-permute-done | bytes 655392 | tf_op jit(solution)/shard_map/ppermute | solution.py:439
  65.3 9.0 %collective-permute-done.12.refs_7_ = bf16[128,640]{1,0:T(8,128)(2,1)S(1)} collective-permute-done((bf16[128,640]{1,0:T(8,128)(2,1)S(1)}, bf16[128,640]{1,0:T(8,128)(2,1)S(1)}, u32[]{:S(2)}, u32[]{:S(2)}) %collective-permute-start.12) | collective-permute-done | bytes 163872 | tf_op jit(solution)/shard_map/ppermute | solution.py:346
  74.3 3.5 %collective-permute-start.17 = (bf16[256,640]{1,0:T(8,128)(2,1)S(1)}, bf16[256,640]{1,0:T(8,128)(2,1)S(1)}, u32[]{:S(2)}, u32[]{:S(2)}) collective-permute-start(bf16[256,640]{1,0:T(8,128)(2,1)S(1)} %pad_maximum_fusion.8), channel_id=1, source_target_pairs={{0,12},{4,0},{8,4},{12,8},{1,13},{5,1},{9,5},{13,9},{2,14},{6,2},{... | collective-permute-start | bytes 983048 | tf_op jit(solution)/shard_map/ppermute | solution.py:346
  80.1 3.3 %project_rows.5 = (bf16[4,256,1280]{2,1,0:T(8,128)(2,1)S(1)}, f32[256,640]{1,0:T(8,128)S(1)}, f32[256,640]{1,0:T(8,128)S(1)}, bf16[128,640]{1,0:T(8,128)(2,1)S(1...) custom-call(bf16[4,64,1280]{2,1,0:T(8,128)(2,1)} %collective-permute-done.8.refs_0_, ...), custom_call_target="tpu_custom_call" | custom-call | tf_op jit(solution)/shard_map/project_rows/pallas_call | solution.py:316
  83.5 3.8 %collective-permute-start.20 = (bf16[128,640]{1,0:T(8,128)(2,1)S(1)}, bf16[128,640]{1,0:T(8,128)(2,1)S(1)}, u32[]{:S(2)}, u32[]{:S(2)}) collective-permute-start(bf16[128,640]{1,0:T(8,128)(2,1)S(1)} %get-tuple-element.59), channel_id=1, source_target_pairs={{0,12},{4,0},{8,4},{12,8},{1,13},{5,1},{9,5},{13,9},{2,14},{6,2},{... | collective-permute-start | bytes 491528 | tf_op jit(solution)/shard_map/ppermute | solution.py:346
  87.3 6.9 %collective-permute-done.16 = bf16[256,640]{1,0:T(8,128)(2,1)S(1)} collective-permute-done((bf16[256,640]{1,0:T(8,128)(2,1)S(1)}, bf16[256,640]{1,0:T(8,128)(2,1)S(1)}, u32[]{:S(2)}, u32[]{:S(2)}) %collective-permute-start.16) | collective-permute-done | bytes 327712 | tf_op jit(solution)/shard_map/ppermute | solution.py:346
  96.0 1.5 collective-permute-done.18
  97.6 1.8 collective-permute-done.20
  100.5 4.1 %collective-permute-start.21 = (bf16[256,640]{1,0:T(8,128)(2,1)S(1)}, bf16[256,640]{1,0:T(8,128)(2,1)S(1)}, u32[]{:S(2)}, u32[]{:S(2)}) collective-permute-start(bf16[256,640]{1,0:T(8,128)(2,1)S(1)} %pad_maximum_fusion.10), channel_id=1, source_target_pairs={{0,12},{4,0},{8,4},{12,8},{1,13},{5,1},{9,5},{13,9},{2,14},{6,2},{... | collective-permute-start | bytes 983048 | tf_op jit(solution)/shard_map/ppermute | solution.py:346
  104.7 3.6 %collective-permute-done.23 = bf16[256,640]{1,0:T(8,128)(2,1)S(1)} collective-permute-done((bf16[256,640]{1,0:T(8,128)(2,1)S(1)}, bf16[256,640]{1,0:T(8,128)(2,1)S(1)}, u32[]{:S(2)}, u32[]{:S(2)}) %collective-permute-start.23) | collective-permute-done | bytes 327712 | tf_op jit(solution)/shard_map/ppermute | solution.py:439
  108.3 1.0 collective-permute-start.29
  109.5 3.2 %collective-permute-done.21 = bf16[256,640]{1,0:T(8,128)(2,1)S(1)} collective-permute-done((bf16[256,640]{1,0:T(8,128)(2,1)S(1)}, bf16[256,640]{1,0:T(8,128)(2,1)S(1)}, u32[]{:S(2)}, u32[]{:S(2)}) %collective-permute-start.21) | collective-permute-done | bytes 327712 | tf_op jit(solution)/shard_map/ppermute | solution.py:346
  112.7 5.6 %collective-permute-done.19 = bf16[256,640]{1,0:T(8,128)(2,1)S(1)} collective-permute-done((bf16[256,640]{1,0:T(8,128)(2,1)S(1)}, bf16[256,640]{1,0:T(8,128)(2,1)S(1)}, u32[]{:S(2)}, u32[]{:S(2)}) %collective-permute-start.19) | collective-permute-done | bytes 327712 | tf_op jit(solution)/shard_map/ppermute | solution.py:346
  118.5 1.7 attention_grad.3.refs_3_
  120.3 1.9 collective-permute-start.28
  122.3 6.6 %collective-permute-done.28.refs_7_.refs_6_ = bf16[256,512]{1,0:T(8,128)(2,1)S(1)} collective-permute-done((bf16[256,512]{1,0:T(8,128)(2,1)S(1)}, bf16[256,512]{1,0:T(8,128)(2,1)S(1)}, u32[]{:S(2)}, u32[]{:S(2)}) %collective-permute-start.28) | collective-permute-done | bytes 262176 | tf_op jit(solution)/shard_map/ppermute | solution.py:346
  128.9 4.4 %collective-permute-done.27.refs_6_.refs_4_ = bf16[256,512]{1,0:T(8,128)(2,1)S(1)} collective-permute-done((bf16[256,512]{1,0:T(8,128)(2,1)S(1)}, bf16[256,512]{1,0:T(8,128)(2,1)S(1)}, u32[]{:S(2)}, u32[]{:S(2)}) %collective-permute-start.27) | collective-permute-done | bytes 262176 | tf_op jit(solution)/shard_map/ppermute | solution.py:346
  133.3 1.7 attention_grad.4.refs_3_
  135.1 1.7 collective-permute-start.31
  137.2 3.5 %collective-permute-start.39 = (bf16[128,512]{1,0:T(8,128)(2,1)S(1)}, bf16[128,512]{1,0:T(8,128)(2,1)S(1)}, u32[]{:S(2)}, u32[]{:S(2)}) collective-permute-start(bf16[128,512]{1,0:T(8,128)(2,1)S(1)} %slice.161), channel_id=1, source_target_pairs={{0,12},{4,0},{8,4},{12,8},{1,13},{5,1},{9,5},{13,9},{2,14},{6,2},{... | collective-permute-start | bytes 393224 | tf_op jit(solution)/shard_map/ppermute | solution.py:346
  140.8 2.8 %collective-permute-done.31.refs_7_.refs_6_ = bf16[256,512]{1,0:T(8,128)(2,1)S(1)} collective-permute-done((bf16[256,512]{1,0:T(8,128)(2,1)S(1)}, bf16[256,512]{1,0:T(8,128)(2,1)S(1)}, u32[]{:S(2)}, u32[]{:S(2)}) %collective-permute-start.31) | collective-permute-done | bytes 262176 | tf_op jit(solution)/shard_map/ppermute | solution.py:346
  143.6 4.3 %collective-permute-start.37 = (bf16[128,512]{1,0:T(8,128)(2,1)S(1)}, bf16[128,512]{1,0:T(8,128)(2,1)S(1)}, u32[]{:S(2)}, u32[]{:S(2)}) collective-permute-start(bf16[128,512]{1,0:T(8,128)(2,1)S(1)} %slice.159), channel_id=1, source_target_pairs={{0,12},{4,0},{8,4},{12,8},{1,13},{5,1},{9,5},{13,9},{2,14},{6,2},{... | collective-permute-start | bytes 393224 | tf_op jit(solution)/shard_map/ppermute | solution.py:346
  147.9 3.3 %collective-permute-done.30.refs_6_.refs_4_ = bf16[256,512]{1,0:T(8,128)(2,1)S(1)} collective-permute-done((bf16[256,512]{1,0:T(8,128)(2,1)S(1)}, bf16[256,512]{1,0:T(8,128)(2,1)S(1)}, u32[]{:S(2)}, u32[]{:S(2)}) %collective-permute-start.30) | collective-permute-done | bytes 262176 | tf_op jit(solution)/shard_map/ppermute | solution.py:346
  152.0 4.8 %collective-permute-done.38 = bf16[128,512]{1,0:T(8,128)(2,1)S(1)} collective-permute-done((bf16[128,512]{1,0:T(8,128)(2,1)S(1)}, bf16[128,512]{1,0:T(8,128)(2,1)S(1)}, u32[]{:S(2)}, u32[]{:S(2)}) %collective-permute-start.38) | collective-permute-done | bytes 131104 | tf_op jit(solution)/shard_map/ppermute | solution.py:346
  156.8 1.0 attention_grad.5.refs_7_.refs_3_
  157.9 2.4 %fisher_rows.3 = (f32[1280,640]{1,0:T(8,128)}, bf16[1280,256]{1,0:T(8,128)(2,1)S(1)}) custom-call(bf16[4,128,1280]{2,1,0:T(8,128)(2,1)S(1)} %copy-done.3, bf16[4,128,1280]{2,1,0:T(8,128)(2,1)S(1)} %get-tuple-element.45.refs_6_.refs_1_, bf16[4,256,1280]{2,1,0:T(8,128)(2,1)S(1)} %get-tuple-element.50.refs_2_, bf16[256,512]{1,0:T(8,128)(2,1)S(1)} %attention_grad.3.refs_3_, ...), custom_call_target="tpu_custom_call" | custom-call | tf_op jit(solution)/shard_map/fisher_rows/pallas_call | solution.py:202
  160.2 1.1 collective-permute-start.42
  161.4 2.4 %fisher_rows.4 = (f32[1280,640]{1,0:T(8,128)}, bf16[1280,256]{1,0:T(8,128)(2,1)S(1)}) custom-call(bf16[4,128,1280]{2,1,0:T(8,128)(2,1)S(1)} %copy-done.3, bf16[4,128,1280]{2,1,0:T(8,128)(2,1)S(1)} %get-tuple-element.45.refs_6_.refs_1_, bf16[4,256,1280]{2,1,0:T(8,128)(2,1)S(1)} %get-tuple-element.50.refs_2_, ...), custom_call_target="tpu_custom_call", output_to_operand_aliasing={{0}: (7, {})} | custom-call | tf_op jit(solution)/shard_map/fisher_rows/pallas_call | solution.py:202
  163.7 1.1 collective-permute-start.41
  164.8 1.5 collective-permute-start.34
  166.9 3.1 %collective-permute-done.34.refs_6_ = bf16[128,512]{1,0:T(8,128)(2,1)S(1)} collective-permute-done((bf16[128,512]{1,0:T(8,128)(2,1)S(1)}, bf16[128,512]{1,0:T(8,128)(2,1)S(1)}, u32[]{:S(2)}, u32[]{:S(2)}) %collective-permute-start.34) | collective-permute-done | bytes 131104 | tf_op jit(solution)/shard_map/ppermute | solution.py:346
  170.0 4.3 %collective-permute-start.35 = (bf16[64,512]{1,0:T(8,128)(2,1)S(1)}, bf16[64,512]{1,0:T(8,128)(2,1)S(1)}, u32[]{:S(2)}, u32[]{:S(2)}) collective-permute-start(bf16[64,512]{1,0:T(8,128)(2,1)S(1)} %slice.157), channel_id=1, source_target_pairs={{0,12},{4,0},{8,4},{12,8},{1,13},{5,1},{9,5},{13,9},{2,14},{6,2},{... | collective-permute-start | bytes 196616 | tf_op jit(solution)/shard_map/ppermute | solution.py:346
  174.3 1.8 collective-permute-done.35
  176.2 4.2 %collective-permute-done.33 = bf16[64,512]{1,0:T(8,128)(2,1)S(1)} collective-permute-done((bf16[64,512]{1,0:T(8,128)(2,1)S(1)}, bf16[64,512]{1,0:T(8,128)(2,1)S(1)}, u32[]{:S(2)}, u32[]{:S(2)}) %collective-permute-start.33) | collective-permute-done | bytes 65568 | tf_op jit(solution)/shard_map/ppermute | solution.py:346
  180.4 1.6 fisher_rows.5
  182.0 1.1 collective-permute-start.40
  183.1 1.5 merge_rows.3.refs_4_
  184.6 7.4 %collective-permute-done.41.refs_1_ = bf16[1280,256]{1,0:T(8,128)(2,1)S(1)} collective-permute-done((bf16[1280,256]{1,0:T(8,128)(2,1)S(1)}, bf16[1280,256]{1,0:T(8,128)(2,1)S(1)}, u32[]{:S(2)}, u32[]{:S(2)}) %collective-permute-start.41) | collective-permute-done | bytes 655392 | tf_op jit(solution)/shard_map/ppermute | solution.py:439
  192.0 1.6 merge_rows.4.refs_4_
  193.6 2.3 %collective-permute-done.40.refs_1_ = bf16[1280,128]{1,0:T(8,128)(2,1)S(1)} collective-permute-done((bf16[1280,128]{1,0:T(8,128)(2,1)S(1)}, bf16[1280,128]{1,0:T(8,128)(2,1)S(1)}, u32[]{:S(2)}, u32[]{:S(2)}) %collective-permute-start.40) | collective-permute-done | bytes 327712 | tf_op jit(solution)/shard_map/ppermute | solution.py:439
  195.9 1.2 merge_rows.5
  (146 shorter events, 18.8 us)
Async XLA Ops:
  0.6 21.2 %copy-start = (bf16[2,256,1280]{2,1,0:T(8,128)(2,1)S(1)}, bf16[2,256,1280]{2,1,0:T(8,128)(2,1)}, u32[]{:S(2)}) copy-start(bf16[2,256,1280]{2,1,0:T(8,128)(2,1)} %param.11) | copy-start | bytes 3932164
  0.7 1.4 copy-start.6
  2.1 8.1 %copy-start.18 = (bf16[128,2560]{1,0:T(8,128)(2,1)S(1)}, bf16[128,2560]{1,0:T(8,128)(2,1)}, u32[]{:S(2)}) copy-start(bf16[128,2560]{1,0:T(8,128)(2,1)} %param.14) | copy-start | bytes 1966084
  2.1 8.1 %copy-start.19 = (bf16[1,128,2560]{2,1,0:T(8,128)(2,1)S(1)}, bf16[1,128,2560]{2,1,0:T(8,128)(2,1)}, u32[]{:S(2)}) copy-start(bf16[1,128,2560]{2,1,0:T(8,128)(2,1)} %param.15) | copy-start | bytes 1966084
  3.3 11.0 %collective-permute-start = (bf16[64,1280]{1,0:T(8,128)(2,1)S(1)}, bf16[64,1280]{1,0:T(8,128)(2,1)S(1)}, u32[]{:S(2)}, u32[]{:S(2)}) collective-permute-start(bf16[64,1280]{1,0:T(8,128)(2,1)S(1)} %get-tuple-element.37), channel_id=1, source_target_pairs={{0,4},{4,8},{8,12},{12,0},{1,5},{5,9},{9,13},{13,1},{2,6},{6,10},{... | collective-permute-start | bytes 491528 | tf_op jit(solution)/shard_map/ppermute | solution.py:346
  6.3 13.4 %collective-permute-start.1 = (bf16[64,1280]{1,0:T(8,128)(2,1)S(1)}, bf16[64,1280]{1,0:T(8,128)(2,1)}, u32[]{:S(2)}, u32[]{:S(2)}) collective-permute-start(bf16[64,1280]{1,0:T(8,128)(2,1)S(1)} %get-tuple-element.38), channel_id=1, source_target_pairs={{0,8},{4,12},{8,0},{12,4},{1,9},{5,13},{9,1},{13,5},{2,10},{6,14},... | collective-permute-start | bytes 491528 | tf_op jit(solution)/shard_map/ppermute | solution.py:346
  8.9 10.9 %collective-permute-start.2 = (bf16[64,1280]{1,0:T(8,128)(2,1)S(1)}, bf16[64,1280]{1,0:T(8,128)(2,1)}, u32[]{:S(2)}, u32[]{:S(2)}) collective-permute-start(bf16[64,1280]{1,0:T(8,128)(2,1)S(1)} %get-tuple-element.39), channel_id=1, source_target_pairs={{0,12},{4,0},{8,4},{12,8},{1,13},{5,1},{9,5},{13,9},{2,14},{6,2},{... | collective-permute-start | bytes 491528 | tf_op jit(solution)/shard_map/ppermute | solution.py:346
  10.3 2.7 %copy-start.15 = (s32[4]{0:T(128)S(1)}, s32[4]{0:T(128)}, u32[]{:S(2)}) copy-start(s32[4]{0:T(128)} %param.10) | copy-start | bytes 52
  10.3 3.4 %copy-start.20 = (s32[3,512]{1,0:T(4,128)S(1)}, s32[3,512]{1,0:T(4,128)}, u32[]{:S(2)}) copy-start(s32[3,512]{1,0:T(4,128)} %param.9) | copy-start | bytes 18436
  11.4 22.3 %collective-permute-start.24 = (bf16[2,128,640]{2,1,0:T(8,128)(2,1)}, bf16[2,128,640]{2,1,0:T(8,128)(2,1)}, u32[]{:S(2)}, u32[]{:S(2)}) collective-permute-start(bf16[2,128,640]{2,1,0:T(8,128)(2,1)} %get-tuple-element.75), channel_id=1, source_target_pairs={{0,1},{1,0},{2,3},{3,2},{4,5},{5,4},{6,7},{7,6},{8,9},{9,8},{10,11... | collective-permute-start | bytes 983048 | tf_op jit(solution)/shard_map/ppermute | solution.py:442
  11.4 26.3 %collective-permute-start.25 = (bf16[2,128,640]{2,1,0:T(8,128)(2,1)}, bf16[2,128,640]{2,1,0:T(8,128)(2,1)}, u32[]{:S(2)}, u32[]{:S(2)}) collective-permute-start(bf16[2,128,640]{2,1,0:T(8,128)(2,1)} %get-tuple-element.76), channel_id=1, source_target_pairs={{0,2},{1,3},{2,0},{3,1},{4,6},{5,7},{6,4},{7,5},{8,10},{9,11},{10,... | collective-permute-start | bytes 983048 | tf_op jit(solution)/shard_map/ppermute | solution.py:442
  14.2 27.7 %collective-permute-start.26 = (bf16[2,128,640]{2,1,0:T(8,128)(2,1)}, bf16[2,128,640]{2,1,0:T(8,128)(2,1)}, u32[]{:S(2)}, u32[]{:S(2)}) collective-permute-start(bf16[2,128,640]{2,1,0:T(8,128)(2,1)} %get-tuple-element.77), channel_id=1, source_target_pairs={{0,3},{1,2},{2,1},{3,0},{4,7},{5,6},{6,5},{7,4},{8,11},{9,10},{10,... | collective-permute-start | bytes 983048 | tf_op jit(solution)/shard_map/ppermute | solution.py:442
  19.8 6.8 %copy-start.4 = (bf16[1280,640]{1,0:T(8,128)(2,1)S(1)}, bf16[1280,640]{1,0:T(8,128)(2,1)}, u32[]{:S(2)}) copy-start(bf16[1280,640]{1,0:T(8,128)(2,1)} %refs_4_.3) | copy-start | bytes 4915204
  21.8 4.7 %copy-start.1 = (bf16[1,1280,640]{2,1,0:T(8,128)(2,1)S(1)}, bf16[1,1280,640]{2,1,0:T(8,128)(2,1)}, u32[]{:S(2)}) copy-start(bf16[1,1280,640]{2,1,0:T(8,128)(2,1)} %param.12) | copy-start | bytes 4915204
  21.8 3.2 %collective-permute-start.3 = (bf16[4,64,1280]{2,1,0:T(8,128)(2,1)}, bf16[4,64,1280]{2,1,0:T(8,128)(2,1)S(1)}, u32[]{:S(2)}, u32[]{:S(2)}) collective-permute-start(bf16[4,64,1280]{2,1,0:T(8,128)(2,1)} %pad_maximum_fusion.3.refs_0_), channel_id=1, source_target_pairs={{0,1},{1,0},{2,3},{3,2},{4,5},{5,4},{6,7},{7,6},{8,9},{9,8},{10,11... | collective-permute-start | bytes 1966088 | tf_op jit(solution)/shard_map/ppermute | solution.py:442
  22.1 21.3 %collective-permute-start.4 = (bf16[4,64,1280]{2,1,0:T(8,128)(2,1)}, bf16[4,64,1280]{2,1,0:T(8,128)(2,1)}, u32[]{:S(2)}, u32[]{:S(2)}) collective-permute-start(bf16[4,64,1280]{2,1,0:T(8,128)(2,1)} %pad_maximum_fusion.3.refs_0_), channel_id=1, source_target_pairs={{0,2},{1,3},{2,0},{3,1},{4,6},{5,7},{6,4},{7,5},{8,10},{9,11},{10,... | collective-permute-start | bytes 1966088 | tf_op jit(solution)/shard_map/ppermute | solution.py:442
  25.0 23.3 %collective-permute-start.8 = (bf16[4,64,1280]{2,1,0:T(8,128)(2,1)}, bf16[4,64,1280]{2,1,0:T(8,128)(2,1)}, u32[]{:S(2)}, u32[]{:S(2)}) collective-permute-start(bf16[4,64,1280]{2,1,0:T(8,128)(2,1)} %pad_maximum_fusion.3.refs_0_), channel_id=1, source_target_pairs={{0,16},{16,0},{1,17},{17,1},{2,18},{18,2},{3,19},{19,3},{4,20},{20... | collective-permute-start | bytes 1966088 | tf_op jit(solution)/shard_map/ppermute | solution.py:439
  30.1 1.1 copy-start.2
  31.2 0.8 copy-start.7
  32.0 0.8 copy-start.11
  32.8 0.9 copy-start.13
  33.7 10.4 %collective-permute-start.5 = (bf16[128,640]{1,0:T(8,128)(2,1)}, bf16[128,640]{1,0:T(8,128)(2,1)}, u32[]{:S(2)}, u32[]{:S(2)}) collective-permute-start(bf16[128,640]{1,0:T(8,128)(2,1)} %get-tuple-element.42), channel_id=1, source_target_pairs={{0,4},{4,8},{8,12},{12,0},{1,5},{5,9},{9,13},{13,1},{2,6},{6,10},{... | collective-permute-start | bytes 491528 | tf_op jit(solution)/shard_map/ppermute | solution.py:346
  37.7 9.2 %collective-permute-start.6 = (bf16[128,640]{1,0:T(8,128)(2,1)}, bf16[128,640]{1,0:T(8,128)(2,1)}, u32[]{:S(2)}, u32[]{:S(2)}) collective-permute-start(bf16[128,640]{1,0:T(8,128)(2,1)} %get-tuple-element.43), channel_id=1, source_target_pairs={{0,12},{4,0},{8,4},{12,8},{1,13},{5,1},{9,5},{13,9},{2,14},{6,2},{... | collective-permute-start | bytes 491528 | tf_op jit(solution)/shard_map/ppermute | solution.py:346
  46.9 5.5 %collective-permute-start.7 = (bf16[4,64,1280]{2,1,0:T(8,128)(2,1)}, bf16[4,64,1280]{2,1,0:T(8,128)(2,1)S(1)}, u32[]{:S(2)}, u32[]{:S(2)}) collective-permute-start(bf16[4,64,1280]{2,1,0:T(8,128)(2,1)} %collective-permute-done.4.refs_0_), channel_id=1, source_target_pairs={{0,1},{1,0},{2,3},{3,2},{4,5},{5,4},{6,7},{7,6},{8,9},{9,8},{10,11... | collective-permute-start | bytes 1966088 | tf_op jit(solution)/shard_map/ppermute | solution.py:442
  47.0 1.1 copy-start.12
  47.0 1.3 copy-start.14
  47.0 5.4 %copy-start.5 = (bf16[1280,640]{1,0:T(8,128)(2,1)S(1)}, bf16[1280,640]{1,0:T(8,128)(2,1)}, u32[]{:S(2)}) copy-start(bf16[1280,640]{1,0:T(8,128)(2,1)} %refs_4_.3) | copy-start | bytes 4915204
  47.2 5.2 %copy-start.3 = (bf16[4,128,1280]{2,1,0:T(8,128)(2,1)S(1)}, bf16[4,128,1280]{2,1,0:T(8,128)(2,1)}, u32[]{:S(2)}) copy-start(bf16[4,128,1280]{2,1,0:T(8,128)(2,1)} %copy-done.2) | copy-start | bytes 3932164
  47.2 17.4 %collective-permute-start.10 = (bf16[4,64,1280]{2,1,0:T(8,128)(2,1)}, bf16[4,64,1280]{2,1,0:T(8,128)(2,1)S(1)}, u32[]{:S(2)}, u32[]{:S(2)}) collective-permute-start(bf16[4,64,1280]{2,1,0:T(8,128)(2,1)} %collective-permute-done.4.refs_0_), channel_id=1, source_target_pairs={{0,16},{16,0},{1,17},{17,1},{2,18},{18,2},{3,19},{19,3},{4,20},{20... | collective-permute-start | bytes 1966088 | tf_op jit(solution)/shard_map/ppermute | solution.py:439
  48.3 31.7 %collective-permute-start.9 = (bf16[4,64,1280]{2,1,0:T(8,128)(2,1)}, bf16[4,64,1280]{2,1,0:T(8,128)(2,1)S(1)}, u32[]{:S(2)}, u32[]{:S(2)}) collective-permute-start(bf16[4,64,1280]{2,1,0:T(8,128)(2,1)} %collective-permute-done.8.refs_0_), channel_id=1, source_target_pairs={{0,1},{1,0},{2,3},{3,2},{4,5},{5,4},{6,7},{7,6},{8,9},{9,8},{10,11... | collective-permute-start | bytes 1966088 | tf_op jit(solution)/shard_map/ppermute | solution.py:442
  49.9 28.1 %collective-permute-start.15 = (bf16[256,640]{1,0:T(8,128)(2,1)S(1)}, bf16[256,640]{1,0:T(8,128)(2,1)S(1)}, u32[]{:S(2)}, u32[]{:S(2)}) collective-permute-start(bf16[256,640]{1,0:T(8,128)(2,1)S(1)} %pad_maximum_fusion.6), channel_id=1, source_target_pairs={{0,12},{4,0},{8,4},{12,8},{1,13},{5,1},{9,5},{13,9},{2,14},{6,2},{... | collective-permute-start | bytes 983048 | tf_op jit(solution)/shard_map/ppermute | solution.py:346
  55.7 8.9 %collective-permute-start.13 = (bf16[128,640]{1,0:T(8,128)(2,1)S(1)}, bf16[128,640]{1,0:T(8,128)(2,1)S(1)}, u32[]{:S(2)}, u32[]{:S(2)}) collective-permute-start(bf16[128,640]{1,0:T(8,128)(2,1)S(1)} %get-tuple-element.47), channel_id=1, source_target_pairs={{0,12},{4,0},{8,4},{12,8},{1,13},{5,1},{9,5},{13,9},{2,14},{6,2},{... | collective-permute-start | bytes 491528 | tf_op jit(solution)/shard_map/ppermute | solution.py:346
  56.8 21.4 %collective-permute-start.14 = (bf16[256,640]{1,0:T(8,128)(2,1)S(1)}, bf16[256,640]{1,0:T(8,128)(2,1)S(1)}, u32[]{:S(2)}, u32[]{:S(2)}) collective-permute-start(bf16[256,640]{1,0:T(8,128)(2,1)S(1)} %pad_maximum_fusion.5), channel_id=1, source_target_pairs={{0,4},{4,8},{8,12},{12,0},{1,5},{5,9},{9,13},{13,1},{2,6},{6,10},{... | collective-permute-start | bytes 983048 | tf_op jit(solution)/shard_map/ppermute | solution.py:346
  64.6 15.5 %collective-permute-start.11 = (bf16[4,64,1280]{2,1,0:T(8,128)(2,1)S(1)}, bf16[4,64,1280]{2,1,0:T(8,128)(2,1)S(1)}, u32[]{:S(2)}, u32[]{:S(2)}) collective-permute-start(bf16[4,64,1280]{2,1,0:T(8,128)(2,1)S(1)} %collective-permute-done.10.refs_2_), channel_id=1, source_target_pairs={{0,1},{1,0},{2,3},{3,2},{4,5},{5,4},{6,7},{7,6},{8,9},{9,8},{10,11... | collective-permute-start | bytes 1966088 | tf_op jit(solution)/shard_map/ppermute | solution.py:442
  64.7 13.6 %copy-start.8 = (f32[256,640]{1,0:T(8,128)S(1)}, f32[256,640]{1,0:T(8,128)}, u32[]{:S(2)}) copy-start(f32[256,640]{1,0:T(8,128)} %copy-done.7) | copy-start | bytes 1966084
  64.7 9.7 %collective-permute-start.12 = (bf16[128,640]{1,0:T(8,128)(2,1)S(1)}, bf16[128,640]{1,0:T(8,128)(2,1)S(1)}, u32[]{:S(2)}, u32[]{:S(2)}) collective-permute-start(bf16[128,640]{1,0:T(8,128)(2,1)S(1)} %get-tuple-element.46), channel_id=1, source_target_pairs={{0,4},{4,8},{8,12},{12,0},{1,5},{5,9},{9,13},{13,1},{2,6},{6,10},{... | collective-permute-start | bytes 491528 | tf_op jit(solution)/shard_map/ppermute | solution.py:346
  74.3 12.9 %collective-permute-start.17 = (bf16[256,640]{1,0:T(8,128)(2,1)S(1)}, bf16[256,640]{1,0:T(8,128)(2,1)S(1)}, u32[]{:S(2)}, u32[]{:S(2)}) collective-permute-start(bf16[256,640]{1,0:T(8,128)(2,1)S(1)} %pad_maximum_fusion.8), channel_id=1, source_target_pairs={{0,12},{4,0},{8,4},{12,8},{1,13},{5,1},{9,5},{13,9},{2,14},{6,2},{... | collective-permute-start | bytes 983048 | tf_op jit(solution)/shard_map/ppermute | solution.py:346
  77.9 1.1 copy-start.17
  78.0 16.2 %collective-permute-start.16 = (bf16[256,640]{1,0:T(8,128)(2,1)S(1)}, bf16[256,640]{1,0:T(8,128)(2,1)S(1)}, u32[]{:S(2)}, u32[]{:S(2)}) collective-permute-start(bf16[256,640]{1,0:T(8,128)(2,1)S(1)} %pad_maximum_fusion.7), channel_id=1, source_target_pairs={{0,4},{4,8},{8,12},{12,0},{1,5},{5,9},{9,13},{13,1},{2,6},{6,10},{... | collective-permute-start | bytes 983048 | tf_op jit(solution)/shard_map/ppermute | solution.py:346
  79.0 17.0 %collective-permute-start.22 = (bf16[1280,256]{1,0:T(8,128)(2,1)S(1)}, bf16[1280,256]{1,0:T(8,128)(2,1)S(1)}, u32[]{:S(2)}, u32[]{:S(2)}) collective-permute-start(bf16[1280,256]{1,0:T(8,128)(2,1)S(1)} %copy-done.17), channel_id=1, source_target_pairs={{0,16},{16,0},{1,17},{17,1},{2,18},{18,2},{3,19},{19,3},{4,20},{20... | collective-permute-start | bytes 1966088 | tf_op jit(solution)/shard_map/ppermute | solution.py:439
  83.4 14.2 %collective-permute-start.18 = (bf16[128,640]{1,0:T(8,128)(2,1)S(1)}, bf16[128,640]{1,0:T(8,128)(2,1)S(1)}, u32[]{:S(2)}, u32[]{:S(2)}) collective-permute-start(bf16[128,640]{1,0:T(8,128)(2,1)S(1)} %get-tuple-element.57), channel_id=1, source_target_pairs={{0,4},{4,8},{8,12},{12,0},{1,5},{5,9},{9,13},{13,1},{2,6},{6,10},{... | collective-permute-start | bytes 491528 | tf_op jit(solution)/shard_map/ppermute | solution.py:346
  83.5 15.9 %collective-permute-start.20 = (bf16[128,640]{1,0:T(8,128)(2,1)S(1)}, bf16[128,640]{1,0:T(8,128)(2,1)S(1)}, u32[]{:S(2)}, u32[]{:S(2)}) collective-permute-start(bf16[128,640]{1,0:T(8,128)(2,1)S(1)} %get-tuple-element.59), channel_id=1, source_target_pairs={{0,12},{4,0},{8,4},{12,8},{1,13},{5,1},{9,5},{13,9},{2,14},{6,2},{... | collective-permute-start | bytes 491528 | tf_op jit(solution)/shard_map/ppermute | solution.py:346
  94.3 0.9 copy-start.9
  94.3 1.0 copy-start.10
  96.0 12.2 %copy-start.16 = (bf16[1280,384]{1,0:T(8,128)(2,1)S(1)}, bf16[1280,384]{1,0:T(8,128)(2,1)}, u32[]{:S(2)}) copy-start(bf16[1280,384]{1,0:T(8,128)(2,1)} %slice.155) | copy-start | bytes 2949124
  99.4 8.9 %collective-permute-start.23 = (bf16[256,640]{1,0:T(8,128)(2,1)S(1)}, bf16[256,640]{1,0:T(8,128)(2,1)S(1)}, u32[]{:S(2)}, u32[]{:S(2)}) collective-permute-start(bf16[256,640]{1,0:T(8,128)(2,1)S(1)} %rotate_heads.1), channel_id=1, source_target_pairs={{0,16},{16,0},{1,17},{17,1},{2,18},{18,2},{3,19},{19,3},{4,20},{20... | collective-permute-start | bytes 983048 | tf_op jit(solution)/shard_map/ppermute | solution.py:439
  100.5 12.2 %collective-permute-start.21 = (bf16[256,640]{1,0:T(8,128)(2,1)S(1)}, bf16[256,640]{1,0:T(8,128)(2,1)S(1)}, u32[]{:S(2)}, u32[]{:S(2)}) collective-permute-start(bf16[256,640]{1,0:T(8,128)(2,1)S(1)} %pad_maximum_fusion.10), channel_id=1, source_target_pairs={{0,12},{4,0},{8,4},{12,8},{1,13},{5,1},{9,5},{13,9},{2,14},{6,2},{... | collective-permute-start | bytes 983048 | tf_op jit(solution)/shard_map/ppermute | solution.py:346
  104.6 13.7 %collective-permute-start.19 = (bf16[256,640]{1,0:T(8,128)(2,1)S(1)}, bf16[256,640]{1,0:T(8,128)(2,1)S(1)}, u32[]{:S(2)}, u32[]{:S(2)}) collective-permute-start(bf16[256,640]{1,0:T(8,128)(2,1)S(1)} %pad_maximum_fusion.9), channel_id=1, source_target_pairs={{0,4},{4,8},{8,12},{12,0},{1,5},{5,9},{9,13},{13,1},{2,6},{6,10},{... | collective-permute-start | bytes 983048 | tf_op jit(solution)/shard_map/ppermute | solution.py:346
  108.3 25.1 %collective-permute-start.29 = (bf16[1280,384]{1,0:T(8,128)(2,1)S(1)}, bf16[1280,384]{1,0:T(8,128)(2,1)S(1)}, u32[]{:S(2)}, u32[]{:S(2)}) collective-permute-start(bf16[1280,384]{1,0:T(8,128)(2,1)S(1)} %copy-done.16), channel_id=1, source_target_pairs={{0,16},{16,0},{1,17},{17,1},{2,18},{18,2},{3,19},{19,3},{4,20},{20... | collective-permute-start | bytes 2949128 | tf_op jit(solution)/shard_map/ppermute | solution.py:439
  120.3 8.7 %collective-permute-start.28 = (bf16[256,512]{1,0:T(8,128)(2,1)S(1)}, bf16[256,512]{1,0:T(8,128)(2,1)S(1)}, u32[]{:S(2)}, u32[]{:S(2)}) collective-permute-start(bf16[256,512]{1,0:T(8,128)(2,1)S(1)} %attention_grad.3.refs_3_), channel_id=1, source_target_pairs={{0,12},{4,0},{8,4},{12,8},{1,13},{5,1},{9,5},{13,9},{2,14},{6,2},{... | collective-permute-start | bytes 786440 | tf_op jit(solution)/shard_map/ppermute | solution.py:346
  122.2 11.2 %collective-permute-start.27 = (bf16[256,512]{1,0:T(8,128)(2,1)S(1)}, bf16[256,512]{1,0:T(8,128)(2,1)S(1)}, u32[]{:S(2)}, u32[]{:S(2)}) collective-permute-start(bf16[256,512]{1,0:T(8,128)(2,1)S(1)} %attention_grad.3.refs_3_), channel_id=1, source_target_pairs={{0,4},{4,8},{8,12},{12,0},{1,5},{5,9},{9,13},{13,1},{2,6},{6,10},{... | collective-permute-start | bytes 786440 | tf_op jit(solution)/shard_map/ppermute | solution.py:346
  135.1 8.5 %collective-permute-start.31 = (bf16[256,512]{1,0:T(8,128)(2,1)S(1)}, bf16[256,512]{1,0:T(8,128)(2,1)S(1)}, u32[]{:S(2)}, u32[]{:S(2)}) collective-permute-start(bf16[256,512]{1,0:T(8,128)(2,1)S(1)} %attention_grad.4.refs_3_), channel_id=1, source_target_pairs={{0,12},{4,0},{8,4},{12,8},{1,13},{5,1},{9,5},{13,9},{2,14},{6,2},{... | collective-permute-start | bytes 786440 | tf_op jit(solution)/shard_map/ppermute | solution.py:346
  136.8 14.4 %collective-permute-start.30 = (bf16[256,512]{1,0:T(8,128)(2,1)S(1)}, bf16[256,512]{1,0:T(8,128)(2,1)S(1)}, u32[]{:S(2)}, u32[]{:S(2)}) collective-permute-start(bf16[256,512]{1,0:T(8,128)(2,1)S(1)} %attention_grad.4.refs_3_), channel_id=1, source_target_pairs={{0,4},{4,8},{8,12},{12,0},{1,5},{5,9},{9,13},{13,1},{2,6},{6,10},{... | collective-permute-start | bytes 786440 | tf_op jit(solution)/shard_map/ppermute | solution.py:346
  137.2 14.8 %collective-permute-start.39 = (bf16[128,512]{1,0:T(8,128)(2,1)S(1)}, bf16[128,512]{1,0:T(8,128)(2,1)S(1)}, u32[]{:S(2)}, u32[]{:S(2)}) collective-permute-start(bf16[128,512]{1,0:T(8,128)(2,1)S(1)} %slice.161), channel_id=1, source_target_pairs={{0,12},{4,0},{8,4},{12,8},{1,13},{5,1},{9,5},{13,9},{2,14},{6,2},{... | collective-permute-start | bytes 393224 | tf_op jit(solution)/shard_map/ppermute | solution.py:346
  140.7 16.1 %collective-permute-start.38 = (bf16[128,512]{1,0:T(8,128)(2,1)S(1)}, bf16[128,512]{1,0:T(8,128)(2,1)S(1)}, u32[]{:S(2)}, u32[]{:S(2)}) collective-permute-start(bf16[128,512]{1,0:T(8,128)(2,1)S(1)} %slice.160), channel_id=1, source_target_pairs={{0,4},{4,8},{8,12},{12,0},{1,5},{5,9},{9,13},{13,1},{2,6},{6,10},{... | collective-permute-start | bytes 393224 | tf_op jit(solution)/shard_map/ppermute | solution.py:346
  143.6 17.7 %collective-permute-start.37 = (bf16[128,512]{1,0:T(8,128)(2,1)S(1)}, bf16[128,512]{1,0:T(8,128)(2,1)S(1)}, u32[]{:S(2)}, u32[]{:S(2)}) collective-permute-start(bf16[128,512]{1,0:T(8,128)(2,1)S(1)} %slice.159), channel_id=1, source_target_pairs={{0,12},{4,0},{8,4},{12,8},{1,13},{5,1},{9,5},{13,9},{2,14},{6,2},{... | collective-permute-start | bytes 393224 | tf_op jit(solution)/shard_map/ppermute | solution.py:346
  151.2 10.1 %collective-permute-start.36 = (bf16[128,512]{1,0:T(8,128)(2,1)S(1)}, bf16[128,512]{1,0:T(8,128)(2,1)S(1)}, u32[]{:S(2)}, u32[]{:S(2)}) collective-permute-start(bf16[128,512]{1,0:T(8,128)(2,1)S(1)} %slice.158), channel_id=1, source_target_pairs={{0,4},{4,8},{8,12},{12,0},{1,5},{5,9},{9,13},{13,1},{2,6},{6,10},{... | collective-permute-start | bytes 393224 | tf_op jit(solution)/shard_map/ppermute | solution.py:346
  160.2 22.9 %collective-permute-start.42 = (bf16[1280,256]{1,0:T(8,128)(2,1)S(1)}, bf16[1280,256]{1,0:T(8,128)(2,1)S(1)}, u32[]{:S(2)}, u32[]{:S(2)}) collective-permute-start(bf16[1280,256]{1,0:T(8,128)(2,1)S(1)} %get-tuple-element.68.refs_0_), channel_id=1, source_target_pairs={{0,16},{16,0},{1,17},{17,1},{2,18},{18,2},{3,19},{19,3},{4,20},{20... | collective-permute-start | bytes 1966088 | tf_op jit(solution)/shard_map/ppermute | solution.py:439
  163.7 28.3 %collective-permute-start.41 = (bf16[1280,256]{1,0:T(8,128)(2,1)S(1)}, bf16[1280,256]{1,0:T(8,128)(2,1)S(1)}, u32[]{:S(2)}, u32[]{:S(2)}) collective-permute-start(bf16[1280,256]{1,0:T(8,128)(2,1)S(1)} %get-tuple-element.67.refs_0_), channel_id=1, source_target_pairs={{0,16},{16,0},{1,17},{17,1},{2,18},{18,2},{3,19},{19,3},{4,20},{20... | collective-permute-start | bytes 1966088 | tf_op jit(solution)/shard_map/ppermute | solution.py:439
  164.8 5.1 %collective-permute-start.34 = (bf16[128,512]{1,0:T(8,128)(2,1)S(1)}, bf16[128,512]{1,0:T(8,128)(2,1)S(1)}, u32[]{:S(2)}, u32[]{:S(2)}) collective-permute-start(bf16[128,512]{1,0:T(8,128)(2,1)S(1)} %attention_grad.5.refs_7_.refs_3_), channel_id=1, source_target_pairs={{0,12},{4,0},{8,4},{12,8},{1,13},{5,1},{9,5},{13,9},{2,14},{6,2},{... | collective-permute-start | bytes 393224 | tf_op jit(solution)/shard_map/ppermute | solution.py:346
  166.3 7.9 %collective-permute-start.32 = (bf16[128,512]{1,0:T(8,128)(2,1)S(1)}, bf16[128,512]{1,0:T(8,128)(2,1)S(1)}, u32[]{:S(2)}, u32[]{:S(2)}) collective-permute-start(bf16[128,512]{1,0:T(8,128)(2,1)S(1)} %attention_grad.5.refs_7_.refs_3_), channel_id=1, source_target_pairs={{0,4},{4,8},{8,12},{12,0},{1,5},{5,9},{9,13},{13,1},{2,6},{6,10},{... | collective-permute-start | bytes 393224 | tf_op jit(solution)/shard_map/ppermute | solution.py:346
  170.0 6.2 %collective-permute-start.35 = (bf16[64,512]{1,0:T(8,128)(2,1)S(1)}, bf16[64,512]{1,0:T(8,128)(2,1)S(1)}, u32[]{:S(2)}, u32[]{:S(2)}) collective-permute-start(bf16[64,512]{1,0:T(8,128)(2,1)S(1)} %slice.157), channel_id=1, source_target_pairs={{0,12},{4,0},{8,4},{12,8},{1,13},{5,1},{9,5},{13,9},{2,14},{6,2},{... | collective-permute-start | bytes 196616 | tf_op jit(solution)/shard_map/ppermute | solution.py:346
  174.3 6.1 %collective-permute-start.33 = (bf16[64,512]{1,0:T(8,128)(2,1)S(1)}, bf16[64,512]{1,0:T(8,128)(2,1)S(1)}, u32[]{:S(2)}, u32[]{:S(2)}) collective-permute-start(bf16[64,512]{1,0:T(8,128)(2,1)S(1)} %slice.156), channel_id=1, source_target_pairs={{0,4},{4,8},{8,12},{12,0},{1,5},{5,9},{9,13},{13,1},{2,6},{6,10},{... | collective-permute-start | bytes 196616 | tf_op jit(solution)/shard_map/ppermute | solution.py:346
  182.0 13.9 %collective-permute-start.40 = (bf16[1280,128]{1,0:T(8,128)(2,1)S(1)}, bf16[1280,128]{1,0:T(8,128)(2,1)S(1)}, u32[]{:S(2)}, u32[]{:S(2)}) collective-permute-start(bf16[1280,128]{1,0:T(8,128)(2,1)S(1)} %get-tuple-element.66.refs_0_), channel_id=1, source_target_pairs={{0,16},{16,0},{1,17},{17,1},{2,18},{18,2},{3,19},{19,3},{4,20},{20... | collective-permute-start | bytes 983048 | tf_op jit(solution)/shard_map/ppermute | solution.py:439

commit v3 on v2

--- a/solution.py
+++ b/solution.py
@@ -92,18 +92,19 @@
 
 
 def attention_kernel(
-    first, block, query_ref, key_ref, value_ref, cot_ref, cosine_ref, sine_ref, out_ref
+    own_first, first, block, query_ref, key_ref, value_ref, cot_ref, cosine_ref, sine_ref, out_ref
 ):
     length, heads = query_ref.shape[0], out_ref.shape[0] // HEAD_SIZE
     scale = HEAD_SIZE ** (-0.5)
     for head in range(heads):
         span = slice((first + head) * HEAD_SIZE, (first + head + 1) * HEAD_SIZE)
+        own = slice((own_first + head) * HEAD_SIZE, (own_first + head + 1) * HEAD_SIZE)
         key, value = key_ref[:, span], value_ref[:, span]
         key_turned = key.T
         for start in range(0, length, block):
             rows = slice(start, start + block)
             cosine, sine = cosine_ref[:, rows], sine_ref[:, rows]
-            query = query_ref[rows, span].T
+            query = query_ref[rows, own].T
             inverse = lax.rsqrt(jnp.mean(query * query, axis=0, keepdims=True) + 1e-06)
             normed = query * inverse
             rotated = normed * cosine + turned_partner(normed) * sine
@@ -121,11 +122,13 @@
             out_ref[head * HEAD_SIZE : (head + 1) * HEAD_SIZE, rows] = grad.astype(out_ref.dtype)
 
 
-def attention_grad(query_pre, key, value, cot, cosine, sine, first, count, waits, block=512):
+def attention_grad(
+    query_pre, key, value, cot, cosine, sine, own_first, first, count, waits, block=512
+):
     length = query_pre.shape[0]
     whole = pl.BlockSpec(memory_space=pltpu.VMEM)
     return pl.pallas_call(
-        drop(functools.partial(attention_kernel, first, block), 6, len(waits)),
+        drop(functools.partial(attention_kernel, own_first, first, block), 6, len(waits)),
         in_specs=[whole] * 6 + [pl.BlockSpec(memory_space=pl.ANY)] * len(waits),
         out_specs=whole,
         out_shape=jax.ShapeDtypeStruct((count * HEAD_SIZE, length), jnp.bfloat16),
@@ -278,7 +281,7 @@
     return (rows * (1.0 + modulation[1:2]) + modulation[0:1]).astype(jnp.bfloat16)
 
 
-def project_kernel(pieces, jobs, weights, waits, *refs):
+def project_kernel(pieces, jobs, cuts, weights, waits, *refs):
     piece_refs, modulation_ref = refs[:pieces], refs[pieces]
     weight_refs = refs[pieces + 1 : pieces + 1 + weights]
     rows_ref, *outs = refs[pieces + 1 + weights + waits :]
@@ -298,26 +301,32 @@
             for index, count in jobs
         ]
         products = products[0] if len(jobs) == 1 else jnp.concatenate(products, axis=0)
-        if 2 * away == size:
-            middle = products.shape[0] // 2
-            outs[size][...] = products[middle:].astype(outs[size].dtype)
-            products = products[:middle]
-        outs[away][...] = products.astype(outs[away].dtype)
-
-
-def project_rows(pieces, modulation, weights, jobs, waits):
+        products = products.astype(outs[0].dtype)
+        middle = products.shape[0] // 2
+        for part, (start, stop) in enumerate(zip(cuts[:-1], cuts[1:])):
+            part_outs = outs[part * (size + 1) : (part + 1) * (size + 1)]
+            if 2 * away == size:
+                part_outs[away][...] = products[:middle, start:stop]
+                part_outs[size][...] = products[middle:, start:stop]
+            else:
+                part_outs[away][...] = products[:, start:stop]
+
+
+def project_rows(pieces, modulation, weights, jobs, cuts, waits):
     size, share, width = pieces[0].shape
     length = sum(count for _, count in jobs) * share
-    columns = weights[0].shape[1]
-    terms = [jax.ShapeDtypeStruct((length, columns), jnp.float32)] * size
-    halves = [jax.ShapeDtypeStruct((length // 2, columns), jnp.bfloat16)] * 2
-    terms = terms[: size // 2] + halves[:1] + terms[size // 2 + 1 :] + halves[1:]
+    lengths = [length // 2 if 2 * away == size else length for away in range(size)] + [length // 2]
+    terms = [
+        jax.ShapeDtypeStruct((lines, stop - start), jnp.bfloat16)
+        for start, stop in zip(cuts[:-1], cuts[1:])
+        for lines in lengths
+    ]
     whole = pl.BlockSpec(memory_space=pltpu.VMEM)
     return pl.pallas_call(
-        functools.partial(project_kernel, len(pieces), jobs, len(weights), len(waits)),
+        functools.partial(project_kernel, len(pieces), jobs, cuts, len(weights), len(waits)),
         in_specs=[whole] * (len(pieces) + 1 + len(weights))
         + [pl.BlockSpec(memory_space=pl.ANY)] * len(waits),
-        out_specs=[whole] * (2 + size),
+        out_specs=[pl.BlockSpec()] * (1 + len(terms)),
         out_shape=[jax.ShapeDtypeStruct((size, len(pieces) * share, width), jnp.bfloat16)] + terms,
         compiler_params=pltpu.CompilerParams(vmem_limit_bytes=VMEM_BYTES),
         name="project_rows",
@@ -326,6 +335,10 @@
 
 def to_f32(block):
     return block.astype(jnp.float32)
+
+
+def added(term, message):
+    return (to_f32(term) + to_f32(message)).astype(term.dtype)
 
 
 def behind(*arrays):
@@ -362,7 +375,7 @@
             lax.all_to_all(parts, "seq", split_axis=1, concat_axis=0, tiled=False)
         )
 
-    def project(self, pieces, modulation, weights, jobs, waits):
+    def project(self, pieces, modulation, weights, jobs, cuts, waits):
         size, half = self.size, self.size // 2
         if not self.short:
             share = pieces[0].shape[1]
@@ -376,10 +389,14 @@
                 ).astype(jnp.bfloat16)
                 for index, count in jobs
             ]
-            return rows, jnp.concatenate(terms, axis=1), ()
-        rows, *terms = project_rows(pieces, modulation, weights, jobs, waits)
-        first = self.step(terms[half], 1), self.step(terms[size], -1)
-        return rows, terms, first
+            terms = jnp.concatenate(terms, axis=1)
+            return rows, [(terms[:, :, a:b], ()) for a, b in zip(cuts[:-1], cuts[1:])]
+        rows, *terms = project_rows(pieces, modulation, weights, jobs, cuts, waits)
+        parts = []
+        for part in range(len(cuts) - 1):
+            own = terms[part * (size + 1) : (part + 1) * (size + 1)]
+            parts.append((own, (self.step(own[half], 1), self.step(own[size], -1))))
+        return rows, parts
 
     def sum(self, terms, first):
         size, half = self.size, self.size // 2
@@ -391,35 +408,38 @@
             term_right, term_left = terms[size - away], terms[away]
             if away == half - 1:
                 term_right = jnp.concatenate(
-                    [term_right[:middle] + to_f32(right), term_right[middle:]], axis=0
+                    [added(term_right[:middle], right), term_right[middle:]], axis=0
                 )
                 term_left = jnp.concatenate(
-                    [term_left[:middle], term_left[middle:] + to_f32(left)], axis=0
+                    [term_left[:middle], added(term_left[middle:], left)], axis=0
                 )
             else:
-                term_right, term_left = term_right + to_f32(right), term_left + to_f32(left)
-            right = self.step(term_right.astype(jnp.bfloat16), 1)
-            left = self.step(term_left.astype(jnp.bfloat16), -1)
+                term_right, term_left = added(term_right, right), added(term_left, left)
+            right, left = self.step(term_right, 1), self.step(term_left, -1)
         if half == 1:
-            return terms[0] + to_f32(jnp.concatenate([right, left], axis=0)), (right, left)
-        return terms[0] + to_f32(right) + to_f32(left), (right, left)
-
-    def gather(self, block):
+            return to_f32(terms[0]) + to_f32(jnp.concatenate([right, left], axis=0)), (right, left)
+        return to_f32(terms[0]) + to_f32(right) + to_f32(left), (right, left)
+
+    def spread(self, block):
         size, half = self.size, self.size // 2
         if not self.short:
-            blocks = self.by_distance(lax.all_gather(block, "seq"))
-            return [blocks], [blocks]
+            return [self.by_distance(lax.all_gather(block, "seq"))]
         blocks = [None] * size
         blocks[0] = block
-        right, left = block, block
         for away in range(1, half):
-            right, left = self.step(right, 1), self.step(left, -1)
-            blocks[away], blocks[size - away] = right, left
-        middle = block.shape[0] // 2
-        blocks[half] = jnp.concatenate(
-            [self.step(right[:middle], 1), self.step(left[middle:], -1)], axis=0
-        )
-        return blocks, [right, left]
+            blocks[away] = self.step(blocks[away - 1], 1)
+            blocks[-away] = self.step(blocks[1 - away], -1)
+        return blocks
+
+    def complete(self, blocks, after):
+        half = self.size // 2
+        if not self.short:
+            return blocks, blocks
+        right, left = blocks[half - 1], blocks[(half + 1) % self.size]
+        right, left = behind(right, left, *after)[:2]
+        middle = right.shape[0] // 2
+        last = [self.step(right[:middle], 1), self.step(left[middle:], -1)]
+        return blocks[:half] + [jnp.concatenate(last, axis=0)] + blocks[half + 1 :], last
 
 
 def on_device(
@@ -453,18 +473,29 @@
         return [block, h_swap(block, 1)]
 
     weights = [own_query, key_weight]
-    jobs = [(0, 2), (1, 2)]
+    head_count = columns // HEAD_SIZE
+    last_heads = max(1, head_count // 5)
+    bounds = [0, (head_count - last_heads) // 2, head_count - last_heads, head_count]
+    cut = bounds[1] * HEAD_SIZE
+    jobs, full = [(0, 2), (1, 2)], [0, columns]
     near_y, near_x = h_swap(own, 2), x_swap(own)
-    rows_own, terms_own, first_own = ring.project(both(own), modulation, weights, jobs, [])
+    rows_own, [(terms, first_own)] = ring.project(both(own), modulation, weights, jobs, full, [])
+    sums_own, _ = ring.sum(terms, first_own)
     near_y, _ = behind(near_y, rows_own)
     far = x_swap(near_y)
-    sums_own, last_own = ring.sum(terms_own, first_own)
     near_y = behind(near_y, *first_own)[0]
-    rows_y, terms_y, first_y = ring.project(both(near_y), modulation, weights, jobs, [rows_own])
-    sums_y, _ = ring.sum(terms_y, first_y)
-    rows_x, terms_x, first_x = ring.project(
-        both(near_x) + both(far), modulation, [own_query], [(0, 4)], [rows_y, *first_y, *last_own]
-    )
+    rows_y, [(terms_y, first_y)] = ring.project(
+        both(near_y), modulation, weights, jobs, full, [rows_own]
+    )
+    rows_x, parts_x = ring.project(
+        both(near_x) + both(far),
+        modulation,
+        [own_query],
+        [(0, 4)],
+        [0, cut, columns] if cut else full,
+        [rows_y],
+    )
+    sums_y, _ = ring.sum(terms_y, behind(*first_y, rows_x)[:-1])
     lines = 2 * share
     key_here = jnp.concatenate([sums_own[lines:], sums_y[lines:]], axis=0)
 
@@ -484,35 +515,43 @@
     ).reshape(2, members * heads * share, columns)
     value_rows, cot_rows = halves[0], halves[1]
 
-    head_count = columns // HEAD_SIZE
-    last_heads = max(1, head_count // 5)
-    bounds = [0, (head_count - last_heads) // 2, head_count - last_heads, head_count]
-    cut = bounds[1] * HEAD_SIZE
     early, _ = behind(own_query[:, :cut], far)
     early = x_swap(early)
 
     rows_here = key_here.shape[0]
     key_here = rotate_heads(key_here, cosine[:rows_here], sine[:rows_here])
-    key_here, early = behind(key_here, early, *first_x)[:2]
+    key_here, early = behind(key_here, early, *parts_x[0][1])[:2]
     key_there = x_swap(key_here)
     key_rows = jnp.concatenate([key_here, key_there], axis=0)
     late, _ = behind(own_query[:, cut:], key_there)
     late = x_swap(late)
 
-    query_x, _ = ring.sum(terms_x, first_x)
-    query_pre = jnp.concatenate([sums_own[:lines], sums_y[:lines], query_x], axis=0)
-    operands = query_pre, key_rows, value_rows, cot_rows, cosine.T, sine.T
+    queries, start = [], 0
+    for terms, first in parts_x:
+        query_x, _ = ring.sum(terms, first)
+        span = slice(start, start + query_x.shape[1])
+        queries.append(
+            jnp.concatenate([sums_own[:lines, span], sums_y[:lines, span], query_x], axis=0)
+        )
+        start = span.stop
+
+    operands = key_rows, value_rows, cot_rows, cosine.T, sine.T
     spans = [(first, last) for first, last in zip(bounds[:-1], bounds[1:]) if first < last]
-    grads, gathered, waits = [], [], []
+    fisher, merged, lows, waits, ready = None, None, [], [], []
     for i, (first, last) in enumerate(spans):
-        grads.append(attention_grad(*operands, first, last - first, waits + [late] * (i == 1)))
-        blocks, waits = ring.gather(grads[-1])
-        gathered.append(blocks)
-    fisher, merged = None, None
-    for i, (first, _) in enumerate(spans):
+        part = 1 if len(queries) > 1 and first * HEAD_SIZE >= cut else 0
+        grad_query = attention_grad(
+            queries[part], *operands, first - part * bounds[1], first, last - first, ready
+        )
+        blocks = ring.spread(behind(grad_query, *waits)[0] if i else grad_query)
+        waits = [block for block in blocks[1:] if block is not None]
+        ready = [grad_query] if i else [grad_query, *waits]
+        blocks, far_blocks = ring.complete(blocks, lows[-1:])
+        if i == 0:
+            waits = [*far_blocks, late]
         first = first * HEAD_SIZE
-        rows = [rows_own, rows_y, rows_x]
-        fisher, low = fisher_rows(rows, gathered[i], first, columns, fisher, grads[i + 2 : i + 3])
+        fisher, low = fisher_rows([rows_own, rows_y, rows_x], blocks, first, columns, fisher, [])
+        lows.append(low)
         other, offset = (late, first - cut) if first >= cut else (early, first)
         merged = merge_rows(low, x_swap(low), own_query, other, first, offset, merged)
     return fisher[None], merged

time: 198 us -> 188 us (0.949)
  waiting for transfers between devices: 87.1 us -> 81.5 us
  local copies, waits for them, and re-layouts: 10.6 us -> 7.68 us
  other arithmetic: 10.2 us -> 7.58 us
    ppermute x27 -> x31, waiting for transfers between devices: 68 us -> 61.3 us  [step(): return lax.ppermute(block, 'seq', pairs)]
    unnamed x43 -> x29, local copies, waits for them, and re-layouts: 7.05 us -> 4.18 us
    ppermute x8, starting transfers between devices: 8.45 us -> 10.6 us  [x_swap(): return lax.ppermute(block, 'member', [(i, i ^ 1) for i in range(members)])]
    ppermute x8, waiting for transfers between devices: 0.02 us -> 2.16 us  [h_swap(): return lax.ppermute(block, 'head', [(i, i ^ bits) for i in range(heads)])]
    another operation x7 -> x1, other arithmetic: 2.13 us -> 0.11 us
    ppermute x27 -> x31, starting transfers between devices: 48.1 us -> 47.8 us  [step(): return lax.ppermute(block, 'seq', pairs)]
  transfers between devices with their start and end apart: 43 -> 47, of which waited for: 22 -> 22; matrix products, arithmetic and copies ran while one was open for 7% -> 6% of each run, Pallas kernels for 12% -> 13%
where the time goes in v3:
time: 188 us
  waiting for transfers between devices  81.5 us (43%)
  starting transfers between devices  61.8 us (33%)
  Pallas kernels  27.3 us (15%)
  local copies, waits for them, and re-layouts  7.68 us (4%)
  other arithmetic  7.58 us (4%)
    ppermute x31, waiting for transfers between devices, step(): return lax.ppermute(block, 'seq', pairs)  61.3 us
    ppermute x31, starting transfers between devices, step(): return lax.ppermute(block, 'seq', pairs)  47.8 us
    ppermute x8, waiting for transfers between devices, x_swap(): return lax.ppermute(block, 'member', [(i, i ^ 1) for i in range(members)])  18.1 us
    ppermute x8, starting transfers between devices, x_swap(): return lax.ppermute(block, 'member', [(i, i ^ 1) for i in range(members)])  10.6 us
    pallas_call x3, Pallas kernels, project_rows(): pl.pallas_call(functools.partial(project_kernel, len(pieces), jobs, cuts,...  10.2 us
    pallas_call x3, Pallas kernels, fisher_rows(): pl.pallas_call(kernel, in_specs=specs, out_specs=[pl.BlockSpec(memory_spa...  6.34 us
    pallas_call x3, Pallas kernels, attention_grad(): pl.pallas_call(drop(functools.partial(attention_kernel, own_first, first,...  4.52 us
    pallas_call x3, Pallas kernels, merge_rows(): pl.pallas_call(kernel, grid=(width // tile,), in_specs=specs, out_specs=p...  4.31 us
  transfers between devices with their start and end apart: 47, of which 22 were waited for; matrix products, arithmetic and copies ran while one was open for 6% of the time, Pallas kernels for 13%

profile of v3, /device:TPU:0, one launch (start us, length us, event | category | flops | bytes accessed | tf_op | source)
XLA Modules:
  0.0 187.6 jit_solution(15000090746701474558)
XLA Ops:
  0.7 1.4 copy-done.4
  3.3 3.1 %collective-permute-start = (bf16[64,1280]{1,0:T(8,128)(2,1)S(1)}, bf16[64,1280]{1,0:T(8,128)(2,1)S(1)}, u32[]{:S(2)}, u32[]{:S(2)}) collective-permute-start(bf16[64,1280]{1,0:T(8,128)(2,1)S(1)} %get-tuple-element.52), channel_id=1, source_target_pairs={{0,4},{4,8},{8,12},{12,0},{1,5},{5,9},{9,13},{13,1},{2,6},{6,10},{... | collective-permute-start | bytes 491528 | tf_op jit(solution)/shard_map/ppermute | solution.py:359
  6.3 2.6 %collective-permute-start.1 = (bf16[64,1280]{1,0:T(8,128)(2,1)S(1)}, bf16[64,1280]{1,0:T(8,128)(2,1)}, u32[]{:S(2)}, u32[]{:S(2)}) collective-permute-start(bf16[64,1280]{1,0:T(8,128)(2,1)S(1)} %get-tuple-element.53), channel_id=1, source_target_pairs={{0,8},{4,12},{8,0},{12,4},{1,9},{5,13},{9,1},{13,5},{2,10},{6,14},... | collective-permute-start | bytes 491528 | tf_op jit(solution)/shard_map/ppermute | solution.py:359
  8.9 1.4 collective-permute-start.2
  10.3 1.1 fusion.2
  11.4 1.5 collective-permute-start.27
  14.4 5.4 %collective-permute-done.1 = bf16[64,1280]{1,0:T(8,128)(2,1)} collective-permute-done((bf16[64,1280]{1,0:T(8,128)(2,1)S(1)}, bf16[64,1280]{1,0:T(8,128)(2,1)}, u32[]{:S(2)}, u32[]{:S(2)}) %collective-permute-start.1) | collective-permute-done | bytes 163872 | tf_op jit(solution)/shard_map/ppermute | solution.py:359
  19.8 1.9 %pad_maximum_fusion.3.refs_0_ = bf16[4,64,1280]{2,1,0:T(8,128)(2,1)} fusion(bf16[1,64,1280]{2,1,0:T(8,128)(2,1)} %bitcast.5, bf16[1,64,1280]{2,1,0:T(8,128)(2,1)} %bitcast.4, bf16[1,64,1280]{2,1,0:T(8,128)(2,1)S(1)} %bitcast.46, bf16[1,64,1280]{2,1,0:T(8,128)(2,1)S(1)} %bitcast.42), kind=kLoop, calls=%fused_computation.15 | loop fusion | flops 983040 | bytes 1310720 | tf_op jit(solution)/shard_map/stack | solution.py:366
  22.6 1.5 collective-permute-start.8
  24.1 1.5 collective-permute-start.4
  29.2 1.4 copy-done.2
  30.6 3.6 %project_rows.3 = (bf16[4,128,1280]{2,1,0:T(8,128)(2,1)S(1)}, bf16[256,640]{1,0:T(8,128)(2,1)S(1)}, bf16[256,640]{1,0:T(8,128)(2,1)S(1)}, bf16[128,640]{1,0:T(8,...) custom-call(bf16[4,64,1280]{2,1,0:T(8,128)(2,1)} %pad_maximum_fusion.3.refs_0_, ...), custom_call_target="tpu_custom_call" | custom-call | tf_op jit(solution)/shard_map/project_rows/pallas_call | solution.py:325
  34.2 4.0 %collective-permute-start.5 = (bf16[128,640]{1,0:T(8,128)(2,1)S(1)}, bf16[128,640]{1,0:T(8,128)(2,1)S(1)}, u32[]{:S(2)}, u32[]{:S(2)}) collective-permute-start(bf16[128,640]{1,0:T(8,128)(2,1)S(1)} %get-tuple-element.57), channel_id=1, source_target_pairs={{0,4},{4,8},{8,12},{12,0},{1,5},{5,9},{9,13},{13,1},{2,6},{6,10},{... | collective-permute-start | bytes 491528 | tf_op jit(solution)/shard_map/ppermute | solution.py:359
  38.2 1.1 collective-permute-start.6
  39.4 1.4 pad_maximum_fusion
  40.9 2.1 %collective-permute-done.4.refs_0_ = bf16[4,64,1280]{2,1,0:T(8,128)(2,1)} collective-permute-done((bf16[4,64,1280]{2,1,0:T(8,128)(2,1)}, bf16[4,64,1280]{2,1,0:T(8,128)(2,1)}, u32[]{:S(2)}, u32[]{:S(2)}) %collective-permute-start.4) | collective-permute-done | bytes 655392 | tf_op jit(solution)/shard_map/ppermute | solution.py:462
  43.0 1.6 collective-permute-start.10
  44.5 2.5 %collective-permute-done.6 = bf16[128,640]{1,0:T(8,128)(2,1)S(1)} collective-permute-done((bf16[128,640]{1,0:T(8,128)(2,1)S(1)}, bf16[128,640]{1,0:T(8,128)(2,1)S(1)}, u32[]{:S(2)}, u32[]{:S(2)}) %collective-permute-start.6) | collective-permute-done | bytes 163872 | tf_op jit(solution)/shard_map/ppermute | solution.py:359
  47.1 2.5 %collective-permute-start.13 = (bf16[256,640]{1,0:T(8,128)(2,1)S(1)}, bf16[256,640]{1,0:T(8,128)(2,1)S(1)}, u32[]{:S(2)}, u32[]{:S(2)}) collective-permute-start(bf16[256,640]{1,0:T(8,128)(2,1)S(1)} %pad_maximum_fusion.7), channel_id=1, source_target_pairs={{0,12},{4,0},{8,4},{12,8},{1,13},{5,1},{9,5},{13,9},{2,14},{6,2},{... | collective-permute-start | bytes 983048 | tf_op jit(solution)/shard_map/ppermute | solution.py:359
  49.8 9.8 %collective-permute-done.10.refs_2_ = bf16[4,64,1280]{2,1,0:T(8,128)(2,1)S(1)} collective-permute-done((bf16[4,64,1280]{2,1,0:T(8,128)(2,1)}, bf16[4,64,1280]{2,1,0:T(8,128)(2,1)S(1)}, u32[]{:S(2)}, u32[]{:S(2)}) %collective-permute-start.10) | collective-permute-done | bytes 655392 | tf_op jit(solution)/shard_map/ppermute | solution.py:459
  59.9 1.3 copy-done.3
  61.2 3.3 %project_rows.4 = (bf16[4,128,1280]{2,1,0:T(8,128)(2,1)S(1)}, bf16[256,640]{1,0:T(8,128)(2,1)S(1)}, bf16[256,640]{1,0:T(8,128)(2,1)S(1)}, bf16[128,640]{1,0:T(8,...) custom-call(bf16[4,64,1280]{2,1,0:T(8,128)(2,1)} %collective-permute-done.4.refs_0_, ...), custom_call_target="tpu_custom_call" | custom-call | tf_op jit(solution)/shard_map/project_rows/pallas_call | solution.py:325
  64.5 1.9 %collective-permute-start.14 = (bf16[128,640]{1,0:T(8,128)(2,1)S(1)}, bf16[128,640]{1,0:T(8,128)(2,1)S(1)}, u32[]{:S(2)}, u32[]{:S(2)}) collective-permute-start(bf16[128,640]{1,0:T(8,128)(2,1)S(1)} %get-tuple-element.67), channel_id=1, source_target_pairs={{0,4},{4,8},{8,12},{12,0},{1,5},{5,9},{9,13},{13,1},{2,6},{6,10},{... | collective-permute-start | bytes 491528 | tf_op jit(solution)/shard_map/ppermute | solution.py:359
  66.5 2.0 %collective-permute-start.15 = (bf16[128,640]{1,0:T(8,128)(2,1)S(1)}, bf16[128,640]{1,0:T(8,128)(2,1)S(1)}, u32[]{:S(2)}, u32[]{:S(2)}) collective-permute-start(bf16[128,640]{1,0:T(8,128)(2,1)S(1)} %get-tuple-element.68), channel_id=1, source_target_pairs={{0,12},{4,0},{8,4},{12,8},{1,13},{5,1},{9,5},{13,9},{2,14},{6,2},{... | collective-permute-start | bytes 491528 | tf_op jit(solution)/shard_map/ppermute | solution.py:359
  68.6 1.6 collective-permute-start.22
  70.2 3.3 %project_rows.5 = (bf16[4,256,1280]{2,1,0:T(8,128)(2,1)S(1)}, bf16[256,256]{1,0:T(8,128)(2,1)S(1)}, bf16[256,256]{1,0:T(8,128)(2,1)S(1)}, bf16[128,256]{1,0:T(8,...) custom-call(bf16[4,64,1280]{2,1,0:T(8,128)(2,1)} %collective-permute, ...), custom_call_target="tpu_custom_call" | custom-call | tf_op jit(solution)/shard_map/project_rows/pallas_call | solution.py:325
  73.6 2.9 %collective-permute-done.15 = bf16[128,640]{1,0:T(8,128)(2,1)S(1)} collective-permute-done((bf16[128,640]{1,0:T(8,128)(2,1)S(1)}, bf16[128,640]{1,0:T(8,128)(2,1)S(1)}, u32[]{:S(2)}, u32[]{:S(2)}) %collective-permute-start.15) | collective-permute-done | bytes 163872 | tf_op jit(solution)/shard_map/ppermute | solution.py:359
  77.3 3.2 %collective-permute-start.24 = (bf16[128,256]{1,0:T(8,128)(2,1)S(1)}, bf16[128,256]{1,0:T(8,128)(2,1)S(1)}, u32[]{:S(2)}, u32[]{:S(2)}) collective-permute-start(bf16[128,256]{1,0:T(8,128)(2,1)S(1)} %get-tuple-element.79), channel_id=1, source_target_pairs={{0,12},{4,0},{8,4},{12,8},{1,13},{5,1},{9,5},{13,9},{2,14},{6,2},{... | collective-permute-start | bytes 196616 | tf_op jit(solution)/shard_map/ppermute | solution.py:359
  80.6 3.8 %collective-permute-start.20 = (bf16[128,384]{1,0:T(8,128)(2,1)S(1)}, bf16[128,384]{1,0:T(8,128)(2,1)S(1)}, u32[]{:S(2)}, u32[]{:S(2)}) collective-permute-start(bf16[128,384]{1,0:T(8,128)(2,1)S(1)} %get-tuple-element.76), channel_id=1, source_target_pairs={{0,12},{4,0},{8,4},{12,8},{1,13},{5,1},{9,5},{13,9},{2,14},{6,2},{... | collective-permute-start | bytes 294920 | tf_op jit(solution)/shard_map/ppermute | solution.py:359
  84.6 2.1 %collective-permute-start.16 = (bf16[256,640]{1,0:T(8,128)(2,1)S(1)}, bf16[256,640]{1,0:T(8,128)(2,1)S(1)}, u32[]{:S(2)}, u32[]{:S(2)}) collective-permute-start(bf16[256,640]{1,0:T(8,128)(2,1)S(1)} %pad_maximum_fusion.8), channel_id=1, source_target_pairs={{0,4},{4,8},{8,12},{12,0},{1,5},{5,9},{9,13},{13,1},{2,6},{6,10},{... | collective-permute-start | bytes 983048 | tf_op jit(solution)/shard_map/ppermute | solution.py:359
  87.7 4.4 %collective-permute-start.30 = (bf16[256,256]{1,0:T(8,128)(2,1)S(1)}, bf16[256,256]{1,0:T(8,128)(2,1)S(1)}, u32[]{:S(2)}, u32[]{:S(2)}) collective-permute-start(bf16[256,256]{1,0:T(8,128)(2,1)S(1)} %pad_maximum_fusion.15), channel_id=1, source_target_pairs={{0,12},{4,0},{8,4},{12,8},{1,13},{5,1},{9,5},{13,9},{2,14},{6,2},{... | collective-permute-start | bytes 393224 | tf_op jit(solution)/shard_map/ppermute | solution.py:359
  92.1 4.1 %collective-permute-done.17 = bf16[256,640]{1,0:T(8,128)(2,1)S(1)} collective-permute-done((bf16[256,640]{1,0:T(8,128)(2,1)S(1)}, bf16[256,640]{1,0:T(8,128)(2,1)S(1)}, u32[]{:S(2)}, u32[]{:S(2)}) %collective-permute-start.17) | collective-permute-done | bytes 327712 | tf_op jit(solution)/shard_map/ppermute | solution.py:359
  96.7 7.7 %collective-permute-done.16 = bf16[256,640]{1,0:T(8,128)(2,1)S(1)} collective-permute-done((bf16[256,640]{1,0:T(8,128)(2,1)S(1)}, bf16[256,640]{1,0:T(8,128)(2,1)S(1)}, u32[]{:S(2)}, u32[]{:S(2)}) %collective-permute-start.16) | collective-permute-done | bytes 327712 | tf_op jit(solution)/shard_map/ppermute | solution.py:359
  104.3 1.5 collective-permute-start.21
  106.8 1.5 collective-permute-start.25
  109.0 5.8 %collective-permute-done.25 = bf16[256,640]{1,0:T(8,128)(2,1)S(1)} collective-permute-done((bf16[256,640]{1,0:T(8,128)(2,1)S(1)}, bf16[256,640]{1,0:T(8,128)(2,1)S(1)}, u32[]{:S(2)}, u32[]{:S(2)}) %collective-permute-start.25) | collective-permute-done | bytes 327712 | tf_op jit(solution)/shard_map/ppermute | solution.py:459
  114.8 1.5 collective-permute-start.35
  116.5 1.7 attention_grad.3.refs_6_.refs_3_
  118.3 1.8 collective-permute-start.32
  120.5 6.3 %collective-permute-done.32.refs_8_.refs_6_ = bf16[256,512]{1,0:T(8,128)(2,1)S(1)} collective-permute-done((bf16[256,512]{1,0:T(8,128)(2,1)S(1)}, bf16[256,512]{1,0:T(8,128)(2,1)S(1)}, u32[]{:S(2)}, u32[]{:S(2)}) %collective-permute-start.32) | collective-permute-done | bytes 262176 | tf_op jit(solution)/shard_map/ppermute | solution.py:359
  126.8 3.8 %collective-permute-done.31.refs_7_.refs_4_ = bf16[256,512]{1,0:T(8,128)(2,1)S(1)} collective-permute-done((bf16[256,512]{1,0:T(8,128)(2,1)S(1)}, bf16[256,512]{1,0:T(8,128)(2,1)S(1)}, u32[]{:S(2)}, u32[]{:S(2)}) %collective-permute-start.31) | collective-permute-done | bytes 262176 | tf_op jit(solution)/shard_map/ppermute | solution.py:359
  130.7 1.8 collective-permute-start.34
  132.8 1.8 attention_grad.4.refs_6_.refs_3_
  134.6 2.4 %collective-permute-done.34 = bf16[128,512]{1,0:T(8,128)(2,1)S(1)} collective-permute-done((bf16[128,512]{1,0:T(8,128)(2,1)S(1)}, bf16[128,512]{1,0:T(8,128)(2,1)S(1)}, u32[]{:S(2)}, u32[]{:S(2)}) %collective-permute-start.34) | collective-permute-done | bytes 131104 | tf_op jit(solution)/shard_map/ppermute | solution.py:359
  137.0 3.1 %collective-permute-done.33 = bf16[128,512]{1,0:T(8,128)(2,1)S(1)} collective-permute-done((bf16[128,512]{1,0:T(8,128)(2,1)S(1)}, bf16[128,512]{1,0:T(8,128)(2,1)S(1)}, u32[]{:S(2)}, u32[]{:S(2)}) %collective-permute-start.33) | collective-permute-done | bytes 131104 | tf_op jit(solution)/shard_map/ppermute | solution.py:359
  140.2 2.0 %collective-permute-start.36 = (bf16[256,512]{1,0:T(8,128)(2,1)S(1)}, bf16[256,512]{1,0:T(8,128)(2,1)S(1)}, u32[]{:S(2)}, u32[]{:S(2)}) collective-permute-start(bf16[256,512]{1,0:T(8,128)(2,1)S(1)} %attention_grad.4.refs_6_.refs_3_), channel_id=1, source_target_pairs={{0,4},{4,8},{8,12},{12,0},{1,5},{5,9},{9,13},{13,1},{2,6},{6,10},{... | collective-permute-start | bytes 786440 | tf_op jit(solution)/shard_map/ppermute | solution.py:359
  142.2 2.4 %fisher_rows.3 = (f32[1280,640]{1,0:T(8,128)}, bf16[1280,256]{1,0:T(8,128)(2,1)S(1)}) custom-call(bf16[4,128,1280]{2,1,0:T(8,128)(2,1)S(1)} %get-tuple-element.55.refs_5_.refs_0_, bf16[4,128,1280]{2,1,0:T(8,128)(2,1)S(1)} %get-tuple-element.60.refs_6_.refs_1_, bf16[4,256,1280]{2,1,0:T(8,128)(2,1)S(1)} %get-tuple-element.61.refs_2_, ...), custom_call_target="tpu_custom_call" | custom-call | tf_op jit(solution)/shard_map/fisher_rows/pallas_call | solution.py:205
  144.6 6.8 %collective-permute-done.37.refs_6_ = bf16[256,512]{1,0:T(8,128)(2,1)S(1)} collective-permute-done((bf16[256,512]{1,0:T(8,128)(2,1)S(1)}, bf16[256,512]{1,0:T(8,128)(2,1)S(1)}, u32[]{:S(2)}, u32[]{:S(2)}) %collective-permute-start.37) | collective-permute-done | bytes 262176 | tf_op jit(solution)/shard_map/ppermute | solution.py:359
  151.6 1.9 %collective-permute-start.40 = (bf16[128,512]{1,0:T(8,128)(2,1)S(1)}, bf16[128,512]{1,0:T(8,128)(2,1)S(1)}, u32[]{:S(2)}, u32[]{:S(2)}) collective-permute-start(bf16[128,512]{1,0:T(8,128)(2,1)S(1)} %slice.149), channel_id=1, source_target_pairs={{0,4},{4,8},{8,12},{12,0},{1,5},{5,9},{9,13},{13,1},{2,6},{6,10},{... | collective-permute-start | bytes 393224 | tf_op jit(solution)/shard_map/ppermute | solution.py:359
  153.9 2.8 %collective-permute-done.41 = bf16[128,512]{1,0:T(8,128)(2,1)S(1)} collective-permute-done((bf16[128,512]{1,0:T(8,128)(2,1)S(1)}, bf16[128,512]{1,0:T(8,128)(2,1)S(1)}, u32[]{:S(2)}, u32[]{:S(2)}) %collective-permute-start.41) | collective-permute-done | bytes 131104 | tf_op jit(solution)/shard_map/ppermute | solution.py:359
  156.7 1.7 collective-permute-done.40
  158.5 2.4 %fisher_rows.4 = (f32[1280,640]{1,0:T(8,128)}, bf16[1280,256]{1,0:T(8,128)(2,1)S(1)}) custom-call(bf16[4,128,1280]{2,1,0:T(8,128)(2,1)S(1)} %get-tuple-element.55.refs_5_.refs_0_, bf16[4,128,1280]{2,1,0:T(8,128)(2,1)S(1)} %get-tuple-element.60.refs_6_.refs_1_, bf16[4,256,1280]{2,1,0:T(8,128)(2,1)S(1)} %get-tuple-element.61.refs_2_, ...), custom_call_target="tpu_custom_call", output_to_operand_aliasing={{0}: (7, {})} | custom-call | tf_op jit(solution)/shard_map/fisher_rows/pallas_call | solution.py:205
  162.7 1.1 collective-permute-start.39
  164.8 2.9 %collective-permute-done.39.refs_6_ = bf16[128,512]{1,0:T(8,128)(2,1)S(1)} collective-permute-done((bf16[128,512]{1,0:T(8,128)(2,1)S(1)}, bf16[128,512]{1,0:T(8,128)(2,1)S(1)}, u32[]{:S(2)}, u32[]{:S(2)}) %collective-permute-start.39) | collective-permute-done | bytes 131104 | tf_op jit(solution)/shard_map/ppermute | solution.py:359
  167.8 3.6 %collective-permute-done.38.refs_4_ = bf16[128,512]{1,0:T(8,128)(2,1)S(1)} collective-permute-done((bf16[128,512]{1,0:T(8,128)(2,1)S(1)}, bf16[128,512]{1,0:T(8,128)(2,1)S(1)}, u32[]{:S(2)}, u32[]{:S(2)}) %collective-permute-start.38) | collective-permute-done | bytes 131104 | tf_op jit(solution)/shard_map/ppermute | solution.py:359
  171.5 2.0 %collective-permute-start.42 = (bf16[64,512]{1,0:T(8,128)(2,1)S(1)}, bf16[64,512]{1,0:T(8,128)(2,1)S(1)}, u32[]{:S(2)}, u32[]{:S(2)}) collective-permute-start(bf16[64,512]{1,0:T(8,128)(2,1)S(1)} %slice.151), channel_id=1, source_target_pairs={{0,4},{4,8},{8,12},{12,0},{1,5},{5,9},{9,13},{13,1},{2,6},{6,10},{... | collective-permute-start | bytes 196616 | tf_op jit(solution)/shard_map/ppermute | solution.py:359
  173.5 2.2 %collective-permute-done.43 = bf16[64,512]{1,0:T(8,128)(2,1)S(1)} collective-permute-done((bf16[64,512]{1,0:T(8,128)(2,1)S(1)}, bf16[64,512]{1,0:T(8,128)(2,1)S(1)}, u32[]{:S(2)}, u32[]{:S(2)}) %collective-permute-start.43) | collective-permute-done | bytes 65568 | tf_op jit(solution)/shard_map/ppermute | solution.py:359
  175.7 1.9 collective-permute-done.42
  177.6 1.6 fisher_rows.5
  179.3 1.6 collective-permute-start.44
  180.9 1.5 merge_rows.3.refs_4_
  182.5 1.6 merge_rows.4.refs_4_
  184.0 2.4 %collective-permute-done.44.refs_1_ = bf16[1280,128]{1,0:T(8,128)(2,1)S(1)} collective-permute-done((bf16[1280,128]{1,0:T(8,128)(2,1)S(1)}, bf16[1280,128]{1,0:T(8,128)(2,1)S(1)}, u32[]{:S(2)}, u32[]{:S(2)}) %collective-permute-start.44) | collective-permute-done | bytes 327712 | tf_op jit(solution)/shard_map/ppermute | solution.py:459
  186.4 1.2 merge_rows.5
  (153 shorter events, 16.5 us)
Async XLA Ops:
  0.6 21.6 %copy-start = (bf16[2,256,1280]{2,1,0:T(8,128)(2,1)S(1)}, bf16[2,256,1280]{2,1,0:T(8,128)(2,1)}, u32[]{:S(2)}) copy-start(bf16[2,256,1280]{2,1,0:T(8,128)(2,1)} %param.11) | copy-start | bytes 3932164
  0.7 1.4 copy-start.4
  2.1 8.1 %copy-start.11 = (bf16[128,2560]{1,0:T(8,128)(2,1)S(1)}, bf16[128,2560]{1,0:T(8,128)(2,1)}, u32[]{:S(2)}) copy-start(bf16[128,2560]{1,0:T(8,128)(2,1)} %param.14) | copy-start | bytes 1966084
  2.1 8.1 %copy-start.12 = (bf16[1,128,2560]{2,1,0:T(8,128)(2,1)S(1)}, bf16[1,128,2560]{2,1,0:T(8,128)(2,1)}, u32[]{:S(2)}) copy-start(bf16[1,128,2560]{2,1,0:T(8,128)(2,1)} %param.15) | copy-start | bytes 1966084
  3.3 10.7 %collective-permute-start = (bf16[64,1280]{1,0:T(8,128)(2,1)S(1)}, bf16[64,1280]{1,0:T(8,128)(2,1)S(1)}, u32[]{:S(2)}, u32[]{:S(2)}) collective-permute-start(bf16[64,1280]{1,0:T(8,128)(2,1)S(1)} %get-tuple-element.52), channel_id=1, source_target_pairs={{0,4},{4,8},{8,12},{12,0},{1,5},{5,9},{9,13},{13,1},{2,6},{6,10},{... | collective-permute-start | bytes 491528 | tf_op jit(solution)/shard_map/ppermute | solution.py:359
  6.3 13.4 %collective-permute-start.1 = (bf16[64,1280]{1,0:T(8,128)(2,1)S(1)}, bf16[64,1280]{1,0:T(8,128)(2,1)}, u32[]{:S(2)}, u32[]{:S(2)}) collective-permute-start(bf16[64,1280]{1,0:T(8,128)(2,1)S(1)} %get-tuple-element.53), channel_id=1, source_target_pairs={{0,8},{4,12},{8,0},{12,4},{1,9},{5,13},{9,1},{13,5},{2,10},{6,14},... | collective-permute-start | bytes 491528 | tf_op jit(solution)/shard_map/ppermute | solution.py:359
  8.9 10.9 %collective-permute-start.2 = (bf16[64,1280]{1,0:T(8,128)(2,1)S(1)}, bf16[64,1280]{1,0:T(8,128)(2,1)}, u32[]{:S(2)}, u32[]{:S(2)}) collective-permute-start(bf16[64,1280]{1,0:T(8,128)(2,1)S(1)} %get-tuple-element.54), channel_id=1, source_target_pairs={{0,12},{4,0},{8,4},{12,8},{1,13},{5,1},{9,5},{13,9},{2,14},{6,2},{... | collective-permute-start | bytes 491528 | tf_op jit(solution)/shard_map/ppermute | solution.py:359
  10.3 2.7 %copy-start.5 = (s32[4]{0:T(128)S(1)}, s32[4]{0:T(128)}, u32[]{:S(2)}) copy-start(s32[4]{0:T(128)} %param.10) | copy-start | bytes 52
  10.3 3.4 %copy-start.13 = (s32[3,512]{1,0:T(4,128)S(1)}, s32[3,512]{1,0:T(4,128)}, u32[]{:S(2)}) copy-start(s32[3,512]{1,0:T(4,128)} %param.9) | copy-start | bytes 18436
  11.4 22.8 %collective-permute-start.26 = (bf16[2,128,640]{2,1,0:T(8,128)(2,1)}, bf16[2,128,640]{2,1,0:T(8,128)(2,1)}, u32[]{:S(2)}, u32[]{:S(2)}) collective-permute-start(bf16[2,128,640]{2,1,0:T(8,128)(2,1)} %get-tuple-element.105), channel_id=1, source_target_pairs={{0,1},{1,0},{2,3},{3,2},{4,5},{5,4},{6,7},{7,6},{8,9},{9,8},{10,11... | collective-permute-start | bytes 983048 | tf_op jit(solution)/shard_map/ppermute | solution.py:462
  11.4 26.8 %collective-permute-start.27 = (bf16[2,128,640]{2,1,0:T(8,128)(2,1)}, bf16[2,128,640]{2,1,0:T(8,128)(2,1)}, u32[]{:S(2)}, u32[]{:S(2)}) collective-permute-start(bf16[2,128,640]{2,1,0:T(8,128)(2,1)} %get-tuple-element.106), channel_id=1, source_target_pairs={{0,2},{1,3},{2,0},{3,1},{4,6},{5,7},{6,4},{7,5},{8,10},{9,11},{10,... | collective-permute-start | bytes 983048 | tf_op jit(solution)/shard_map/ppermute | solution.py:462
  14.0 25.4 %collective-permute-start.28 = (bf16[2,128,640]{2,1,0:T(8,128)(2,1)}, bf16[2,128,640]{2,1,0:T(8,128)(2,1)}, u32[]{:S(2)}, u32[]{:S(2)}) collective-permute-start(bf16[2,128,640]{2,1,0:T(8,128)(2,1)} %get-tuple-element.107), channel_id=1, source_target_pairs={{0,3},{1,2},{2,1},{3,0},{4,7},{5,6},{6,5},{7,4},{8,11},{9,10},{10,... | collective-permute-start | bytes 983048 | tf_op jit(solution)/shard_map/ppermute | solution.py:462
  21.7 4.4 %copy-start.1 = (bf16[1,1280,640]{2,1,0:T(8,128)(2,1)S(1)}, bf16[1,1280,640]{2,1,0:T(8,128)(2,1)}, u32[]{:S(2)}) copy-start(bf16[1,1280,640]{2,1,0:T(8,128)(2,1)} %param.12) | copy-start | bytes 4915204
  21.7 2.4 %collective-permute-start.3 = (bf16[4,64,1280]{2,1,0:T(8,128)(2,1)}, bf16[4,64,1280]{2,1,0:T(8,128)(2,1)}, u32[]{:S(2)}, u32[]{:S(2)}) collective-permute-start(bf16[4,64,1280]{2,1,0:T(8,128)(2,1)} %pad_maximum_fusion.3.refs_0_), channel_id=1, source_target_pairs={{0,1},{1,0},{2,3},{3,2},{4,5},{5,4},{6,7},{7,6},{8,9},{9,8},{10,11... | collective-permute-start | bytes 1966088 | tf_op jit(solution)/shard_map/ppermute | solution.py:462
  22.6 22.0 %collective-permute-start.8 = (bf16[4,64,1280]{2,1,0:T(8,128)(2,1)}, bf16[4,64,1280]{2,1,0:T(8,128)(2,1)}, u32[]{:S(2)}, u32[]{:S(2)}) collective-permute-start(bf16[4,64,1280]{2,1,0:T(8,128)(2,1)} %pad_maximum_fusion.3.refs_0_), channel_id=1, source_target_pairs={{0,16},{16,0},{1,17},{17,1},{2,18},{18,2},{3,19},{19,3},{4,20},{20... | collective-permute-start | bytes 1966088 | tf_op jit(solution)/shard_map/ppermute | solution.py:459
  24.1 18.8 %collective-permute-start.4 = (bf16[4,64,1280]{2,1,0:T(8,128)(2,1)}, bf16[4,64,1280]{2,1,0:T(8,128)(2,1)}, u32[]{:S(2)}, u32[]{:S(2)}) collective-permute-start(bf16[4,64,1280]{2,1,0:T(8,128)(2,1)} %pad_maximum_fusion.3.refs_0_), channel_id=1, source_target_pairs={{0,2},{1,3},{2,0},{3,1},{4,6},{5,7},{6,4},{7,5},{8,10},{9,11},{10,... | collective-permute-start | bytes 1966088 | tf_op jit(solution)/shard_map/ppermute | solution.py:462
  29.2 1.4 copy-start.2
  30.6 8.8 %copy-start.8 = (bf16[2,128,640]{2,1,0:T(8,128)(2,1)S(1)}, bf16[2,128,640]{2,1,0:T(8,128)(2,1)}, u32[]{:S(2)}) copy-start(bf16[2,128,640]{2,1,0:T(8,128)(2,1)} %get-tuple-element.104) | copy-start | bytes 983044
  34.2 10.4 %collective-permute-start.5 = (bf16[128,640]{1,0:T(8,128)(2,1)S(1)}, bf16[128,640]{1,0:T(8,128)(2,1)S(1)}, u32[]{:S(2)}, u32[]{:S(2)}) collective-permute-start(bf16[128,640]{1,0:T(8,128)(2,1)S(1)} %get-tuple-element.57), channel_id=1, source_target_pairs={{0,4},{4,8},{8,12},{12,0},{1,5},{5,9},{9,13},{13,1},{2,6},{6,10},{... | collective-permute-start | bytes 491528 | tf_op jit(solution)/shard_map/ppermute | solution.py:359
  38.2 8.8 %collective-permute-start.6 = (bf16[128,640]{1,0:T(8,128)(2,1)S(1)}, bf16[128,640]{1,0:T(8,128)(2,1)S(1)}, u32[]{:S(2)}, u32[]{:S(2)}) collective-permute-start(bf16[128,640]{1,0:T(8,128)(2,1)S(1)} %get-tuple-element.58), channel_id=1, source_target_pairs={{0,12},{4,0},{8,4},{12,8},{1,13},{5,1},{9,5},{13,9},{2,14},{6,2},{... | collective-permute-start | bytes 491528 | tf_op jit(solution)/shard_map/ppermute | solution.py:359
  43.0 16.6 %collective-permute-start.10 = (bf16[4,64,1280]{2,1,0:T(8,128)(2,1)}, bf16[4,64,1280]{2,1,0:T(8,128)(2,1)S(1)}, u32[]{:S(2)}, u32[]{:S(2)}) collective-permute-start(bf16[4,64,1280]{2,1,0:T(8,128)(2,1)} %collective-permute-done.4.refs_0_), channel_id=1, source_target_pairs={{0,16},{16,0},{1,17},{17,1},{2,18},{18,2},{3,19},{19,3},{4,20},{20... | collective-permute-start | bytes 1966088 | tf_op jit(solution)/shard_map/ppermute | solution.py:459
  44.5 25.6 %collective-permute-start.9 = (bf16[4,64,1280]{2,1,0:T(8,128)(2,1)}, bf16[4,64,1280]{2,1,0:T(8,128)(2,1)S(1)}, u32[]{:S(2)}, u32[]{:S(2)}) collective-permute-start(bf16[4,64,1280]{2,1,0:T(8,128)(2,1)} %collective-permute-done.8.refs_0_), channel_id=1, source_target_pairs={{0,1},{1,0},{2,3},{3,2},{4,5},{5,4},{6,7},{7,6},{8,9},{9,8},{10,11... | collective-permute-start | bytes 1966088 | tf_op jit(solution)/shard_map/ppermute | solution.py:462
  47.1 19.3 %collective-permute-start.13 = (bf16[256,640]{1,0:T(8,128)(2,1)S(1)}, bf16[256,640]{1,0:T(8,128)(2,1)S(1)}, u32[]{:S(2)}, u32[]{:S(2)}) collective-permute-start(bf16[256,640]{1,0:T(8,128)(2,1)S(1)} %pad_maximum_fusion.7), channel_id=1, source_target_pairs={{0,12},{4,0},{8,4},{12,8},{1,13},{5,1},{9,5},{13,9},{2,14},{6,2},{... | collective-permute-start | bytes 983048 | tf_op jit(solution)/shard_map/ppermute | solution.py:359
  49.6 10.3 %collective-permute-start.7 = (bf16[4,64,1280]{2,1,0:T(8,128)(2,1)}, bf16[4,64,1280]{2,1,0:T(8,128)(2,1)S(1)}, u32[]{:S(2)}, u32[]{:S(2)}) collective-permute-start(bf16[4,64,1280]{2,1,0:T(8,128)(2,1)} %collective-permute-done.4.refs_0_), channel_id=1, source_target_pairs={{0,1},{1,0},{2,3},{3,2},{4,5},{5,4},{6,7},{7,6},{8,9},{9,8},{10,11... | collective-permute-start | bytes 1966088 | tf_op jit(solution)/shard_map/ppermute | solution.py:462
  49.7 18.7 %collective-permute-start.12 = (bf16[256,640]{1,0:T(8,128)(2,1)S(1)}, bf16[256,640]{1,0:T(8,128)(2,1)S(1)}, u32[]{:S(2)}, u32[]{:S(2)}) collective-permute-start(bf16[256,640]{1,0:T(8,128)(2,1)S(1)} %pad_maximum_fusion.6), channel_id=1, source_target_pairs={{0,4},{4,8},{8,12},{12,0},{1,5},{5,9},{9,13},{13,1},{2,6},{6,10},{... | collective-permute-start | bytes 983048 | tf_op jit(solution)/shard_map/ppermute | solution.py:359
  59.6 10.6 %collective-permute-start.11 = (bf16[4,64,1280]{2,1,0:T(8,128)(2,1)S(1)}, bf16[4,64,1280]{2,1,0:T(8,128)(2,1)S(1)}, u32[]{:S(2)}, u32[]{:S(2)}) collective-permute-start(bf16[4,64,1280]{2,1,0:T(8,128)(2,1)S(1)} %collective-permute-done.10.refs_2_), channel_id=1, source_target_pairs={{0,1},{1,0},{2,3},{3,2},{4,5},{5,4},{6,7},{7,6},{8,9},{9,8},{10,11... | collective-permute-start | bytes 1966088 | tf_op jit(solution)/shard_map/ppermute | solution.py:462
  59.7 1.4 copy-start.3
  64.5 4.0 %copy-start.10 = (bf16[1280,256]{1,0:T(8,128)(2,1)S(1)}, bf16[1280,256]{1,0:T(8,128)(2,1)}, u32[]{:S(2)}) copy-start(bf16[1280,256]{1,0:T(8,128)(2,1)} %slice.164) | copy-start | bytes 1966084
  64.5 9.0 %collective-permute-start.14 = (bf16[128,640]{1,0:T(8,128)(2,1)S(1)}, bf16[128,640]{1,0:T(8,128)(2,1)S(1)}, u32[]{:S(2)}, u32[]{:S(2)}) collective-permute-start(bf16[128,640]{1,0:T(8,128)(2,1)S(1)} %get-tuple-element.67), channel_id=1, source_target_pairs={{0,4},{4,8},{8,12},{12,0},{1,5},{5,9},{9,13},{13,1},{2,6},{6,10},{... | collective-permute-start | bytes 491528 | tf_op jit(solution)/shard_map/ppermute | solution.py:359
  66.5 10.0 %collective-permute-start.15 = (bf16[128,640]{1,0:T(8,128)(2,1)S(1)}, bf16[128,640]{1,0:T(8,128)(2,1)S(1)}, u32[]{:S(2)}, u32[]{:S(2)}) collective-permute-start(bf16[128,640]{1,0:T(8,128)(2,1)S(1)} %get-tuple-element.68), channel_id=1, source_target_pairs={{0,12},{4,0},{8,4},{12,8},{1,13},{5,1},{9,5},{13,9},{2,14},{6,2},{... | collective-permute-start | bytes 491528 | tf_op jit(solution)/shard_map/ppermute | solution.py:359
  68.5 5.0 %copy-start.6 = (f32[256,640]{1,0:T(8,128)}, f32[256,640]{1,0:T(8,128)S(1)}, u32[]{:S(2)}) copy-start(f32[256,640]{1,0:T(8,128)S(1)} %convert_add_fusion.1) | copy-start | bytes 1966084
  68.6 38.2 %collective-permute-start.22 = (bf16[1280,256]{1,0:T(8,128)(2,1)S(1)}, bf16[1280,256]{1,0:T(8,128)(2,1)S(1)}, u32[]{:S(2)}, u32[]{:S(2)}) collective-permute-start(bf16[1280,256]{1,0:T(8,128)(2,1)S(1)} %copy-done.10), channel_id=1, source_target_pairs={{0,16},{16,0},{1,17},{17,1},{2,18},{18,2},{3,19},{19,3},{4,20},{20... | collective-permute-start | bytes 1966088 | tf_op jit(solution)/shard_map/ppermute | solution.py:459
  76.6 7.9 %collective-permute-start.23 = (bf16[128,256]{1,0:T(8,128)(2,1)S(1)}, bf16[128,256]{1,0:T(8,128)(2,1)S(1)}, u32[]{:S(2)}, u32[]{:S(2)}) collective-permute-start(bf16[128,256]{1,0:T(8,128)(2,1)S(1)} %get-tuple-element.78), channel_id=1, source_target_pairs={{0,4},{4,8},{8,12},{12,0},{1,5},{5,9},{9,13},{13,1},{2,6},{6,10},{... | collective-permute-start | bytes 196616 | tf_op jit(solution)/shard_map/ppermute | solution.py:359
  77.3 7.3 %collective-permute-start.24 = (bf16[128,256]{1,0:T(8,128)(2,1)S(1)}, bf16[128,256]{1,0:T(8,128)(2,1)S(1)}, u32[]{:S(2)}, u32[]{:S(2)}) collective-permute-start(bf16[128,256]{1,0:T(8,128)(2,1)S(1)} %get-tuple-element.79), channel_id=1, source_target_pairs={{0,12},{4,0},{8,4},{12,8},{1,13},{5,1},{9,5},{13,9},{2,14},{6,2},{... | collective-permute-start | bytes 196616 | tf_op jit(solution)/shard_map/ppermute | solution.py:359
  80.5 27.8 %collective-permute-start.18 = (bf16[128,384]{1,0:T(8,128)(2,1)S(1)}, bf16[128,384]{1,0:T(8,128)(2,1)S(1)}, u32[]{:S(2)}, u32[]{:S(2)}) collective-permute-start(bf16[128,384]{1,0:T(8,128)(2,1)S(1)} %get-tuple-element.74), channel_id=1, source_target_pairs={{0,4},{4,8},{8,12},{12,0},{1,5},{5,9},{9,13},{13,1},{2,6},{6,10},{... | collective-permute-start | bytes 294920 | tf_op jit(solution)/shard_map/ppermute | solution.py:359
  80.6 7.1 %collective-permute-start.20 = (bf16[128,384]{1,0:T(8,128)(2,1)S(1)}, bf16[128,384]{1,0:T(8,128)(2,1)S(1)}, u32[]{:S(2)}, u32[]{:S(2)}) collective-permute-start(bf16[128,384]{1,0:T(8,128)(2,1)S(1)} %get-tuple-element.76), channel_id=1, source_target_pairs={{0,12},{4,0},{8,4},{12,8},{1,13},{5,1},{9,5},{13,9},{2,14},{6,2},{... | collective-permute-start | bytes 294920 | tf_op jit(solution)/shard_map/ppermute | solution.py:359
  84.5 11.8 %collective-permute-start.17 = (bf16[256,640]{1,0:T(8,128)(2,1)S(1)}, bf16[256,640]{1,0:T(8,128)(2,1)S(1)}, u32[]{:S(2)}, u32[]{:S(2)}) collective-permute-start(bf16[256,640]{1,0:T(8,128)(2,1)S(1)} %pad_maximum_fusion.9), channel_id=1, source_target_pairs={{0,12},{4,0},{8,4},{12,8},{1,13},{5,1},{9,5},{13,9},{2,14},{6,2},{... | collective-permute-start | bytes 983048 | tf_op jit(solution)/shard_map/ppermute | solution.py:359
  84.6 19.7 %collective-permute-start.16 = (bf16[256,640]{1,0:T(8,128)(2,1)S(1)}, bf16[256,640]{1,0:T(8,128)(2,1)S(1)}, u32[]{:S(2)}, u32[]{:S(2)}) collective-permute-start(bf16[256,640]{1,0:T(8,128)(2,1)S(1)} %pad_maximum_fusion.8), channel_id=1, source_target_pairs={{0,4},{4,8},{8,12},{12,0},{1,5},{5,9},{9,13},{13,1},{2,6},{6,10},{... | collective-permute-start | bytes 983048 | tf_op jit(solution)/shard_map/ppermute | solution.py:359
  87.7 28.6 %collective-permute-start.30 = (bf16[256,256]{1,0:T(8,128)(2,1)S(1)}, bf16[256,256]{1,0:T(8,128)(2,1)S(1)}, u32[]{:S(2)}, u32[]{:S(2)}) collective-permute-start(bf16[256,256]{1,0:T(8,128)(2,1)S(1)} %pad_maximum_fusion.15), channel_id=1, source_target_pairs={{0,12},{4,0},{8,4},{12,8},{1,13},{5,1},{9,5},{13,9},{2,14},{6,2},{... | collective-permute-start | bytes 393224 | tf_op jit(solution)/shard_map/ppermute | solution.py:359
  92.1 13.9 %slice-start = ((f32[256,640]{1,0:T(8,128)}), f32[128,640]{1,0:T(8,128)S(1)}, s32[]{:S(2)}) async-start(f32[256,640]{1,0:T(8,128)} %copy-done.6), calls=%async_computation | async-start | bytes 655360 | tf_op jit(solution)/shard_map/slice | solution.py:500
  96.3 20.1 %collective-permute-start.29 = (bf16[256,256]{1,0:T(8,128)(2,1)S(1)}, bf16[256,256]{1,0:T(8,128)(2,1)S(1)}, u32[]{:S(2)}, u32[]{:S(2)}) collective-permute-start(bf16[256,256]{1,0:T(8,128)(2,1)S(1)} %pad_maximum_fusion.14), channel_id=1, source_target_pairs={{0,4},{4,8},{8,12},{12,0},{1,5},{5,9},{9,13},{13,1},{2,6},{6,10},{... | collective-permute-start | bytes 393224 | tf_op jit(solution)/shard_map/ppermute | solution.py:359
  104.3 16.1 %collective-permute-start.21 = (bf16[256,384]{1,0:T(8,128)(2,1)S(1)}, bf16[256,384]{1,0:T(8,128)(2,1)S(1)}, u32[]{:S(2)}, u32[]{:S(2)}) collective-permute-start(bf16[256,384]{1,0:T(8,128)(2,1)S(1)} %pad_maximum_fusion.13), channel_id=1, source_target_pairs={{0,12},{4,0},{8,4},{12,8},{1,13},{5,1},{9,5},{13,9},{2,14},{6,2},{... | collective-permute-start | bytes 589832 | tf_op jit(solution)/shard_map/ppermute | solution.py:359
  106.0 8.8 %copy-start.9 = (bf16[1280,384]{1,0:T(8,128)(2,1)S(1)}, bf16[1280,384]{1,0:T(8,128)(2,1)}, u32[]{:S(2)}) copy-start(bf16[1280,384]{1,0:T(8,128)(2,1)} %slice.169) | copy-start | bytes 2949124
  106.8 8.0 %collective-permute-start.25 = (bf16[256,640]{1,0:T(8,128)(2,1)S(1)}, bf16[256,640]{1,0:T(8,128)(2,1)S(1)}, u32[]{:S(2)}, u32[]{:S(2)}) collective-permute-start(bf16[256,640]{1,0:T(8,128)(2,1)S(1)} %rotate_heads.1), channel_id=1, source_target_pairs={{0,16},{16,0},{1,17},{17,1},{2,18},{18,2},{3,19},{19,3},{4,20},{20... | collective-permute-start | bytes 983048 | tf_op jit(solution)/shard_map/ppermute | solution.py:459
  108.4 12.0 %collective-permute-start.19 = (bf16[256,384]{1,0:T(8,128)(2,1)S(1)}, bf16[256,384]{1,0:T(8,128)(2,1)S(1)}, u32[]{:S(2)}, u32[]{:S(2)}) collective-permute-start(bf16[256,384]{1,0:T(8,128)(2,1)S(1)} %pad_maximum_fusion.12), channel_id=1, source_target_pairs={{0,4},{4,8},{8,12},{12,0},{1,5},{5,9},{9,13},{13,1},{2,6},{6,10},{... | collective-permute-start | bytes 589832 | tf_op jit(solution)/shard_map/ppermute | solution.py:359
  114.8 25.3 %collective-permute-start.35 = (bf16[1280,384]{1,0:T(8,128)(2,1)S(1)}, bf16[1280,384]{1,0:T(8,128)(2,1)S(1)}, u32[]{:S(2)}, u32[]{:S(2)}) collective-permute-start(bf16[1280,384]{1,0:T(8,128)(2,1)S(1)} %copy-done.9), channel_id=1, source_target_pairs={{0,16},{16,0},{1,17},{17,1},{2,18},{18,2},{3,19},{19,3},{4,20},{20... | collective-permute-start | bytes 2949128 | tf_op jit(solution)/shard_map/ppermute | solution.py:459
  116.5 3.9 %copy-start.7 = (f32[256,640]{1,0:T(8,128)S(1)}, f32[256,640]{1,0:T(8,128)}, u32[]{:S(2)}) copy-start(f32[256,640]{1,0:T(8,128)} %copy-done.6) | copy-start | bytes 1966084
  118.3 8.5 %collective-permute-start.32 = (bf16[256,512]{1,0:T(8,128)(2,1)S(1)}, bf16[256,512]{1,0:T(8,128)(2,1)S(1)}, u32[]{:S(2)}, u32[]{:S(2)}) collective-permute-start(bf16[256,512]{1,0:T(8,128)(2,1)S(1)} %attention_grad.3.refs_6_.refs_3_), channel_id=1, source_target_pairs={{0,12},{4,0},{8,4},{12,8},{1,13},{5,1},{9,5},{13,9},{2,14},{6,2},{... | collective-permute-start | bytes 786440 | tf_op jit(solution)/shard_map/ppermute | solution.py:359
  120.1 10.6 %collective-permute-start.31 = (bf16[256,512]{1,0:T(8,128)(2,1)S(1)}, bf16[256,512]{1,0:T(8,128)(2,1)S(1)}, u32[]{:S(2)}, u32[]{:S(2)}) collective-permute-start(bf16[256,512]{1,0:T(8,128)(2,1)S(1)} %attention_grad.3.refs_6_.refs_3_), channel_id=1, source_target_pairs={{0,4},{4,8},{8,12},{12,0},{1,5},{5,9},{9,13},{13,1},{2,6},{6,10},{... | collective-permute-start | bytes 786440 | tf_op jit(solution)/shard_map/ppermute | solution.py:359
  130.7 6.3 %collective-permute-start.34 = (bf16[128,512]{1,0:T(8,128)(2,1)S(1)}, bf16[128,512]{1,0:T(8,128)(2,1)S(1)}, u32[]{:S(2)}, u32[]{:S(2)}) collective-permute-start(bf16[128,512]{1,0:T(8,128)(2,1)S(1)} %slice.147), channel_id=1, source_target_pairs={{0,12},{4,0},{8,4},{12,8},{1,13},{5,1},{9,5},{13,9},{2,14},{6,2},{... | collective-permute-start | bytes 393224 | tf_op jit(solution)/shard_map/ppermute | solution.py:359
  132.5 7.6 %collective-permute-start.33 = (bf16[128,512]{1,0:T(8,128)(2,1)S(1)}, bf16[128,512]{1,0:T(8,128)(2,1)S(1)}, u32[]{:S(2)}, u32[]{:S(2)}) collective-permute-start(bf16[128,512]{1,0:T(8,128)(2,1)S(1)} %slice.146), channel_id=1, source_target_pairs={{0,4},{4,8},{8,12},{12,0},{1,5},{5,9},{9,13},{13,1},{2,6},{6,10},{... | collective-permute-start | bytes 393224 | tf_op jit(solution)/shard_map/ppermute | solution.py:359
  140.1 11.2 %collective-permute-start.37 = (bf16[256,512]{1,0:T(8,128)(2,1)S(1)}, bf16[256,512]{1,0:T(8,128)(2,1)S(1)}, u32[]{:S(2)}, u32[]{:S(2)}) collective-permute-start(bf16[256,512]{1,0:T(8,128)(2,1)S(1)} %attention_grad.4.refs_6_.refs_3_), channel_id=1, source_target_pairs={{0,12},{4,0},{8,4},{12,8},{1,13},{5,1},{9,5},{13,9},{2,14},{6,2},{... | collective-permute-start | bytes 786440 | tf_op jit(solution)/shard_map/ppermute | solution.py:359
  140.2 11.2 %collective-permute-start.36 = (bf16[256,512]{1,0:T(8,128)(2,1)S(1)}, bf16[256,512]{1,0:T(8,128)(2,1)S(1)}, u32[]{:S(2)}, u32[]{:S(2)}) collective-permute-start(bf16[256,512]{1,0:T(8,128)(2,1)S(1)} %attention_grad.4.refs_6_.refs_3_), channel_id=1, source_target_pairs={{0,4},{4,8},{8,12},{12,0},{1,5},{5,9},{9,13},{13,1},{2,6},{6,10},{... | collective-permute-start | bytes 786440 | tf_op jit(solution)/shard_map/ppermute | solution.py:359
  151.4 5.4 %collective-permute-start.41 = (bf16[128,512]{1,0:T(8,128)(2,1)S(1)}, bf16[128,512]{1,0:T(8,128)(2,1)S(1)}, u32[]{:S(2)}, u32[]{:S(2)}) collective-permute-start(bf16[128,512]{1,0:T(8,128)(2,1)S(1)} %slice.150), channel_id=1, source_target_pairs={{0,12},{4,0},{8,4},{12,8},{1,13},{5,1},{9,5},{13,9},{2,14},{6,2},{... | collective-permute-start | bytes 393224 | tf_op jit(solution)/shard_map/ppermute | solution.py:359
  151.6 6.9 %collective-permute-start.40 = (bf16[128,512]{1,0:T(8,128)(2,1)S(1)}, bf16[128,512]{1,0:T(8,128)(2,1)S(1)}, u32[]{:S(2)}, u32[]{:S(2)}) collective-permute-start(bf16[128,512]{1,0:T(8,128)(2,1)S(1)} %slice.149), channel_id=1, source_target_pairs={{0,4},{4,8},{8,12},{12,0},{1,5},{5,9},{9,13},{13,1},{2,6},{6,10},{... | collective-permute-start | bytes 393224 | tf_op jit(solution)/shard_map/ppermute | solution.py:359
  153.4 27.4 %collective-permute-start.46 = (bf16[1280,256]{1,0:T(8,128)(2,1)S(1)}, bf16[1280,256]{1,0:T(8,128)(2,1)S(1)}, u32[]{:S(2)}, u32[]{:S(2)}) collective-permute-start(bf16[1280,256]{1,0:T(8,128)(2,1)S(1)} %get-tuple-element.89.refs_0_), channel_id=1, source_target_pairs={{0,16},{16,0},{1,17},{17,1},{2,18},{18,2},{3,19},{19,3},{4,20},{20... | collective-permute-start | bytes 1966088 | tf_op jit(solution)/shard_map/ppermute | solution.py:459
  160.9 21.6 %collective-permute-start.45 = (bf16[1280,256]{1,0:T(8,128)(2,1)S(1)}, bf16[1280,256]{1,0:T(8,128)(2,1)S(1)}, u32[]{:S(2)}, u32[]{:S(2)}) collective-permute-start(bf16[1280,256]{1,0:T(8,128)(2,1)S(1)} %get-tuple-element.93.refs_0_), channel_id=1, source_target_pairs={{0,16},{16,0},{1,17},{17,1},{2,18},{18,2},{3,19},{19,3},{4,20},{20... | collective-permute-start | bytes 1966088 | tf_op jit(solution)/shard_map/ppermute | solution.py:459
  162.7 5.0 %collective-permute-start.39 = (bf16[128,512]{1,0:T(8,128)(2,1)S(1)}, bf16[128,512]{1,0:T(8,128)(2,1)S(1)}, u32[]{:S(2)}, u32[]{:S(2)}) collective-permute-start(bf16[128,512]{1,0:T(8,128)(2,1)S(1)} %attention_grad.5.refs_3_), channel_id=1, source_target_pairs={{0,12},{4,0},{8,4},{12,8},{1,13},{5,1},{9,5},{13,9},{2,14},{6,2},{... | collective-permute-start | bytes 393224 | tf_op jit(solution)/shard_map/ppermute | solution.py:359
  163.9 7.5 %collective-permute-start.38 = (bf16[128,512]{1,0:T(8,128)(2,1)S(1)}, bf16[128,512]{1,0:T(8,128)(2,1)S(1)}, u32[]{:S(2)}, u32[]{:S(2)}) collective-permute-start(bf16[128,512]{1,0:T(8,128)(2,1)S(1)} %attention_grad.5.refs_3_), channel_id=1, source_target_pairs={{0,4},{4,8},{8,12},{12,0},{1,5},{5,9},{9,13},{13,1},{2,6},{6,10},{... | collective-permute-start | bytes 393224 | tf_op jit(solution)/shard_map/ppermute | solution.py:359
  171.4 4.3 %collective-permute-start.43 = (bf16[64,512]{1,0:T(8,128)(2,1)S(1)}, bf16[64,512]{1,0:T(8,128)(2,1)S(1)}, u32[]{:S(2)}, u32[]{:S(2)}) collective-permute-start(bf16[64,512]{1,0:T(8,128)(2,1)S(1)} %slice.152), channel_id=1, source_target_pairs={{0,12},{4,0},{8,4},{12,8},{1,13},{5,1},{9,5},{13,9},{2,14},{6,2},{... | collective-permute-start | bytes 196616 | tf_op jit(solution)/shard_map/ppermute | solution.py:359
  171.5 6.1 %collective-permute-start.42 = (bf16[64,512]{1,0:T(8,128)(2,1)S(1)}, bf16[64,512]{1,0:T(8,128)(2,1)S(1)}, u32[]{:S(2)}, u32[]{:S(2)}) collective-permute-start(bf16[64,512]{1,0:T(8,128)(2,1)S(1)} %slice.151), channel_id=1, source_target_pairs={{0,4},{4,8},{8,12},{12,0},{1,5},{5,9},{9,13},{13,1},{2,6},{6,10},{... | collective-permute-start | bytes 196616 | tf_op jit(solution)/shard_map/ppermute | solution.py:359
  179.3 7.1 %collective-permute-start.44 = (bf16[1280,128]{1,0:T(8,128)(2,1)S(1)}, bf16[1280,128]{1,0:T(8,128)(2,1)S(1)}, u32[]{:S(2)}, u32[]{:S(2)}) collective-permute-start(bf16[1280,128]{1,0:T(8,128)(2,1)S(1)} %get-tuple-element.98.refs_0_), channel_id=1, source_target_pairs={{0,16},{16,0},{1,17},{17,1},{2,18},{18,2},{3,19},{19,3},{4,20},{20... | collective-permute-start | bytes 983048 | tf_op jit(solution)/shard_map/ppermute | solution.py:459

commit v4 on v3

--- a/solution.py
+++ b/solution.py
@@ -487,6 +487,7 @@
     rows_y, [(terms_y, first_y)] = ring.project(
         both(near_y), modulation, weights, jobs, full, [rows_own]
     )
+    near_x, far, _ = behind(near_x, far, rows_y)
     rows_x, parts_x = ring.project(
         both(near_x) + both(far),
         modulation,

time: 188 us -> 184 us (0.979)
  waiting for transfers between devices: 81.5 us -> 77.2 us
    ppermute x8, waiting for transfers between devices: 18.1 us -> 14.8 us  [x_swap(): return lax.ppermute(block, 'member', [(i, i ^ 1) for i in range(members)])]
where the time goes in v4:
time: 184 us
  waiting for transfers between devices  77.2 us (42%)
  starting transfers between devices  63.4 us (34%)
  Pallas kernels  26.7 us (15%)
  other arithmetic  7.62 us (4%)
  local copies, waits for them, and re-layouts  7.47 us (4%)
    ppermute x31, waiting for transfers between devices, step(): return lax.ppermute(block, 'seq', pairs)  60.1 us
    ppermute x31, starting transfers between devices, step(): return lax.ppermute(block, 'seq', pairs)  48.5 us
    ppermute x8, waiting for transfers between devices, x_swap(): return lax.ppermute(block, 'member', [(i, i ^ 1) for i in range(members)])  14.8 us
    ppermute x8, starting transfers between devices, x_swap(): return lax.ppermute(block, 'member', [(i, i ^ 1) for i in range(members)])  10.8 us
    pallas_call x3, Pallas kernels, project_rows(): pl.pallas_call(functools.partial(project_kernel, len(pieces), jobs, cuts,...  9.11 us
    pallas_call x3, Pallas kernels, fisher_rows(): pl.pallas_call(kernel, in_specs=specs, out_specs=[pl.BlockSpec(memory_spa...  6.34 us
    pallas_call x3, Pallas kernels, attention_grad(): pl.pallas_call(drop(functools.partial(attention_kernel, own_first, first,...  4.51 us
    pallas_call x3, Pallas kernels, merge_rows(): pl.pallas_call(kernel, grid=(width // tile,), in_specs=specs, out_specs=p...  4.31 us
  transfers between devices with their start and end apart: 47, of which 22 were waited for; matrix products, arithmetic and copies ran while one was open for 6% of the time, Pallas kernels for 13%

profile of v4, /device:TPU:0, one launch (start us, length us, event | category | flops | bytes accessed | tf_op | source)
XLA Modules:
  0.0 184.1 jit_solution(4317803993903569439)
XLA Ops:
  0.7 1.4 copy-done.4
  2.1 1.7 spread_rows.1
  3.9 3.0 %collective-permute-start = (bf16[64,1280]{1,0:T(8,128)(2,1)}, bf16[64,1280]{1,0:T(8,128)(2,1)}, u32[]{:S(2)}, u32[]{:S(2)}) collective-permute-start(bf16[64,1280]{1,0:T(8,128)(2,1)} %get-tuple-element.54), channel_id=1, source_target_pairs={{0,4},{4,8},{8,12},{12,0},{1,5},{5,9},{9,13},{13,1},{2,6},{6,10},{... | collective-permute-start | bytes 491528 | tf_op jit(solution)/shard_map/ppermute | solution.py:359
  6.9 2.6 %collective-permute-start.1 = (bf16[64,1280]{1,0:T(8,128)(2,1)S(1)}, bf16[64,1280]{1,0:T(8,128)(2,1)}, u32[]{:S(2)}, u32[]{:S(2)}) collective-permute-start(bf16[64,1280]{1,0:T(8,128)(2,1)S(1)} %get-tuple-element.55), channel_id=1, source_target_pairs={{0,8},{4,12},{8,0},{12,4},{1,9},{5,13},{9,1},{13,5},{2,10},{6,14},... | collective-permute-start | bytes 491528 | tf_op jit(solution)/shard_map/ppermute | solution.py:359
  9.5 1.3 collective-permute-start.2
  10.8 1.1 fusion.2
  11.9 1.5 collective-permute-start.27
  15.5 5.1 %collective-permute-done.1 = bf16[64,1280]{1,0:T(8,128)(2,1)} collective-permute-done((bf16[64,1280]{1,0:T(8,128)(2,1)S(1)}, bf16[64,1280]{1,0:T(8,128)(2,1)}, u32[]{:S(2)}, u32[]{:S(2)}) %collective-permute-start.1) | collective-permute-done | bytes 163872 | tf_op jit(solution)/shard_map/ppermute | solution.py:359
  20.5 2.0 %pad_maximum_fusion.3.refs_0_ = bf16[4,64,1280]{2,1,0:T(8,128)(2,1)} fusion(bf16[1,64,1280]{2,1,0:T(8,128)(2,1)} %bitcast.5, bf16[1,64,1280]{2,1,0:T(8,128)(2,1)} %bitcast.4, bf16[1,64,1280]{2,1,0:T(8,128)(2,1)} %bitcast.3, bf16[1,64,1280]{2,1,0:T(8,128)(2,1)S(1)} %bitcast.42), kind=kLoop, calls=%fused_computation.15 | loop fusion | flops 983040 | bytes 1310720 | tf_op jit(solution)/shard_map/stack | solution.py:366
  22.8 1.6 collective-permute-start.4
  27.9 1.6 collective-permute-start.8
  29.5 1.4 copy-done.2
  30.9 3.5 %project_rows.3 = (bf16[4,128,1280]{2,1,0:T(8,128)(2,1)S(1)}, bf16[256,640]{1,0:T(8,128)(2,1)S(1)}, bf16[256,640]{1,0:T(8,128)(2,1)S(1)}, bf16[128,640]{1,0:T(8,...) custom-call(bf16[4,64,1280]{2,1,0:T(8,128)(2,1)} %pad_maximum_fusion.3.refs_0_, ...), custom_call_target="tpu_custom_call" | custom-call | tf_op jit(solution)/shard_map/project_rows/pallas_call | solution.py:325
  34.4 4.0 %collective-permute-start.5 = (bf16[128,640]{1,0:T(8,128)(2,1)S(1)}, bf16[128,640]{1,0:T(8,128)(2,1)S(1)}, u32[]{:S(2)}, u32[]{:S(2)}) collective-permute-start(bf16[128,640]{1,0:T(8,128)(2,1)S(1)} %get-tuple-element.59), channel_id=1, source_target_pairs={{0,4},{4,8},{8,12},{12,0},{1,5},{5,9},{9,13},{13,1},{2,6},{6,10},{... | collective-permute-start | bytes 491528 | tf_op jit(solution)/shard_map/ppermute | solution.py:359
  38.5 1.1 collective-permute-start.6
  39.6 1.4 pad_maximum_fusion
  41.1 2.3 %collective-permute-done.4.refs_0_ = bf16[4,64,1280]{2,1,0:T(8,128)(2,1)} collective-permute-done((bf16[4,64,1280]{2,1,0:T(8,128)(2,1)}, bf16[4,64,1280]{2,1,0:T(8,128)(2,1)}, u32[]{:S(2)}, u32[]{:S(2)}) %collective-permute-start.4) | collective-permute-done | bytes 655392 | tf_op jit(solution)/shard_map/ppermute | solution.py:462
  43.5 1.6 collective-permute-start.9
  45.0 2.3 %collective-permute-done.6 = bf16[128,640]{1,0:T(8,128)(2,1)S(1)} collective-permute-done((bf16[128,640]{1,0:T(8,128)(2,1)S(1)}, bf16[128,640]{1,0:T(8,128)(2,1)S(1)}, u32[]{:S(2)}, u32[]{:S(2)}) %collective-permute-start.6) | collective-permute-done | bytes 163872 | tf_op jit(solution)/shard_map/ppermute | solution.py:359
  47.5 2.5 %collective-permute-start.13 = (bf16[256,640]{1,0:T(8,128)(2,1)S(1)}, bf16[256,640]{1,0:T(8,128)(2,1)S(1)}, u32[]{:S(2)}, u32[]{:S(2)}) collective-permute-start(bf16[256,640]{1,0:T(8,128)(2,1)S(1)} %pad_maximum_fusion.7), channel_id=1, source_target_pairs={{0,12},{4,0},{8,4},{12,8},{1,13},{5,1},{9,5},{13,9},{2,14},{6,2},{... | collective-permute-start | bytes 983048 | tf_op jit(solution)/shard_map/ppermute | solution.py:359
  50.2 3.3 %project_rows.4 = (bf16[4,128,1280]{2,1,0:T(8,128)(2,1)S(1)}, bf16[256,640]{1,0:T(8,128)(2,1)S(1)}, bf16[256,640]{1,0:T(8,128)(2,1)S(1)}, bf16[128,640]{1,0:T(8,...) custom-call(bf16[4,64,1280]{2,1,0:T(8,128)(2,1)} %collective-permute-done.4.refs_0_, ...), custom_call_target="tpu_custom_call" | custom-call | tf_op jit(solution)/shard_map/project_rows/pallas_call | solution.py:325
  53.5 6.6 %collective-permute-done.9.refs_2_ = bf16[4,64,1280]{2,1,0:T(8,128)(2,1)S(1)} collective-permute-done((bf16[4,64,1280]{2,1,0:T(8,128)(2,1)}, bf16[4,64,1280]{2,1,0:T(8,128)(2,1)S(1)}, u32[]{:S(2)}, u32[]{:S(2)}) %collective-permute-start.9) | collective-permute-done | bytes 655392 | tf_op jit(solution)/shard_map/ppermute | solution.py:459
  60.9 3.0 %collective-permute-start.14 = (bf16[128,640]{1,0:T(8,128)(2,1)S(1)}, bf16[128,640]{1,0:T(8,128)(2,1)S(1)}, u32[]{:S(2)}, u32[]{:S(2)}) collective-permute-start(bf16[128,640]{1,0:T(8,128)(2,1)S(1)} %get-tuple-element.71), channel_id=1, source_target_pairs={{0,4},{4,8},{8,12},{12,0},{1,5},{5,9},{9,13},{13,1},{2,6},{6,10},{... | collective-permute-start | bytes 491528 | tf_op jit(solution)/shard_map/ppermute | solution.py:359
  63.9 1.3 collective-permute-start.15
  66.6 1.4 collective-permute-start.22
  68.0 2.3 %project_rows.5 = (bf16[4,256,1280]{2,1,0:T(8,128)(2,1)S(1)}, bf16[256,256]{1,0:T(8,128)(2,1)S(1)}, bf16[256,256]{1,0:T(8,128)(2,1)S(1)}, bf16[128,256]{1,0:T(8,...) custom-call(bf16[4,64,1280]{2,1,0:T(8,128)(2,1)S(1)} %collective-per, ...), custom_call_target="tpu_custom_call" | custom-call | tf_op jit(solution)/shard_map/project_rows/pallas_call | solution.py:325
  70.3 2.6 %collective-permute-done.15 = bf16[128,640]{1,0:T(8,128)(2,1)S(1)} collective-permute-done((bf16[128,640]{1,0:T(8,128)(2,1)S(1)}, bf16[128,640]{1,0:T(8,128)(2,1)S(1)}, u32[]{:S(2)}, u32[]{:S(2)}) %collective-permute-start.15) | collective-permute-done | bytes 163872 | tf_op jit(solution)/shard_map/ppermute | solution.py:359
  73.6 3.3 %collective-permute-start.24 = (bf16[128,256]{1,0:T(8,128)(2,1)S(1)}, bf16[128,256]{1,0:T(8,128)(2,1)S(1)}, u32[]{:S(2)}, u32[]{:S(2)}) collective-permute-start(bf16[128,256]{1,0:T(8,128)(2,1)S(1)} %get-tuple-element.83), channel_id=1, source_target_pairs={{0,12},{4,0},{8,4},{12,8},{1,13},{5,1},{9,5},{13,9},{2,14},{6,2},{... | collective-permute-start | bytes 196616 | tf_op jit(solution)/shard_map/ppermute | solution.py:359
  77.0 3.8 %collective-permute-start.20 = (bf16[128,384]{1,0:T(8,128)(2,1)S(1)}, bf16[128,384]{1,0:T(8,128)(2,1)S(1)}, u32[]{:S(2)}, u32[]{:S(2)}) collective-permute-start(bf16[128,384]{1,0:T(8,128)(2,1)S(1)} %get-tuple-element.80), channel_id=1, source_target_pairs={{0,12},{4,0},{8,4},{12,8},{1,13},{5,1},{9,5},{13,9},{2,14},{6,2},{... | collective-permute-start | bytes 294920 | tf_op jit(solution)/shard_map/ppermute | solution.py:359
  81.0 2.1 %collective-permute-start.16 = (bf16[256,640]{1,0:T(8,128)(2,1)S(1)}, bf16[256,640]{1,0:T(8,128)(2,1)S(1)}, u32[]{:S(2)}, u32[]{:S(2)}) collective-permute-start(bf16[256,640]{1,0:T(8,128)(2,1)S(1)} %pad_maximum_fusion.8), channel_id=1, source_target_pairs={{0,4},{4,8},{8,12},{12,0},{1,5},{5,9},{9,13},{13,1},{2,6},{6,10},{... | collective-permute-start | bytes 983048 | tf_op jit(solution)/shard_map/ppermute | solution.py:359
  84.1 4.4 %collective-permute-start.30 = (bf16[256,256]{1,0:T(8,128)(2,1)S(1)}, bf16[256,256]{1,0:T(8,128)(2,1)S(1)}, u32[]{:S(2)}, u32[]{:S(2)}) collective-permute-start(bf16[256,256]{1,0:T(8,128)(2,1)S(1)} %pad_maximum_fusion.15), channel_id=1, source_target_pairs={{0,12},{4,0},{8,4},{12,8},{1,13},{5,1},{9,5},{13,9},{2,14},{6,2},{... | collective-permute-start | bytes 393224 | tf_op jit(solution)/shard_map/ppermute | solution.py:359
  88.5 4.1 %collective-permute-done.17 = bf16[256,640]{1,0:T(8,128)(2,1)S(1)} collective-permute-done((bf16[256,640]{1,0:T(8,128)(2,1)S(1)}, bf16[256,640]{1,0:T(8,128)(2,1)S(1)}, u32[]{:S(2)}, u32[]{:S(2)}) %collective-permute-start.17) | collective-permute-done | bytes 327712 | tf_op jit(solution)/shard_map/ppermute | solution.py:359
  93.3 7.4 %collective-permute-done.16 = bf16[256,640]{1,0:T(8,128)(2,1)S(1)} collective-permute-done((bf16[256,640]{1,0:T(8,128)(2,1)S(1)}, bf16[256,640]{1,0:T(8,128)(2,1)S(1)}, u32[]{:S(2)}, u32[]{:S(2)}) %collective-permute-start.16) | collective-permute-done | bytes 327712 | tf_op jit(solution)/shard_map/ppermute | solution.py:359
  100.7 1.6 collective-permute-start.21
  103.2 1.6 collective-permute-start.25
  105.4 5.8 %collective-permute-done.25 = bf16[256,640]{1,0:T(8,128)(2,1)S(1)} collective-permute-done((bf16[256,640]{1,0:T(8,128)(2,1)S(1)}, bf16[256,640]{1,0:T(8,128)(2,1)S(1)}, u32[]{:S(2)}, u32[]{:S(2)}) %collective-permute-start.25) | collective-permute-done | bytes 327712 | tf_op jit(solution)/shard_map/ppermute | solution.py:459
  111.2 1.7 collective-permute-start.35
  113.2 1.7 attention_grad.3.refs_6_.refs_3_
  114.9 1.6 collective-permute-start.32
  117.1 6.5 %collective-permute-done.32.refs_8_.refs_6_ = bf16[256,512]{1,0:T(8,128)(2,1)S(1)} collective-permute-done((bf16[256,512]{1,0:T(8,128)(2,1)S(1)}, bf16[256,512]{1,0:T(8,128)(2,1)S(1)}, u32[]{:S(2)}, u32[]{:S(2)}) %collective-permute-start.32) | collective-permute-done | bytes 262176 | tf_op jit(solution)/shard_map/ppermute | solution.py:359
  123.6 3.6 %collective-permute-done.31.refs_7_.refs_4_ = bf16[256,512]{1,0:T(8,128)(2,1)S(1)} collective-permute-done((bf16[256,512]{1,0:T(8,128)(2,1)S(1)}, bf16[256,512]{1,0:T(8,128)(2,1)S(1)}, u32[]{:S(2)}, u32[]{:S(2)}) %collective-permute-start.31) | collective-permute-done | bytes 262176 | tf_op jit(solution)/shard_map/ppermute | solution.py:359
  127.2 1.8 collective-permute-start.34
  129.3 1.8 attention_grad.4.refs_6_.refs_3_
  131.1 2.4 %collective-permute-done.34 = bf16[128,512]{1,0:T(8,128)(2,1)S(1)} collective-permute-done((bf16[128,512]{1,0:T(8,128)(2,1)S(1)}, bf16[128,512]{1,0:T(8,128)(2,1)S(1)}, u32[]{:S(2)}, u32[]{:S(2)}) %collective-permute-start.34) | collective-permute-done | bytes 131104 | tf_op jit(solution)/shard_map/ppermute | solution.py:359
  133.5 3.1 %collective-permute-done.33 = bf16[128,512]{1,0:T(8,128)(2,1)S(1)} collective-permute-done((bf16[128,512]{1,0:T(8,128)(2,1)S(1)}, bf16[128,512]{1,0:T(8,128)(2,1)S(1)}, u32[]{:S(2)}, u32[]{:S(2)}) %collective-permute-start.33) | collective-permute-done | bytes 131104 | tf_op jit(solution)/shard_map/ppermute | solution.py:359
  136.6 2.0 %collective-permute-start.36 = (bf16[256,512]{1,0:T(8,128)(2,1)S(1)}, bf16[256,512]{1,0:T(8,128)(2,1)S(1)}, u32[]{:S(2)}, u32[]{:S(2)}) collective-permute-start(bf16[256,512]{1,0:T(8,128)(2,1)S(1)} %attention_grad.4.refs_6_.refs_3_), channel_id=1, source_target_pairs={{0,4},{4,8},{8,12},{12,0},{1,5},{5,9},{9,13},{13,1},{2,6},{6,10},{... | collective-permute-start | bytes 786440 | tf_op jit(solution)/shard_map/ppermute | solution.py:359
  138.7 2.4 %fisher_rows.3 = (f32[1280,640]{1,0:T(8,128)}, bf16[1280,256]{1,0:T(8,128)(2,1)S(1)}) custom-call(bf16[4,128,1280]{2,1,0:T(8,128)(2,1)S(1)} %get-tuple-element.57.refs_5_.refs_0_, bf16[4,128,1280]{2,1,0:T(8,128)(2,1)S(1)} %get-tuple-element.62.refs_6_.refs_1_, bf16[4,256,1280]{2,1,0:T(8,128)(2,1)S(1)} %get-tuple-element.65.refs_2_, ...), custom_call_target="tpu_custom_call" | custom-call | tf_op jit(solution)/shard_map/fisher_rows/pallas_call | solution.py:205
  141.0 6.7 %collective-permute-done.37.refs_6_ = bf16[256,512]{1,0:T(8,128)(2,1)S(1)} collective-permute-done((bf16[256,512]{1,0:T(8,128)(2,1)S(1)}, bf16[256,512]{1,0:T(8,128)(2,1)S(1)}, u32[]{:S(2)}, u32[]{:S(2)}) %collective-permute-start.37) | collective-permute-done | bytes 262176 | tf_op jit(solution)/shard_map/ppermute | solution.py:359
  148.0 1.8 collective-permute-start.40
  150.3 2.7 %collective-permute-done.41 = bf16[128,512]{1,0:T(8,128)(2,1)S(1)} collective-permute-done((bf16[128,512]{1,0:T(8,128)(2,1)S(1)}, bf16[128,512]{1,0:T(8,128)(2,1)S(1)}, u32[]{:S(2)}, u32[]{:S(2)}) %collective-permute-start.41) | collective-permute-done | bytes 131104 | tf_op jit(solution)/shard_map/ppermute | solution.py:359
  153.1 1.8 collective-permute-done.40
  154.9 2.4 %fisher_rows.4 = (f32[1280,640]{1,0:T(8,128)}, bf16[1280,256]{1,0:T(8,128)(2,1)S(1)}) custom-call(bf16[4,128,1280]{2,1,0:T(8,128)(2,1)S(1)} %get-tuple-element.57.refs_5_.refs_0_, bf16[4,128,1280]{2,1,0:T(8,128)(2,1)S(1)} %get-tuple-element.62.refs_6_.refs_1_, bf16[4,256,1280]{2,1,0:T(8,128)(2,1)S(1)} %get-tuple-element.65.refs_2_, ...), custom_call_target="tpu_custom_call", output_to_operand_aliasing={{0}: (7, {})} | custom-call | tf_op jit(solution)/shard_map/fisher_rows/pallas_call | solution.py:205
  159.2 1.2 collective-permute-start.39
  161.3 2.9 %collective-permute-done.39.refs_6_ = bf16[128,512]{1,0:T(8,128)(2,1)S(1)} collective-permute-done((bf16[128,512]{1,0:T(8,128)(2,1)S(1)}, bf16[128,512]{1,0:T(8,128)(2,1)S(1)}, u32[]{:S(2)}, u32[]{:S(2)}) %collective-permute-start.39) | collective-permute-done | bytes 131104 | tf_op jit(solution)/shard_map/ppermute | solution.py:359
  164.2 3.7 %collective-permute-done.38.refs_4_ = bf16[128,512]{1,0:T(8,128)(2,1)S(1)} collective-permute-done((bf16[128,512]{1,0:T(8,128)(2,1)S(1)}, bf16[128,512]{1,0:T(8,128)(2,1)S(1)}, u32[]{:S(2)}, u32[]{:S(2)}) %collective-permute-start.38) | collective-permute-done | bytes 131104 | tf_op jit(solution)/shard_map/ppermute | solution.py:359
  168.0 2.0 %collective-permute-start.42 = (bf16[64,512]{1,0:T(8,128)(2,1)S(1)}, bf16[64,512]{1,0:T(8,128)(2,1)S(1)}, u32[]{:S(2)}, u32[]{:S(2)}) collective-permute-start(bf16[64,512]{1,0:T(8,128)(2,1)S(1)} %slice.151), channel_id=1, source_target_pairs={{0,4},{4,8},{8,12},{12,0},{1,5},{5,9},{9,13},{13,1},{2,6},{6,10},{... | collective-permute-start | bytes 196616 | tf_op jit(solution)/shard_map/ppermute | solution.py:359
  170.0 2.2 %collective-permute-done.43 = bf16[64,512]{1,0:T(8,128)(2,1)S(1)} collective-permute-done((bf16[64,512]{1,0:T(8,128)(2,1)S(1)}, bf16[64,512]{1,0:T(8,128)(2,1)S(1)}, u32[]{:S(2)}, u32[]{:S(2)}) %collective-permute-start.43) | collective-permute-done | bytes 65568 | tf_op jit(solution)/shard_map/ppermute | solution.py:359
  172.2 1.9 %collective-permute-done.42 = bf16[64,512]{1,0:T(8,128)(2,1)S(1)} collective-permute-done((bf16[64,512]{1,0:T(8,128)(2,1)S(1)}, bf16[64,512]{1,0:T(8,128)(2,1)S(1)}, u32[]{:S(2)}, u32[]{:S(2)}) %collective-permute-start.42) | collective-permute-done | bytes 65568 | tf_op jit(solution)/shard_map/ppermute | solution.py:359
  174.1 1.6 fisher_rows.5
  175.7 1.7 collective-permute-start.44
  177.5 1.5 merge_rows.3.refs_4_
  179.0 1.6 merge_rows.4.refs_4_
  180.6 2.3 %collective-permute-done.44.refs_1_ = bf16[1280,128]{1,0:T(8,128)(2,1)S(1)} collective-permute-done((bf16[1280,128]{1,0:T(8,128)(2,1)S(1)}, bf16[1280,128]{1,0:T(8,128)(2,1)S(1)}, u32[]{:S(2)}, u32[]{:S(2)}) %collective-permute-start.44) | collective-permute-done | bytes 327712 | tf_op jit(solution)/shard_map/ppermute | solution.py:459
  182.9 1.2 merge_rows.5
  (153 shorter events, 17.4 us)
Async XLA Ops:
  0.6 13.9 %copy-start = (bf16[2,256,1280]{2,1,0:T(8,128)(2,1)S(1)}, bf16[2,256,1280]{2,1,0:T(8,128)(2,1)}, u32[]{:S(2)}) copy-start(bf16[2,256,1280]{2,1,0:T(8,128)(2,1)} %param.11) | copy-start | bytes 3932164
  0.7 1.4 copy-start.4
  2.1 8.7 %copy-start.11 = (bf16[128,2560]{1,0:T(8,128)(2,1)S(1)}, bf16[128,2560]{1,0:T(8,128)(2,1)}, u32[]{:S(2)}) copy-start(bf16[128,2560]{1,0:T(8,128)(2,1)} %param.14) | copy-start | bytes 1966084
  2.1 8.7 %copy-start.12 = (bf16[1,128,2560]{2,1,0:T(8,128)(2,1)S(1)}, bf16[1,128,2560]{2,1,0:T(8,128)(2,1)}, u32[]{:S(2)}) copy-start(bf16[1,128,2560]{2,1,0:T(8,128)(2,1)} %param.15) | copy-start | bytes 1966084
  3.9 11.2 %collective-permute-start = (bf16[64,1280]{1,0:T(8,128)(2,1)}, bf16[64,1280]{1,0:T(8,128)(2,1)}, u32[]{:S(2)}, u32[]{:S(2)}) collective-permute-start(bf16[64,1280]{1,0:T(8,128)(2,1)} %get-tuple-element.54), channel_id=1, source_target_pairs={{0,4},{4,8},{8,12},{12,0},{1,5},{5,9},{9,13},{13,1},{2,6},{6,10},{... | collective-permute-start | bytes 491528 | tf_op jit(solution)/shard_map/ppermute | solution.py:359
  6.9 13.7 %collective-permute-start.1 = (bf16[64,1280]{1,0:T(8,128)(2,1)S(1)}, bf16[64,1280]{1,0:T(8,128)(2,1)}, u32[]{:S(2)}, u32[]{:S(2)}) collective-permute-start(bf16[64,1280]{1,0:T(8,128)(2,1)S(1)} %get-tuple-element.55), channel_id=1, source_target_pairs={{0,8},{4,12},{8,0},{12,4},{1,9},{5,13},{9,1},{13,5},{2,10},{6,14},... | collective-permute-start | bytes 491528 | tf_op jit(solution)/shard_map/ppermute | solution.py:359
  9.5 11.1 %collective-permute-start.2 = (bf16[64,1280]{1,0:T(8,128)(2,1)S(1)}, bf16[64,1280]{1,0:T(8,128)(2,1)}, u32[]{:S(2)}, u32[]{:S(2)}) collective-permute-start(bf16[64,1280]{1,0:T(8,128)(2,1)S(1)} %get-tuple-element.56), channel_id=1, source_target_pairs={{0,12},{4,0},{8,4},{12,8},{1,13},{5,1},{9,5},{13,9},{2,14},{6,2},{... | collective-permute-start | bytes 491528 | tf_op jit(solution)/shard_map/ppermute | solution.py:359
  10.8 2.7 %copy-start.5 = (s32[4]{0:T(128)S(1)}, s32[4]{0:T(128)}, u32[]{:S(2)}) copy-start(s32[4]{0:T(128)} %param.10) | copy-start | bytes 52
  10.8 3.3 %copy-start.13 = (s32[3,512]{1,0:T(4,128)S(1)}, s32[3,512]{1,0:T(4,128)}, u32[]{:S(2)}) copy-start(s32[3,512]{1,0:T(4,128)} %param.9) | copy-start | bytes 18436
  11.9 22.5 %collective-permute-start.26 = (bf16[2,128,640]{2,1,0:T(8,128)(2,1)}, bf16[2,128,640]{2,1,0:T(8,128)(2,1)}, u32[]{:S(2)}, u32[]{:S(2)}) collective-permute-start(bf16[2,128,640]{2,1,0:T(8,128)(2,1)} %get-tuple-element.109), channel_id=1, source_target_pairs={{0,1},{1,0},{2,3},{3,2},{4,5},{5,4},{6,7},{7,6},{8,9},{9,8},{10,11... | collective-permute-start | bytes 983048 | tf_op jit(solution)/shard_map/ppermute | solution.py:462
  11.9 26.6 %collective-permute-start.27 = (bf16[2,128,640]{2,1,0:T(8,128)(2,1)}, bf16[2,128,640]{2,1,0:T(8,128)(2,1)}, u32[]{:S(2)}, u32[]{:S(2)}) collective-permute-start(bf16[2,128,640]{2,1,0:T(8,128)(2,1)} %get-tuple-element.110), channel_id=1, source_target_pairs={{0,2},{1,3},{2,0},{3,1},{4,6},{5,7},{6,4},{7,5},{8,10},{9,11},{10,... | collective-permute-start | bytes 983048 | tf_op jit(solution)/shard_map/ppermute | solution.py:462
  14.8 10.1 %copy-start.1 = (bf16[1,1280,640]{2,1,0:T(8,128)(2,1)S(1)}, bf16[1,1280,640]{2,1,0:T(8,128)(2,1)}, u32[]{:S(2)}) copy-start(bf16[1,1280,640]{2,1,0:T(8,128)(2,1)} %param.12) | copy-start | bytes 4915204
  15.1 24.6 %collective-permute-start.28 = (bf16[2,128,640]{2,1,0:T(8,128)(2,1)}, bf16[2,128,640]{2,1,0:T(8,128)(2,1)}, u32[]{:S(2)}, u32[]{:S(2)}) collective-permute-start(bf16[2,128,640]{2,1,0:T(8,128)(2,1)} %get-tuple-element.111), channel_id=1, source_target_pairs={{0,3},{1,2},{2,1},{3,0},{4,7},{5,6},{6,5},{7,4},{8,11},{9,10},{10,... | collective-permute-start | bytes 983048 | tf_op jit(solution)/shard_map/ppermute | solution.py:462
  22.5 5.4 %collective-permute-start.3 = (bf16[4,64,1280]{2,1,0:T(8,128)(2,1)}, bf16[4,64,1280]{2,1,0:T(8,128)(2,1)}, u32[]{:S(2)}, u32[]{:S(2)}) collective-permute-start(bf16[4,64,1280]{2,1,0:T(8,128)(2,1)} %pad_maximum_fusion.3.refs_0_), channel_id=1, source_target_pairs={{0,1},{1,0},{2,3},{3,2},{4,5},{5,4},{6,7},{7,6},{8,9},{9,8},{10,11... | collective-permute-start | bytes 1966088 | tf_op jit(solution)/shard_map/ppermute | solution.py:462
  22.8 20.6 %collective-permute-start.4 = (bf16[4,64,1280]{2,1,0:T(8,128)(2,1)}, bf16[4,64,1280]{2,1,0:T(8,128)(2,1)}, u32[]{:S(2)}, u32[]{:S(2)}) collective-permute-start(bf16[4,64,1280]{2,1,0:T(8,128)(2,1)} %pad_maximum_fusion.3.refs_0_), channel_id=1, source_target_pairs={{0,2},{1,3},{2,0},{3,1},{4,6},{5,7},{6,4},{7,5},{8,10},{9,11},{10,... | collective-permute-start | bytes 1966088 | tf_op jit(solution)/shard_map/ppermute | solution.py:462
  26.8 12.8 %copy-start.8 = (bf16[2,128,640]{2,1,0:T(8,128)(2,1)S(1)}, bf16[2,128,640]{2,1,0:T(8,128)(2,1)}, u32[]{:S(2)}) copy-start(bf16[2,128,640]{2,1,0:T(8,128)(2,1)} %get-tuple-element.108) | copy-start | bytes 983044
  27.9 25.6 %collective-permute-start.8 = (bf16[4,64,1280]{2,1,0:T(8,128)(2,1)}, bf16[4,64,1280]{2,1,0:T(8,128)(2,1)S(1)}, u32[]{:S(2)}, u32[]{:S(2)}) collective-permute-start(bf16[4,64,1280]{2,1,0:T(8,128)(2,1)} %pad_maximum_fusion.3.refs_0_), channel_id=1, source_target_pairs={{0,16},{16,0},{1,17},{17,1},{2,18},{18,2},{3,19},{19,3},{4,20},{20... | collective-permute-start | bytes 1966088 | tf_op jit(solution)/shard_map/ppermute | solution.py:459
  29.5 1.4 copy-start.2
  34.4 10.6 %collective-permute-start.5 = (bf16[128,640]{1,0:T(8,128)(2,1)S(1)}, bf16[128,640]{1,0:T(8,128)(2,1)S(1)}, u32[]{:S(2)}, u32[]{:S(2)}) collective-permute-start(bf16[128,640]{1,0:T(8,128)(2,1)S(1)} %get-tuple-element.59), channel_id=1, source_target_pairs={{0,4},{4,8},{8,12},{12,0},{1,5},{5,9},{9,13},{13,1},{2,6},{6,10},{... | collective-permute-start | bytes 491528 | tf_op jit(solution)/shard_map/ppermute | solution.py:359
  38.5 8.9 %collective-permute-start.6 = (bf16[128,640]{1,0:T(8,128)(2,1)S(1)}, bf16[128,640]{1,0:T(8,128)(2,1)S(1)}, u32[]{:S(2)}, u32[]{:S(2)}) collective-permute-start(bf16[128,640]{1,0:T(8,128)(2,1)S(1)} %get-tuple-element.60), channel_id=1, source_target_pairs={{0,12},{4,0},{8,4},{12,8},{1,13},{5,1},{9,5},{13,9},{2,14},{6,2},{... | collective-permute-start | bytes 491528 | tf_op jit(solution)/shard_map/ppermute | solution.py:359
  43.4 6.7 %copy-start.3 = (bf16[1280,640]{1,0:T(8,128)(2,1)S(1)}, bf16[1280,640]{1,0:T(8,128)(2,1)}, u32[]{:S(2)}) copy-start(bf16[1280,640]{1,0:T(8,128)(2,1)} %refs_4_.3) | copy-start | bytes 4915204
  43.5 16.6 %collective-permute-start.9 = (bf16[4,64,1280]{2,1,0:T(8,128)(2,1)}, bf16[4,64,1280]{2,1,0:T(8,128)(2,1)S(1)}, u32[]{:S(2)}, u32[]{:S(2)}) collective-permute-start(bf16[4,64,1280]{2,1,0:T(8,128)(2,1)} %collective-permute-done.4.refs_0_), channel_id=1, source_target_pairs={{0,16},{16,0},{1,17},{17,1},{2,18},{18,2},{3,19},{19,3},{4,20},{20... | collective-permute-start | bytes 1966088 | tf_op jit(solution)/shard_map/ppermute | solution.py:459
  47.4 2.8 %collective-permute-start.7 = (bf16[4,64,1280]{2,1,0:T(8,128)(2,1)}, bf16[4,64,1280]{2,1,0:T(8,128)(2,1)S(1)}, u32[]{:S(2)}, u32[]{:S(2)}) collective-permute-start(bf16[4,64,1280]{2,1,0:T(8,128)(2,1)} %collective-permute-done.4.refs_0_), channel_id=1, source_target_pairs={{0,1},{1,0},{2,3},{3,2},{4,5},{5,4},{6,7},{7,6},{8,9},{9,8},{10,11... | collective-permute-start | bytes 1966088 | tf_op jit(solution)/shard_map/ppermute | solution.py:462
  47.5 16.4 %collective-permute-start.13 = (bf16[256,640]{1,0:T(8,128)(2,1)S(1)}, bf16[256,640]{1,0:T(8,128)(2,1)S(1)}, u32[]{:S(2)}, u32[]{:S(2)}) collective-permute-start(bf16[256,640]{1,0:T(8,128)(2,1)S(1)} %pad_maximum_fusion.7), channel_id=1, source_target_pairs={{0,12},{4,0},{8,4},{12,8},{1,13},{5,1},{9,5},{13,9},{2,14},{6,2},{... | collective-permute-start | bytes 983048 | tf_op jit(solution)/shard_map/ppermute | solution.py:359
  50.1 15.3 %collective-permute-start.12 = (bf16[256,640]{1,0:T(8,128)(2,1)S(1)}, bf16[256,640]{1,0:T(8,128)(2,1)S(1)}, u32[]{:S(2)}, u32[]{:S(2)}) collective-permute-start(bf16[256,640]{1,0:T(8,128)(2,1)S(1)} %pad_maximum_fusion.6), channel_id=1, source_target_pairs={{0,4},{4,8},{8,12},{12,0},{1,5},{5,9},{9,13},{13,1},{2,6},{6,10},{... | collective-permute-start | bytes 983048 | tf_op jit(solution)/shard_map/ppermute | solution.py:359
  60.1 7.9 %collective-permute-start.10 = (bf16[4,64,1280]{2,1,0:T(8,128)(2,1)S(1)}, bf16[4,64,1280]{2,1,0:T(8,128)(2,1)S(1)}, u32[]{:S(2)}, u32[]{:S(2)}) collective-permute-start(bf16[4,64,1280]{2,1,0:T(8,128)(2,1)S(1)} %collective-permute-done.8.refs_0_), channel_id=1, source_target_pairs={{0,1},{1,0},{2,3},{3,2},{4,5},{5,4},{6,7},{7,6},{8,9},{9,8},{10,11... | collective-permute-start | bytes 1966088 | tf_op jit(solution)/shard_map/ppermute | solution.py:462
  60.1 7.9 %collective-permute-start.11 = (bf16[4,64,1280]{2,1,0:T(8,128)(2,1)S(1)}, bf16[4,64,1280]{2,1,0:T(8,128)(2,1)S(1)}, u32[]{:S(2)}, u32[]{:S(2)}) collective-permute-start(bf16[4,64,1280]{2,1,0:T(8,128)(2,1)S(1)} %collective-permute-done.9.refs_2_), channel_id=1, source_target_pairs={{0,1},{1,0},{2,3},{3,2},{4,5},{5,4},{6,7},{7,6},{8,9},{9,8},{10,11... | collective-permute-start | bytes 1966088 | tf_op jit(solution)/shard_map/ppermute | solution.py:462
  60.9 9.4 %collective-permute-start.14 = (bf16[128,640]{1,0:T(8,128)(2,1)S(1)}, bf16[128,640]{1,0:T(8,128)(2,1)S(1)}, u32[]{:S(2)}, u32[]{:S(2)}) collective-permute-start(bf16[128,640]{1,0:T(8,128)(2,1)S(1)} %get-tuple-element.71), channel_id=1, source_target_pairs={{0,4},{4,8},{8,12},{12,0},{1,5},{5,9},{9,13},{13,1},{2,6},{6,10},{... | collective-permute-start | bytes 491528 | tf_op jit(solution)/shard_map/ppermute | solution.py:359
  63.9 8.9 %collective-permute-start.15 = (bf16[128,640]{1,0:T(8,128)(2,1)S(1)}, bf16[128,640]{1,0:T(8,128)(2,1)S(1)}, u32[]{:S(2)}, u32[]{:S(2)}) collective-permute-start(bf16[128,640]{1,0:T(8,128)(2,1)S(1)} %get-tuple-element.72), channel_id=1, source_target_pairs={{0,12},{4,0},{8,4},{12,8},{1,13},{5,1},{9,5},{13,9},{2,14},{6,2},{... | collective-permute-start | bytes 491528 | tf_op jit(solution)/shard_map/ppermute | solution.py:359
  65.4 1.3 copy-start.10
  65.5 4.8 %copy-start.6 = (f32[256,640]{1,0:T(8,128)}, f32[256,640]{1,0:T(8,128)S(1)}, u32[]{:S(2)}) copy-start(f32[256,640]{1,0:T(8,128)S(1)} %convert_add_fusion.1) | copy-start | bytes 1966084
  66.6 36.6 %collective-permute-start.22 = (bf16[1280,256]{1,0:T(8,128)(2,1)S(1)}, bf16[1280,256]{1,0:T(8,128)(2,1)S(1)}, u32[]{:S(2)}, u32[]{:S(2)}) collective-permute-start(bf16[1280,256]{1,0:T(8,128)(2,1)S(1)} %copy-done.10), channel_id=1, source_target_pairs={{0,16},{16,0},{1,17},{17,1},{2,18},{18,2},{3,19},{19,3},{4,20},{20... | collective-permute-start | bytes 1966088 | tf_op jit(solution)/shard_map/ppermute | solution.py:459
  73.0 7.9 %collective-permute-start.23 = (bf16[128,256]{1,0:T(8,128)(2,1)S(1)}, bf16[128,256]{1,0:T(8,128)(2,1)S(1)}, u32[]{:S(2)}, u32[]{:S(2)}) collective-permute-start(bf16[128,256]{1,0:T(8,128)(2,1)S(1)} %get-tuple-element.82), channel_id=1, source_target_pairs={{0,4},{4,8},{8,12},{12,0},{1,5},{5,9},{9,13},{13,1},{2,6},{6,10},{... | collective-permute-start | bytes 196616 | tf_op jit(solution)/shard_map/ppermute | solution.py:359
  73.6 7.4 %collective-permute-start.24 = (bf16[128,256]{1,0:T(8,128)(2,1)S(1)}, bf16[128,256]{1,0:T(8,128)(2,1)S(1)}, u32[]{:S(2)}, u32[]{:S(2)}) collective-permute-start(bf16[128,256]{1,0:T(8,128)(2,1)S(1)} %get-tuple-element.83), channel_id=1, source_target_pairs={{0,12},{4,0},{8,4},{12,8},{1,13},{5,1},{9,5},{13,9},{2,14},{6,2},{... | collective-permute-start | bytes 196616 | tf_op jit(solution)/shard_map/ppermute | solution.py:359
  76.9 27.9 %collective-permute-start.18 = (bf16[128,384]{1,0:T(8,128)(2,1)S(1)}, bf16[128,384]{1,0:T(8,128)(2,1)S(1)}, u32[]{:S(2)}, u32[]{:S(2)}) collective-permute-start(bf16[128,384]{1,0:T(8,128)(2,1)S(1)} %get-tuple-element.78), channel_id=1, source_target_pairs={{0,4},{4,8},{8,12},{12,0},{1,5},{5,9},{9,13},{13,1},{2,6},{6,10},{... | collective-permute-start | bytes 294920 | tf_op jit(solution)/shard_map/ppermute | solution.py:359
  77.0 7.1 %collective-permute-start.20 = (bf16[128,384]{1,0:T(8,128)(2,1)S(1)}, bf16[128,384]{1,0:T(8,128)(2,1)S(1)}, u32[]{:S(2)}, u32[]{:S(2)}) collective-permute-start(bf16[128,384]{1,0:T(8,128)(2,1)S(1)} %get-tuple-element.80), channel_id=1, source_target_pairs={{0,12},{4,0},{8,4},{12,8},{1,13},{5,1},{9,5},{13,9},{2,14},{6,2},{... | collective-permute-start | bytes 294920 | tf_op jit(solution)/shard_map/ppermute | solution.py:359
  80.9 11.7 %collective-permute-start.17 = (bf16[256,640]{1,0:T(8,128)(2,1)S(1)}, bf16[256,640]{1,0:T(8,128)(2,1)S(1)}, u32[]{:S(2)}, u32[]{:S(2)}) collective-permute-start(bf16[256,640]{1,0:T(8,128)(2,1)S(1)} %pad_maximum_fusion.9), channel_id=1, source_target_pairs={{0,12},{4,0},{8,4},{12,8},{1,13},{5,1},{9,5},{13,9},{2,14},{6,2},{... | collective-permute-start | bytes 983048 | tf_op jit(solution)/shard_map/ppermute | solution.py:359
  81.0 19.7 %collective-permute-start.16 = (bf16[256,640]{1,0:T(8,128)(2,1)S(1)}, bf16[256,640]{1,0:T(8,128)(2,1)S(1)}, u32[]{:S(2)}, u32[]{:S(2)}) collective-permute-start(bf16[256,640]{1,0:T(8,128)(2,1)S(1)} %pad_maximum_fusion.8), channel_id=1, source_target_pairs={{0,4},{4,8},{8,12},{12,0},{1,5},{5,9},{9,13},{13,1},{2,6},{6,10},{... | collective-permute-start | bytes 983048 | tf_op jit(solution)/shard_map/ppermute | solution.py:359
  84.1 28.9 %collective-permute-start.30 = (bf16[256,256]{1,0:T(8,128)(2,1)S(1)}, bf16[256,256]{1,0:T(8,128)(2,1)S(1)}, u32[]{:S(2)}, u32[]{:S(2)}) collective-permute-start(bf16[256,256]{1,0:T(8,128)(2,1)S(1)} %pad_maximum_fusion.15), channel_id=1, source_target_pairs={{0,12},{4,0},{8,4},{12,8},{1,13},{5,1},{9,5},{13,9},{2,14},{6,2},{... | collective-permute-start | bytes 393224 | tf_op jit(solution)/shard_map/ppermute | solution.py:359
  88.5 13.9 %slice-start = ((f32[256,640]{1,0:T(8,128)}), f32[128,640]{1,0:T(8,128)S(1)}, s32[]{:S(2)}) async-start(f32[256,640]{1,0:T(8,128)} %copy-done.6), calls=%async_computation | async-start | bytes 655360 | tf_op jit(solution)/shard_map/slice | solution.py:501
  92.6 20.3 %collective-permute-start.29 = (bf16[256,256]{1,0:T(8,128)(2,1)S(1)}, bf16[256,256]{1,0:T(8,128)(2,1)S(1)}, u32[]{:S(2)}, u32[]{:S(2)}) collective-permute-start(bf16[256,256]{1,0:T(8,128)(2,1)S(1)} %pad_maximum_fusion.14), channel_id=1, source_target_pairs={{0,4},{4,8},{8,12},{12,0},{1,5},{5,9},{9,13},{13,1},{2,6},{6,10},{... | collective-permute-start | bytes 393224 | tf_op jit(solution)/shard_map/ppermute | solution.py:359
  100.7 16.3 %collective-permute-start.21 = (bf16[256,384]{1,0:T(8,128)(2,1)S(1)}, bf16[256,384]{1,0:T(8,128)(2,1)S(1)}, u32[]{:S(2)}, u32[]{:S(2)}) collective-permute-start(bf16[256,384]{1,0:T(8,128)(2,1)S(1)} %pad_maximum_fusion.13), channel_id=1, source_target_pairs={{0,12},{4,0},{8,4},{12,8},{1,13},{5,1},{9,5},{13,9},{2,14},{6,2},{... | collective-permute-start | bytes 589832 | tf_op jit(solution)/shard_map/ppermute | solution.py:359
  102.4 8.8 %copy-start.9 = (bf16[1280,384]{1,0:T(8,128)(2,1)S(1)}, bf16[1280,384]{1,0:T(8,128)(2,1)}, u32[]{:S(2)}) copy-start(bf16[1280,384]{1,0:T(8,128)(2,1)} %slice.169) | copy-start | bytes 2949124
  103.2 8.0 %collective-permute-start.25 = (bf16[256,640]{1,0:T(8,128)(2,1)S(1)}, bf16[256,640]{1,0:T(8,128)(2,1)S(1)}, u32[]{:S(2)}, u32[]{:S(2)}) collective-permute-start(bf16[256,640]{1,0:T(8,128)(2,1)S(1)} %rotate_heads.1), channel_id=1, source_target_pairs={{0,16},{16,0},{1,17},{17,1},{2,18},{18,2},{3,19},{19,3},{4,20},{20... | collective-permute-start | bytes 983048 | tf_op jit(solution)/shard_map/ppermute | solution.py:459
  104.9 12.2 %collective-permute-start.19 = (bf16[256,384]{1,0:T(8,128)(2,1)S(1)}, bf16[256,384]{1,0:T(8,128)(2,1)S(1)}, u32[]{:S(2)}, u32[]{:S(2)}) collective-permute-start(bf16[256,384]{1,0:T(8,128)(2,1)S(1)} %pad_maximum_fusion.12), channel_id=1, source_target_pairs={{0,4},{4,8},{8,12},{12,0},{1,5},{5,9},{9,13},{13,1},{2,6},{6,10},{... | collective-permute-start | bytes 589832 | tf_op jit(solution)/shard_map/ppermute | solution.py:359
  111.2 25.4 %collective-permute-start.35 = (bf16[1280,384]{1,0:T(8,128)(2,1)S(1)}, bf16[1280,384]{1,0:T(8,128)(2,1)S(1)}, u32[]{:S(2)}, u32[]{:S(2)}) collective-permute-start(bf16[1280,384]{1,0:T(8,128)(2,1)S(1)} %copy-done.9), channel_id=1, source_target_pairs={{0,16},{16,0},{1,17},{17,1},{2,18},{18,2},{3,19},{19,3},{4,20},{20... | collective-permute-start | bytes 2949128 | tf_op jit(solution)/shard_map/ppermute | solution.py:459
  113.1 3.8 %copy-start.7 = (f32[256,640]{1,0:T(8,128)S(1)}, f32[256,640]{1,0:T(8,128)}, u32[]{:S(2)}) copy-start(f32[256,640]{1,0:T(8,128)} %copy-done.6) | copy-start | bytes 1966084
  114.9 8.7 %collective-permute-start.32 = (bf16[256,512]{1,0:T(8,128)(2,1)S(1)}, bf16[256,512]{1,0:T(8,128)(2,1)S(1)}, u32[]{:S(2)}, u32[]{:S(2)}) collective-permute-start(bf16[256,512]{1,0:T(8,128)(2,1)S(1)} %attention_grad.3.refs_6_.refs_3_), channel_id=1, source_target_pairs={{0,12},{4,0},{8,4},{12,8},{1,13},{5,1},{9,5},{13,9},{2,14},{6,2},{... | collective-permute-start | bytes 786440 | tf_op jit(solution)/shard_map/ppermute | solution.py:359
  116.5 10.6 %collective-permute-start.31 = (bf16[256,512]{1,0:T(8,128)(2,1)S(1)}, bf16[256,512]{1,0:T(8,128)(2,1)S(1)}, u32[]{:S(2)}, u32[]{:S(2)}) collective-permute-start(bf16[256,512]{1,0:T(8,128)(2,1)S(1)} %attention_grad.3.refs_6_.refs_3_), channel_id=1, source_target_pairs={{0,4},{4,8},{8,12},{12,0},{1,5},{5,9},{9,13},{13,1},{2,6},{6,10},{... | collective-permute-start | bytes 786440 | tf_op jit(solution)/shard_map/ppermute | solution.py:359
  127.2 6.3 %collective-permute-start.34 = (bf16[128,512]{1,0:T(8,128)(2,1)S(1)}, bf16[128,512]{1,0:T(8,128)(2,1)S(1)}, u32[]{:S(2)}, u32[]{:S(2)}) collective-permute-start(bf16[128,512]{1,0:T(8,128)(2,1)S(1)} %slice.147), channel_id=1, source_target_pairs={{0,12},{4,0},{8,4},{12,8},{1,13},{5,1},{9,5},{13,9},{2,14},{6,2},{... | collective-permute-start | bytes 393224 | tf_op jit(solution)/shard_map/ppermute | solution.py:359
  129.0 7.6 %collective-permute-start.33 = (bf16[128,512]{1,0:T(8,128)(2,1)S(1)}, bf16[128,512]{1,0:T(8,128)(2,1)S(1)}, u32[]{:S(2)}, u32[]{:S(2)}) collective-permute-start(bf16[128,512]{1,0:T(8,128)(2,1)S(1)} %slice.146), channel_id=1, source_target_pairs={{0,4},{4,8},{8,12},{12,0},{1,5},{5,9},{9,13},{13,1},{2,6},{6,10},{... | collective-permute-start | bytes 393224 | tf_op jit(solution)/shard_map/ppermute | solution.py:359
  136.6 11.1 %collective-permute-start.37 = (bf16[256,512]{1,0:T(8,128)(2,1)S(1)}, bf16[256,512]{1,0:T(8,128)(2,1)S(1)}, u32[]{:S(2)}, u32[]{:S(2)}) collective-permute-start(bf16[256,512]{1,0:T(8,128)(2,1)S(1)} %attention_grad.4.refs_6_.refs_3_), channel_id=1, source_target_pairs={{0,12},{4,0},{8,4},{12,8},{1,13},{5,1},{9,5},{13,9},{2,14},{6,2},{... | collective-permute-start | bytes 786440 | tf_op jit(solution)/shard_map/ppermute | solution.py:359
  136.6 11.1 %collective-permute-start.36 = (bf16[256,512]{1,0:T(8,128)(2,1)S(1)}, bf16[256,512]{1,0:T(8,128)(2,1)S(1)}, u32[]{:S(2)}, u32[]{:S(2)}) collective-permute-start(bf16[256,512]{1,0:T(8,128)(2,1)S(1)} %attention_grad.4.refs_6_.refs_3_), channel_id=1, source_target_pairs={{0,4},{4,8},{8,12},{12,0},{1,5},{5,9},{9,13},{13,1},{2,6},{6,10},{... | collective-permute-start | bytes 786440 | tf_op jit(solution)/shard_map/ppermute | solution.py:359
  147.8 5.3 %collective-permute-start.41 = (bf16[128,512]{1,0:T(8,128)(2,1)S(1)}, bf16[128,512]{1,0:T(8,128)(2,1)S(1)}, u32[]{:S(2)}, u32[]{:S(2)}) collective-permute-start(bf16[128,512]{1,0:T(8,128)(2,1)S(1)} %slice.150), channel_id=1, source_target_pairs={{0,12},{4,0},{8,4},{12,8},{1,13},{5,1},{9,5},{13,9},{2,14},{6,2},{... | collective-permute-start | bytes 393224 | tf_op jit(solution)/shard_map/ppermute | solution.py:359
  148.0 6.9 %collective-permute-start.40 = (bf16[128,512]{1,0:T(8,128)(2,1)S(1)}, bf16[128,512]{1,0:T(8,128)(2,1)S(1)}, u32[]{:S(2)}, u32[]{:S(2)}) collective-permute-start(bf16[128,512]{1,0:T(8,128)(2,1)S(1)} %slice.149), channel_id=1, source_target_pairs={{0,4},{4,8},{8,12},{12,0},{1,5},{5,9},{9,13},{13,1},{2,6},{6,10},{... | collective-permute-start | bytes 393224 | tf_op jit(solution)/shard_map/ppermute | solution.py:359
  149.8 27.6 %collective-permute-start.46 = (bf16[1280,256]{1,0:T(8,128)(2,1)S(1)}, bf16[1280,256]{1,0:T(8,128)(2,1)S(1)}, u32[]{:S(2)}, u32[]{:S(2)}) collective-permute-start(bf16[1280,256]{1,0:T(8,128)(2,1)S(1)} %get-tuple-element.93.refs_0_), channel_id=1, source_target_pairs={{0,16},{16,0},{1,17},{17,1},{2,18},{18,2},{3,19},{19,3},{4,20},{20... | collective-permute-start | bytes 1966088 | tf_op jit(solution)/shard_map/ppermute | solution.py:459
  157.3 21.7 %collective-permute-start.45 = (bf16[1280,256]{1,0:T(8,128)(2,1)S(1)}, bf16[1280,256]{1,0:T(8,128)(2,1)S(1)}, u32[]{:S(2)}, u32[]{:S(2)}) collective-permute-start(bf16[1280,256]{1,0:T(8,128)(2,1)S(1)} %get-tuple-element.97.refs_0_), channel_id=1, source_target_pairs={{0,16},{16,0},{1,17},{17,1},{2,18},{18,2},{3,19},{19,3},{4,20},{20... | collective-permute-start | bytes 1966088 | tf_op jit(solution)/shard_map/ppermute | solution.py:459
  159.2 5.0 %collective-permute-start.39 = (bf16[128,512]{1,0:T(8,128)(2,1)S(1)}, bf16[128,512]{1,0:T(8,128)(2,1)S(1)}, u32[]{:S(2)}, u32[]{:S(2)}) collective-permute-start(bf16[128,512]{1,0:T(8,128)(2,1)S(1)} %attention_grad.5.refs_3_), channel_id=1, source_target_pairs={{0,12},{4,0},{8,4},{12,8},{1,13},{5,1},{9,5},{13,9},{2,14},{6,2},{... | collective-permute-start | bytes 393224 | tf_op jit(solution)/shard_map/ppermute | solution.py:359
  160.3 7.5 %collective-permute-start.38 = (bf16[128,512]{1,0:T(8,128)(2,1)S(1)}, bf16[128,512]{1,0:T(8,128)(2,1)S(1)}, u32[]{:S(2)}, u32[]{:S(2)}) collective-permute-start(bf16[128,512]{1,0:T(8,128)(2,1)S(1)} %attention_grad.5.refs_3_), channel_id=1, source_target_pairs={{0,4},{4,8},{8,12},{12,0},{1,5},{5,9},{9,13},{13,1},{2,6},{6,10},{... | collective-permute-start | bytes 393224 | tf_op jit(solution)/shard_map/ppermute | solution.py:359
  167.9 4.3 %collective-permute-start.43 = (bf16[64,512]{1,0:T(8,128)(2,1)S(1)}, bf16[64,512]{1,0:T(8,128)(2,1)S(1)}, u32[]{:S(2)}, u32[]{:S(2)}) collective-permute-start(bf16[64,512]{1,0:T(8,128)(2,1)S(1)} %slice.152), channel_id=1, source_target_pairs={{0,12},{4,0},{8,4},{12,8},{1,13},{5,1},{9,5},{13,9},{2,14},{6,2},{... | collective-permute-start | bytes 196616 | tf_op jit(solution)/shard_map/ppermute | solution.py:359
  168.0 6.1 %collective-permute-start.42 = (bf16[64,512]{1,0:T(8,128)(2,1)S(1)}, bf16[64,512]{1,0:T(8,128)(2,1)S(1)}, u32[]{:S(2)}, u32[]{:S(2)}) collective-permute-start(bf16[64,512]{1,0:T(8,128)(2,1)S(1)} %slice.151), channel_id=1, source_target_pairs={{0,4},{4,8},{8,12},{12,0},{1,5},{5,9},{9,13},{13,1},{2,6},{6,10},{... | collective-permute-start | bytes 196616 | tf_op jit(solution)/shard_map/ppermute | solution.py:359
  175.7 7.1 %collective-permute-start.44 = (bf16[1280,128]{1,0:T(8,128)(2,1)S(1)}, bf16[1280,128]{1,0:T(8,128)(2,1)S(1)}, u32[]{:S(2)}, u32[]{:S(2)}) collective-permute-start(bf16[1280,128]{1,0:T(8,128)(2,1)S(1)} %get-tuple-element.102.refs_0_), channel_id=1, source_target_pairs={{0,16},{16,0},{1,17},{17,1},{2,18},{18,2},{3,19},{19,3},{4,20},{20... | collective-permute-start | bytes 983048 | tf_op jit(solution)/shard_map/ppermute | solution.py:459
